TPU v7x, 32 devices: a whole 2x2x4 slice. The times are simulated.
32 devices in a mesh: depth: 2 (over x), xy: 16 (over z, y, core).
Axes of the slice: x: 2, y: 2, z: 4, core: 2. Of those that a mesh axis runs over, the one named last changes fastest.
Arguments:
- surface_data: float32 [2, 2, 256, 2048], P(None, None, 'xy'), may hold values from -6 to 6
- frequencies: float32 [2], replicated, may hold values from 1 to 4
- coefficients: float32 [2, 2, 15], replicated, may hold values from -1 to 1
- slowness: float32 [4, 256, 2048], P('depth', 'xy'), may hold values from 0.4 to 1.2
- perturbation: float32 [4, 256, 2048], P('depth', 'xy'), may hold values from -6 to 6
Outputs:
- gradient: float32 [4, 256, 2048], P('depth', 'xy')
- image_field: float32 [4, 256, 2048], P('depth', 'xy')
All inputs are finite; a program needn't handle non-finite values.
Results may differ from a plain program's by a relative error of at most 0.0001.
Values sent between devices are 32-bit elements; how exact they have to be, the bound alone decides.
No kernel may reach another device: no remote copies, remote signals or barrier semaphores. Data moves between devices by JAX's collectives and lax.ppermute only.
A program may use at most 64 MiB of HBM per device.

v0:
```python
import jax
import jax.numpy as jnp
from jax import lax
from jax.sharding import PartitionSpec as P

layer_thickness = 0.5


def extended_2(cells, sides, width):
    for axis, dim in sides:
        count = lax.axis_size(axis)
        ends = count - 1
        head = lax.slice_in_dim(cells, 0, width, axis=dim)
        tail = lax.slice_in_dim(cells, cells.shape[dim] - width, cells.shape[dim], axis=dim)
        cells = jnp.concatenate(
            [
                lax.ppermute(tail, axis, [(i, (i + 1) % count) for i in range(ends)]),
                cells,
                lax.ppermute(head, axis, [((i + 1) % count, i) for i in range(ends)]),
            ],
            axis=dim,
        )
    return cells


def shifted(value, axis, steps):
    count = lax.axis_size(axis)
    initial, last = (max(0, -steps), min(count, count - steps))
    return lax.ppermute(value, axis, [(source, source + steps) for source in range(initial, last)])


def apply_stencil(extended, tap_re, tap_im):
    out_rows = extended.shape[2] - 4
    col_count = extended.shape[3]
    padded = jnp.pad(extended, ((0, 0), (0, 0), (0, 0), (1, 1)))
    acc_re = jnp.zeros((extended.shape[0], out_rows, col_count), jnp.float32)
    acc_im = jnp.zeros((extended.shape[0], out_rows, col_count), jnp.float32)
    for row_off in range(5):
        for col_off in range(3):
            tap_index = row_off * 3 + col_off
            part_re = padded[:, 0, row_off : row_off + out_rows, col_off : col_off + col_count]
            part_im = padded[:, 1, row_off : row_off + out_rows, col_off : col_off + col_count]
            weight_re = tap_re[:, tap_index][:, None, None]
            weight_im = tap_im[:, tap_index][:, None, None]
            acc_re = acc_re + weight_re * part_re - weight_im * part_im
            acc_im = acc_im + weight_re * part_im + weight_im * part_re
    return (acc_re, acc_im)


def adjoint_stencil(extended, tap_re, tap_im):
    out_rows = extended.shape[2] - 4
    col_count = extended.shape[3]
    padded = jnp.pad(extended, ((0, 0), (0, 0), (0, 0), (1, 1)))
    acc_re = jnp.zeros((extended.shape[0], out_rows, col_count), jnp.float32)
    acc_im = jnp.zeros((extended.shape[0], out_rows, col_count), jnp.float32)
    for row_off in range(5):
        for col_off in range(3):
            tap_index = row_off * 3 + col_off
            row_from = 4 - row_off
            col_from = 2 - col_off
            part_re = padded[:, 0, row_from : row_from + out_rows, col_from : col_from + col_count]
            part_im = padded[:, 1, row_from : row_from + out_rows, col_from : col_from + col_count]
            weight_re = tap_re[:, tap_index][:, None, None]
            weight_im = tap_im[:, tap_index][:, None, None]
            acc_re = acc_re + weight_re * part_re + weight_im * part_im
            acc_im = acc_im + weight_re * part_im - weight_im * part_re
    return (acc_re, acc_im)


def phase_parts(freqs, slow_plane):
    angle = freqs[:, None, None] * layer_thickness * slow_plane[None]
    return (jnp.cos(angle), jnp.sin(angle))


def forward_steps(wavefield, freqs, taps, slowness, freq_total):
    tap_re = taps[:, 0]
    tap_im = taps[:, 1]
    step_count = slowness.shape[0]
    states = []
    current = wavefield
    for level in range(step_count):
        extended = extended_2(current, (("xy", 2),), 2)
        acc_re, acc_im = apply_stencil(extended, tap_re, tap_im)
        phase_re, phase_im = phase_parts(freqs, slowness[level])
        next_re = phase_re * acc_re - phase_im * acc_im
        next_im = phase_re * acc_im + phase_im * acc_re
        current = jnp.stack([next_re, next_im], axis=1)
        states.append(current)
    stacked = jnp.stack(states, axis=1)
    image_part = (
        jnp.sum(stacked[:, :, 0] * stacked[:, :, 0] + stacked[:, :, 1] * stacked[:, :, 1], axis=0)
        / freq_total
    )
    return (stacked, states[-1], image_part)


def backward_steps(adjoint, states, freqs, taps, slowness, perturbation, freq_total):
    tap_re = taps[:, 0]
    tap_im = taps[:, 1]
    step_count = slowness.shape[0]
    parts = [None] * step_count
    for level in reversed(range(step_count)):
        wave_re = states[:, level, 0]
        wave_im = states[:, level, 1]
        grad_re = adjoint[:, 0] + 2.0 * perturbation[level] * wave_re
        grad_im = adjoint[:, 1] + 2.0 * perturbation[level] * wave_im
        parts[level] = (
            layer_thickness
            / freq_total
            * jnp.sum(freqs[:, None, None] * (grad_im * wave_re - grad_re * wave_im), axis=0)
        )
        phase_re, phase_im = phase_parts(freqs, slowness[level])
        back_re = phase_re * grad_re + phase_im * grad_im
        back_im = phase_re * grad_im - phase_im * grad_re
        extended = extended_2(jnp.stack([back_re, back_im], axis=1), (("xy", 2),), 2)
        acc_re, acc_im = adjoint_stencil(extended, tap_re, tap_im)
        adjoint = jnp.stack([acc_re, acc_im], axis=1)
    return (adjoint, jnp.stack(parts, axis=0))


def on_device(surface_data, frequencies, coefficients, slowness, perturbation):
    freq_count = frequencies.shape[0]
    step_count = slowness.shape[0]
    row_count = slowness.shape[1]
    col_count = slowness.shape[2]
    layers = lax.axis_size("depth")
    depth_index = lax.axis_index("depth")
    stored_zero = jnp.zeros((freq_count, step_count, 2, row_count, col_count), jnp.float32)
    plane_zero = jnp.zeros((step_count, row_count, col_count), jnp.float32)
    start = jnp.where(depth_index == 0, surface_data, jnp.zeros_like(surface_data))

    def forward_segment(segment_no, carry):
        current, stored, image_sum = carry
        states, bottom, image_part = forward_steps(
            current, frequencies, coefficients, slowness, freq_count
        )
        chosen = depth_index == segment_no
        stored = jnp.where(chosen, states, stored)
        image_sum = jnp.where(chosen, image_part, image_sum)
        current = shifted(bottom, "depth", 1)
        return (current, stored, image_sum)

    unused_field, stored, image_field = lax.fori_loop(
        0, layers, forward_segment, (start, stored_zero, plane_zero)
    )

    def backward_segment(segment_no, carry):
        adjoint, gradient_sum = carry
        top_field, parts = backward_steps(
            adjoint, stored, frequencies, coefficients, slowness, perturbation, freq_count
        )
        gradient_sum = jnp.where(depth_index == layers - 1 - segment_no, parts, gradient_sum)
        adjoint = shifted(top_field, "depth", -1)
        return (adjoint, gradient_sum)

    adjoint_zero = jnp.zeros_like(surface_data)
    unused_adjoint, gradient = lax.fori_loop(
        0, layers, backward_segment, (adjoint_zero, plane_zero)
    )
    return (gradient, image_field)


def solution(mesh):
    in_specs = (P(None, None, "xy", None), P(), P(), P("depth", "xy", None), P("depth", "xy", None))
    out_specs = (P("depth", "xy", None), P("depth", "xy", None))
    return jax.shard_map(
        on_device, mesh=mesh, in_specs=in_specs, out_specs=out_specs, check_vma=False
    )
```

profile of v0, /device:TPU:20, one launch (start us, length us, event | category | flops | bytes accessed | tf_op | source)
XLA Modules:
  0.0 170.8 jit_solution(5028114466290360011)
XLA Ops:
  3.1 81.1 %while.38 = (s32[]{:T(128)}, f32[2,2,16,2048]{3,2,1,0:T(8,128)S(1)}, f32[2,2,2,16,2048]{4,3,2,0,1:T(8,128)S(1)}, f32[2,16,2048]{2,1,0:T(8,128)S(1)}, f32[2]{0:T(...) while((s32[]{:T(128)}, ...), condition=%wide.region_2.3_spmd.clone, body=%wide.region_0.2_spmd.clone.sunk | while | flops 22514500 | bytes 37046552 | solution.py:143
  5.1 2.4 %collective-permute-start.1 = (f32[2,2,2,2048]{3,2,1,0:T(2,128)S(1)}, f32[2,2,2,2048]{3,2,1,0:T(2,128)S(1)}, u32[]{:S(2)}, u32[]{:S(2)}) collective-permute-start(f32[2,2,2,2048]{3,2,1,0:T(2,128)S(1)} %get-tuple-element.843), channel_id=1, source_target_pairs={{0,1},{1,2},{2,3},{3,4},{4,5},{5,6},{6,7},{7,8},{8,9},{9,10},{10,1... | collective-permute-start | bytes 196616 | tf_op jit(solution)/shard_map/while/body/eval_jaxpr/ppermute | solution.py:17
  11.1 2.9 %fusion.132 = (f32[2,1,16,2048]{3,2,1,0:T(8,128)S(1)}, f32[2,1,16,2048]{3,2,1,0:T(8,128)S(1)}, f32[2,1,16,2048]{3,2,1,0:T(8,128)S(1)}) fusion(f32[16,2048]{1,0:T(8,128)S(1)} %get-tuple-element.841, f32[2]{0:T(128)S(1)} %broadcast_multiply_fusion.4, f32[2,2,20,2050]{3,2,1,0:T(8,128)S(1)} %select_maximum_fusion.15, f32[2]{0:T(128)S(1)} %get-tuple-element.845, ...), kind=kLoop, calls=%fused_computation.47.clone.1 | loop fusion | flops 8454144 | bytes 8338944 | tf_op jit(solution)/shard_map/while/body/eval_jaxpr/sub | solution.py:85
  17.2 2.4 %collective-permute-start.3 = (f32[2,2,2,2048]{3,2,1,0:T(2,128)S(1)}, f32[2,2,2,2048]{3,2,1,0:T(2,128)S(1)}, u32[]{:S(2)}, u32[]{:S(2)}) collective-permute-start(f32[2,2,2,2048]{3,2,1,0:T(2,128)S(1)} %get-tuple-element.880), channel_id=1, source_target_pairs={{0,1},{1,2},{2,3},{3,4},{4,5},{5,6},{6,7},{7,8},{8,9},{9,10},{10,1... | collective-permute-start | bytes 196616 | tf_op jit(solution)/shard_map/while/body/eval_jaxpr/ppermute | solution.py:17
  19.6 3.7 %collective-permute-done.3 = f32[2,2,2,2048]{3,2,1,0:T(2,128)S(1)} collective-permute-done((f32[2,2,2,2048]{3,2,1,0:T(2,128)S(1)}, f32[2,2,2,2048]{3,2,1,0:T(2,128)S(1)}, u32[]{:S(2)}, u32[]{:S(2)}) %collective-permute-start.3) | collective-permute-done | bytes 65568 | tf_op jit(solution)/shard_map/while/body/eval_jaxpr/ppermute | solution.py:17
  23.9 2.9 %fusion.135 = (f32[2,1,16,2048]{3,2,1,0:T(8,128)S(1)}, f32[2,1,16,2048]{3,2,1,0:T(8,128)S(1)}, f32[2,1,16,2048]{3,2,1,0:T(8,128)S(1)}) fusion(f32[16,2048]{1,0:T(8,128)S(1)} %get-tuple-element.840, f32[2]{0:T(128)S(1)} %broadcast_multiply_fusion.4, f32[2,2,20,2050]{3,2,1,0:T(8,128)S(1)} %select_maximum_fusion.16, f32[2]{0:T(128)S(1)} %get-tuple-element.845, ...), kind=kLoop, calls=%fused_computation.49.clone.1 | loop fusion | flops 7995392 | bytes 8782072 | tf_op jit(solution)/shard_map/while/body/eval_jaxpr/sub | solution.py:85
  28.1 3.4 %collective-permute-start.4 = (f32[2,2,16,2048]{3,2,1,0:T(8,128)S(1)}, f32[2,2,16,2048]{3,2,1,0:T(8,128)S(1)}, u32[]{:S(2)}, u32[]{:S(2)}) collective-permute-start(f32[2,2,16,2048]{3,2,1,0:T(8,128)S(1)} %get-tuple-element.886), channel_id=1, source_target_pairs={{0,16},{1,17},{2,18},{3,19},{4,20},{5,21},{6,22},{7,23},{8,24},{9,... | collective-permute-start | bytes 1572872 | tf_op jit(solution)/shard_map/while/body/eval_jaxpr/ppermute | solution.py:29
  32.0 11.2 %collective-permute-done.4 = f32[2,2,16,2048]{3,2,1,0:T(8,128)S(1)} collective-permute-done((f32[2,2,16,2048]{3,2,1,0:T(8,128)S(1)}, f32[2,2,16,2048]{3,2,1,0:T(8,128)S(1)}, u32[]{:S(2)}, u32[]{:S(2)}) %collective-permute-start.4) | collective-permute-done | bytes 524320 | tf_op jit(solution)/shard_map/while/body/eval_jaxpr/ppermute | solution.py:29
  45.2 2.4 %collective-permute-start.1 = (f32[2,2,2,2048]{3,2,1,0:T(2,128)S(1)}, f32[2,2,2,2048]{3,2,1,0:T(2,128)S(1)}, u32[]{:S(2)}, u32[]{:S(2)}) collective-permute-start(f32[2,2,2,2048]{3,2,1,0:T(2,128)S(1)} %get-tuple-element.843), channel_id=1, source_target_pairs={{0,1},{1,2},{2,3},{3,4},{4,5},{5,6},{6,7},{7,8},{8,9},{9,10},{10,1... | collective-permute-start | bytes 196616 | tf_op jit(solution)/shard_map/while/body/eval_jaxpr/ppermute | solution.py:17
  51.3 2.9 %fusion.132 = (f32[2,1,16,2048]{3,2,1,0:T(8,128)S(1)}, f32[2,1,16,2048]{3,2,1,0:T(8,128)S(1)}, f32[2,1,16,2048]{3,2,1,0:T(8,128)S(1)}) fusion(f32[16,2048]{1,0:T(8,128)S(1)} %get-tuple-element.841, f32[2]{0:T(128)S(1)} %broadcast_multiply_fusion.4, f32[2,2,20,2050]{3,2,1,0:T(8,128)S(1)} %select_maximum_fusion.15, f32[2]{0:T(128)S(1)} %get-tuple-element.845, ...), kind=kLoop, calls=%fused_computation.47.clone.1 | loop fusion | flops 8454144 | bytes 8338944 | tf_op jit(solution)/shard_map/while/body/eval_jaxpr/sub | solution.py:85
  57.3 2.4 %collective-permute-start.3 = (f32[2,2,2,2048]{3,2,1,0:T(2,128)S(1)}, f32[2,2,2,2048]{3,2,1,0:T(2,128)S(1)}, u32[]{:S(2)}, u32[]{:S(2)}) collective-permute-start(f32[2,2,2,2048]{3,2,1,0:T(2,128)S(1)} %get-tuple-element.880), channel_id=1, source_target_pairs={{0,1},{1,2},{2,3},{3,4},{4,5},{5,6},{6,7},{7,8},{8,9},{9,10},{10,1... | collective-permute-start | bytes 196616 | tf_op jit(solution)/shard_map/while/body/eval_jaxpr/ppermute | solution.py:17
  59.8 3.5 %collective-permute-done.3 = f32[2,2,2,2048]{3,2,1,0:T(2,128)S(1)} collective-permute-done((f32[2,2,2,2048]{3,2,1,0:T(2,128)S(1)}, f32[2,2,2,2048]{3,2,1,0:T(2,128)S(1)}, u32[]{:S(2)}, u32[]{:S(2)}) %collective-permute-start.3) | collective-permute-done | bytes 65568 | tf_op jit(solution)/shard_map/while/body/eval_jaxpr/ppermute | solution.py:17
  63.9 2.9 %fusion.135 = (f32[2,1,16,2048]{3,2,1,0:T(8,128)S(1)}, f32[2,1,16,2048]{3,2,1,0:T(8,128)S(1)}, f32[2,1,16,2048]{3,2,1,0:T(8,128)S(1)}) fusion(f32[16,2048]{1,0:T(8,128)S(1)} %get-tuple-element.840, f32[2]{0:T(128)S(1)} %broadcast_multiply_fusion.4, f32[2,2,20,2050]{3,2,1,0:T(8,128)S(1)} %select_maximum_fusion.16, f32[2]{0:T(128)S(1)} %get-tuple-element.845, ...), kind=kLoop, calls=%fused_computation.49.clone.1 | loop fusion | flops 7995392 | bytes 8782072 | tf_op jit(solution)/shard_map/while/body/eval_jaxpr/sub | solution.py:85
  68.0 4.4 %collective-permute-start.4 = (f32[2,2,16,2048]{3,2,1,0:T(8,128)S(1)}, f32[2,2,16,2048]{3,2,1,0:T(8,128)S(1)}, u32[]{:S(2)}, u32[]{:S(2)}) collective-permute-start(f32[2,2,16,2048]{3,2,1,0:T(8,128)S(1)} %get-tuple-element.886), channel_id=1, source_target_pairs={{0,16},{1,17},{2,18},{3,19},{4,20},{5,21},{6,22},{7,23},{8,24},{9,... | collective-permute-start | bytes 1572872 | tf_op jit(solution)/shard_map/while/body/eval_jaxpr/ppermute | solution.py:29
  73.0 11.2 %collective-permute-done.4 = f32[2,2,16,2048]{3,2,1,0:T(8,128)S(1)} collective-permute-done((f32[2,2,16,2048]{3,2,1,0:T(8,128)S(1)}, f32[2,2,16,2048]{3,2,1,0:T(8,128)S(1)}, u32[]{:S(2)}, u32[]{:S(2)}) %collective-permute-start.4) | collective-permute-done | bytes 524320 | tf_op jit(solution)/shard_map/while/body/eval_jaxpr/ppermute | solution.py:29
  85.8 84.3 %while.39 = (s32[]{:T(128)}, f32[2,2,16,2048]{3,2,0,1:T(8,128)S(1)}, f32[2,16,2048]{2,1,0:T(8,128)S(1)}, f32[2,2,15]{2,0,1:T(2,128)S(1)}, f32[2]{0:T(128)S(1)}, ...) while((s32[]{:T(128)}, ...), condition=%wide.region_6.7_spmd.clone, body=%wide.region_3.6_spmd.clone.sunk | while | flops 30805124 | bytes 53612084 | solution.py:157
  89.0 2.4 %collective-permute-start.6 = (f32[2,2,2,2048]{3,2,0,1:T(2,128)S(1)}, f32[2,2,2,2048]{3,2,0,1:T(2,128)S(1)}, u32[]{:S(2)}, u32[]{:S(2)}) collective-permute-start(f32[2,2,2,2048]{3,2,0,1:T(2,128)S(1)} %get-tuple-element.904), channel_id=1, source_target_pairs={{0,1},{1,2},{2,3},{3,4},{4,5},{5,6},{6,7},{7,8},{8,9},{9,10},{10,1... | collective-permute-start | bytes 196616 | tf_op jit(solution)/shard_map/while/body/eval_jaxpr/ppermute | solution.py:17
  95.2 2.9 %fusion.142 = (f32[2,1,16,2048]{3,2,0,1:T(8,128)S(1)}, f32[2,1,16,2048]{3,2,0,1:T(8,128)S(1)}, f32[2,1,16,2048]{3,2,0,1:T(8,128)S(1)}) fusion(f32[16,2048]{1,0:T(8,128)S(1)} %get-tuple-element.897, f32[2]{0:T(128)S(1)} %broadcast_multiply_fusion.5, f32[2,2,2,16,2048]{4,3,0,2,1:T(8,128)S(1)} %get-tuple-element.1005, ...), kind=kLoop, calls=%fused_computation.129.clone.1 | loop fusion | flops 8257536 | bytes 9437432 | tf_op jit(solution)/shard_map/while/body/eval_jaxpr/sub | solution.py:114
  101.2 2.4 %collective-permute-start.8 = (f32[2,2,2,2048]{3,2,0,1:T(2,128)S(1)}, f32[2,2,2,2048]{3,2,0,1:T(2,128)S(1)}, u32[]{:S(2)}, u32[]{:S(2)}) collective-permute-start(f32[2,2,2,2048]{3,2,0,1:T(2,128)S(1)} %get-tuple-element.943), channel_id=1, source_target_pairs={{0,1},{1,2},{2,3},{3,4},{4,5},{5,6},{6,7},{7,8},{8,9},{9,10},{10,1... | collective-permute-start | bytes 196616 | tf_op jit(solution)/shard_map/while/body/eval_jaxpr/ppermute | solution.py:17
  112.7 15.0 %collective-permute-done.9 = f32[2,2,16,2048]{3,2,0,1:T(8,128)S(1)} collective-permute-done((f32[2,2,16,2048]{3,2,0,1:T(8,128)S(1)}, f32[2,2,16,2048]{3,2,0,1:T(8,128)S(1)}, u32[]{:S(2)}, u32[]{:S(2)}) %collective-permute-start.9) | collective-permute-done | bytes 524320 | tf_op jit(solution)/shard_map/while/body/eval_jaxpr/ppermute | solution.py:29
  130.9 2.4 %collective-permute-start.6 = (f32[2,2,2,2048]{3,2,0,1:T(2,128)S(1)}, f32[2,2,2,2048]{3,2,0,1:T(2,128)S(1)}, u32[]{:S(2)}, u32[]{:S(2)}) collective-permute-start(f32[2,2,2,2048]{3,2,0,1:T(2,128)S(1)} %get-tuple-element.904), channel_id=1, source_target_pairs={{0,1},{1,2},{2,3},{3,4},{4,5},{5,6},{6,7},{7,8},{8,9},{9,10},{10,1... | collective-permute-start | bytes 196616 | tf_op jit(solution)/shard_map/while/body/eval_jaxpr/ppermute | solution.py:17
  137.1 2.9 %fusion.142 = (f32[2,1,16,2048]{3,2,0,1:T(8,128)S(1)}, f32[2,1,16,2048]{3,2,0,1:T(8,128)S(1)}, f32[2,1,16,2048]{3,2,0,1:T(8,128)S(1)}) fusion(f32[16,2048]{1,0:T(8,128)S(1)} %get-tuple-element.897, f32[2]{0:T(128)S(1)} %broadcast_multiply_fusion.5, f32[2,2,2,16,2048]{4,3,0,2,1:T(8,128)S(1)} %get-tuple-element.1005, ...), kind=kLoop, calls=%fused_computation.129.clone.1 | loop fusion | flops 8257536 | bytes 9437432 | tf_op jit(solution)/shard_map/while/body/eval_jaxpr/sub | solution.py:114
  143.1 2.4 %collective-permute-start.8 = (f32[2,2,2,2048]{3,2,0,1:T(2,128)S(1)}, f32[2,2,2,2048]{3,2,0,1:T(2,128)S(1)}, u32[]{:S(2)}, u32[]{:S(2)}) collective-permute-start(f32[2,2,2,2048]{3,2,0,1:T(2,128)S(1)} %get-tuple-element.943), channel_id=1, source_target_pairs={{0,1},{1,2},{2,3},{3,4},{4,5},{5,6},{6,7},{7,8},{8,9},{9,10},{10,1... | collective-permute-start | bytes 196616 | tf_op jit(solution)/shard_map/while/body/eval_jaxpr/ppermute | solution.py:17
  155.0 15.1 %collective-permute-done.9 = f32[2,2,16,2048]{3,2,0,1:T(8,128)S(1)} collective-permute-done((f32[2,2,16,2048]{3,2,0,1:T(8,128)S(1)}, f32[2,2,16,2048]{3,2,0,1:T(8,128)S(1)}, u32[]{:S(2)}, u32[]{:S(2)}) %collective-permute-start.9) | collective-permute-done | bytes 524320 | tf_op jit(solution)/shard_map/while/body/eval_jaxpr/ppermute | solution.py:29
  (128 shorter events, 65.1 us)
Async XLA Ops:
  1.7 1.0 copy-start
  3.1 5.2 %collective-permute-start = (f32[2,2,2,2048]{3,2,1,0:T(2,128)S(1)}, f32[2,2,2,2048]{3,2,1,0:T(2,128)S(1)}, u32[]{:S(2)}, u32[]{:S(2)}) collective-permute-start(f32[2,2,2,2048]{3,2,1,0:T(2,128)S(1)} %get-tuple-element.842), channel_id=1, source_target_pairs={{1,0},{2,1},{3,2},{4,3},{5,4},{6,5},{7,6},{8,7},{9,8},{10,9},{11,1... | collective-permute-start | bytes 196616 | tf_op jit(solution)/shard_map/while/body/eval_jaxpr/ppermute | solution.py:19
  5.1 5.6 %collective-permute-start.1 = (f32[2,2,2,2048]{3,2,1,0:T(2,128)S(1)}, f32[2,2,2,2048]{3,2,1,0:T(2,128)S(1)}, u32[]{:S(2)}, u32[]{:S(2)}) collective-permute-start(f32[2,2,2,2048]{3,2,1,0:T(2,128)S(1)} %get-tuple-element.843), channel_id=1, source_target_pairs={{0,1},{1,2},{2,3},{3,4},{4,5},{5,6},{6,7},{7,8},{8,9},{9,10},{10,1... | collective-permute-start | bytes 196616 | tf_op jit(solution)/shard_map/while/body/eval_jaxpr/ppermute | solution.py:17
  15.2 4.4 %collective-permute-start.2 = (f32[2,2,2,2048]{3,2,1,0:T(2,128)S(1)}, f32[2,2,2,2048]{3,2,1,0:T(2,128)S(1)}, u32[]{:S(2)}, u32[]{:S(2)}) collective-permute-start(f32[2,2,2,2048]{3,2,1,0:T(2,128)S(1)} %get-tuple-element.879), channel_id=1, source_target_pairs={{1,0},{2,1},{3,2},{4,3},{5,4},{6,5},{7,6},{8,7},{9,8},{10,9},{11,1... | collective-permute-start | bytes 196616 | tf_op jit(solution)/shard_map/while/body/eval_jaxpr/ppermute | solution.py:19
  17.2 6.2 %collective-permute-start.3 = (f32[2,2,2,2048]{3,2,1,0:T(2,128)S(1)}, f32[2,2,2,2048]{3,2,1,0:T(2,128)S(1)}, u32[]{:S(2)}, u32[]{:S(2)}) collective-permute-start(f32[2,2,2,2048]{3,2,1,0:T(2,128)S(1)} %get-tuple-element.880), channel_id=1, source_target_pairs={{0,1},{1,2},{2,3},{3,4},{4,5},{5,6},{6,7},{7,8},{8,9},{9,10},{10,1... | collective-permute-start | bytes 196616 | tf_op jit(solution)/shard_map/while/body/eval_jaxpr/ppermute | solution.py:17
  28.1 15.2 %collective-permute-start.4 = (f32[2,2,16,2048]{3,2,1,0:T(8,128)S(1)}, f32[2,2,16,2048]{3,2,1,0:T(8,128)S(1)}, u32[]{:S(2)}, u32[]{:S(2)}) collective-permute-start(f32[2,2,16,2048]{3,2,1,0:T(8,128)S(1)} %get-tuple-element.886), channel_id=1, source_target_pairs={{0,16},{1,17},{2,18},{3,19},{4,20},{5,21},{6,22},{7,23},{8,24},{9,... | collective-permute-start | bytes 1572872 | tf_op jit(solution)/shard_map/while/body/eval_jaxpr/ppermute | solution.py:29
  43.3 5.2 %collective-permute-start = (f32[2,2,2,2048]{3,2,1,0:T(2,128)S(1)}, f32[2,2,2,2048]{3,2,1,0:T(2,128)S(1)}, u32[]{:S(2)}, u32[]{:S(2)}) collective-permute-start(f32[2,2,2,2048]{3,2,1,0:T(2,128)S(1)} %get-tuple-element.842), channel_id=1, source_target_pairs={{1,0},{2,1},{3,2},{4,3},{5,4},{6,5},{7,6},{8,7},{9,8},{10,9},{11,1... | collective-permute-start | bytes 196616 | tf_op jit(solution)/shard_map/while/body/eval_jaxpr/ppermute | solution.py:19
  45.2 5.6 %collective-permute-start.1 = (f32[2,2,2,2048]{3,2,1,0:T(2,128)S(1)}, f32[2,2,2,2048]{3,2,1,0:T(2,128)S(1)}, u32[]{:S(2)}, u32[]{:S(2)}) collective-permute-start(f32[2,2,2,2048]{3,2,1,0:T(2,128)S(1)} %get-tuple-element.843), channel_id=1, source_target_pairs={{0,1},{1,2},{2,3},{3,4},{4,5},{5,6},{6,7},{7,8},{8,9},{9,10},{10,1... | collective-permute-start | bytes 196616 | tf_op jit(solution)/shard_map/while/body/eval_jaxpr/ppermute | solution.py:17
  55.4 4.4 %collective-permute-start.2 = (f32[2,2,2,2048]{3,2,1,0:T(2,128)S(1)}, f32[2,2,2,2048]{3,2,1,0:T(2,128)S(1)}, u32[]{:S(2)}, u32[]{:S(2)}) collective-permute-start(f32[2,2,2,2048]{3,2,1,0:T(2,128)S(1)} %get-tuple-element.879), channel_id=1, source_target_pairs={{1,0},{2,1},{3,2},{4,3},{5,4},{6,5},{7,6},{8,7},{9,8},{10,9},{11,1... | collective-permute-start | bytes 196616 | tf_op jit(solution)/shard_map/while/body/eval_jaxpr/ppermute | solution.py:19
  57.3 6.0 %collective-permute-start.3 = (f32[2,2,2,2048]{3,2,1,0:T(2,128)S(1)}, f32[2,2,2,2048]{3,2,1,0:T(2,128)S(1)}, u32[]{:S(2)}, u32[]{:S(2)}) collective-permute-start(f32[2,2,2,2048]{3,2,1,0:T(2,128)S(1)} %get-tuple-element.880), channel_id=1, source_target_pairs={{0,1},{1,2},{2,3},{3,4},{4,5},{5,6},{6,7},{7,8},{8,9},{9,10},{10,1... | collective-permute-start | bytes 196616 | tf_op jit(solution)/shard_map/while/body/eval_jaxpr/ppermute | solution.py:17
  68.0 16.2 %collective-permute-start.4 = (f32[2,2,16,2048]{3,2,1,0:T(8,128)S(1)}, f32[2,2,16,2048]{3,2,1,0:T(8,128)S(1)}, u32[]{:S(2)}, u32[]{:S(2)}) collective-permute-start(f32[2,2,16,2048]{3,2,1,0:T(8,128)S(1)} %get-tuple-element.886), channel_id=1, source_target_pairs={{0,16},{1,17},{2,18},{3,19},{4,20},{5,21},{6,22},{7,23},{8,24},{9,... | collective-permute-start | bytes 1572872 | tf_op jit(solution)/shard_map/while/body/eval_jaxpr/ppermute | solution.py:29
  84.9 0.9 copy-start.3
  87.1 5.3 %collective-permute-start.5 = (f32[2,2,2,2048]{3,2,0,1:T(2,128)S(1)}, f32[2,2,2,2048]{3,2,0,1:T(2,128)S(1)}, u32[]{:S(2)}, u32[]{:S(2)}) collective-permute-start(f32[2,2,2,2048]{3,2,0,1:T(2,128)S(1)} %get-tuple-element.903), channel_id=1, source_target_pairs={{1,0},{2,1},{3,2},{4,3},{5,4},{6,5},{7,6},{8,7},{9,8},{10,9},{11,1... | collective-permute-start | bytes 196616 | tf_op jit(solution)/shard_map/while/body/eval_jaxpr/ppermute | solution.py:19
  89.0 5.6 %collective-permute-start.6 = (f32[2,2,2,2048]{3,2,0,1:T(2,128)S(1)}, f32[2,2,2,2048]{3,2,0,1:T(2,128)S(1)}, u32[]{:S(2)}, u32[]{:S(2)}) collective-permute-start(f32[2,2,2,2048]{3,2,0,1:T(2,128)S(1)} %get-tuple-element.904), channel_id=1, source_target_pairs={{0,1},{1,2},{2,3},{3,4},{4,5},{5,6},{6,7},{7,8},{8,9},{9,10},{10,1... | collective-permute-start | bytes 196616 | tf_op jit(solution)/shard_map/while/body/eval_jaxpr/ppermute | solution.py:17
  99.3 6.3 %collective-permute-start.7 = (f32[2,2,2,2048]{3,2,0,1:T(2,128)S(1)}, f32[2,2,2,2048]{3,2,0,1:T(2,128)S(1)}, u32[]{:S(2)}, u32[]{:S(2)}) collective-permute-start(f32[2,2,2,2048]{3,2,0,1:T(2,128)S(1)} %get-tuple-element.942), channel_id=1, source_target_pairs={{1,0},{2,1},{3,2},{4,3},{5,4},{6,5},{7,6},{8,7},{9,8},{10,9},{11,1... | collective-permute-start | bytes 196616 | tf_op jit(solution)/shard_map/while/body/eval_jaxpr/ppermute | solution.py:19
  101.2 6.0 %collective-permute-start.8 = (f32[2,2,2,2048]{3,2,0,1:T(2,128)S(1)}, f32[2,2,2,2048]{3,2,0,1:T(2,128)S(1)}, u32[]{:S(2)}, u32[]{:S(2)}) collective-permute-start(f32[2,2,2,2048]{3,2,0,1:T(2,128)S(1)} %get-tuple-element.943), channel_id=1, source_target_pairs={{0,1},{1,2},{2,3},{3,4},{4,5},{5,6},{6,7},{7,8},{8,9},{9,10},{10,1... | collective-permute-start | bytes 196616 | tf_op jit(solution)/shard_map/while/body/eval_jaxpr/ppermute | solution.py:17
  111.2 16.4 %collective-permute-start.9 = (f32[2,2,16,2048]{3,2,0,1:T(8,128)S(1)}, f32[2,2,16,2048]{3,2,0,1:T(8,128)S(1)}, u32[]{:S(2)}, u32[]{:S(2)}) collective-permute-start(f32[2,2,16,2048]{3,2,0,1:T(8,128)S(1)} %pad_maximum_fusion.21), channel_id=1, source_target_pairs={{16,0},{17,1},{18,2},{19,3},{20,4},{21,5},{22,6},{23,7},{24,8},{25... | collective-permute-start | bytes 1572872 | tf_op jit(solution)/shard_map/while/body/eval_jaxpr/ppermute | solution.py:29
  112.6 15.1 %copy-start.4 = (f32[2,16,2048]{2,1,0:T(8,128)S(1)}, f32[2,16,2048]{2,1,0:T(8,128)}, u32[]{:S(2)}) copy-start(f32[2,16,2048]{2,1,0:T(8,128)} %get-tuple-element.1033) | copy-start | bytes 786436 | tf_op jit(solution)/shard_map/while
  129.0 5.3 %collective-permute-start.5 = (f32[2,2,2,2048]{3,2,0,1:T(2,128)S(1)}, f32[2,2,2,2048]{3,2,0,1:T(2,128)S(1)}, u32[]{:S(2)}, u32[]{:S(2)}) collective-permute-start(f32[2,2,2,2048]{3,2,0,1:T(2,128)S(1)} %get-tuple-element.903), channel_id=1, source_target_pairs={{1,0},{2,1},{3,2},{4,3},{5,4},{6,5},{7,6},{8,7},{9,8},{10,9},{11,1... | collective-permute-start | bytes 196616 | tf_op jit(solution)/shard_map/while/body/eval_jaxpr/ppermute | solution.py:19
  130.9 5.6 %collective-permute-start.6 = (f32[2,2,2,2048]{3,2,0,1:T(2,128)S(1)}, f32[2,2,2,2048]{3,2,0,1:T(2,128)S(1)}, u32[]{:S(2)}, u32[]{:S(2)}) collective-permute-start(f32[2,2,2,2048]{3,2,0,1:T(2,128)S(1)} %get-tuple-element.904), channel_id=1, source_target_pairs={{0,1},{1,2},{2,3},{3,4},{4,5},{5,6},{6,7},{7,8},{8,9},{9,10},{10,1... | collective-permute-start | bytes 196616 | tf_op jit(solution)/shard_map/while/body/eval_jaxpr/ppermute | solution.py:17
  141.2 6.3 %collective-permute-start.7 = (f32[2,2,2,2048]{3,2,0,1:T(2,128)S(1)}, f32[2,2,2,2048]{3,2,0,1:T(2,128)S(1)}, u32[]{:S(2)}, u32[]{:S(2)}) collective-permute-start(f32[2,2,2,2048]{3,2,0,1:T(2,128)S(1)} %get-tuple-element.942), channel_id=1, source_target_pairs={{1,0},{2,1},{3,2},{4,3},{5,4},{6,5},{7,6},{8,7},{9,8},{10,9},{11,1... | collective-permute-start | bytes 196616 | tf_op jit(solution)/shard_map/while/body/eval_jaxpr/ppermute | solution.py:19
  143.1 6.5 %collective-permute-start.8 = (f32[2,2,2,2048]{3,2,0,1:T(2,128)S(1)}, f32[2,2,2,2048]{3,2,0,1:T(2,128)S(1)}, u32[]{:S(2)}, u32[]{:S(2)}) collective-permute-start(f32[2,2,2,2048]{3,2,0,1:T(2,128)S(1)} %get-tuple-element.943), channel_id=1, source_target_pairs={{0,1},{1,2},{2,3},{3,4},{4,5},{5,6},{6,7},{7,8},{8,9},{9,10},{10,1... | collective-permute-start | bytes 196616 | tf_op jit(solution)/shard_map/while/body/eval_jaxpr/ppermute | solution.py:17
  153.6 16.6 %collective-permute-start.9 = (f32[2,2,16,2048]{3,2,0,1:T(8,128)S(1)}, f32[2,2,16,2048]{3,2,0,1:T(8,128)S(1)}, u32[]{:S(2)}, u32[]{:S(2)}) collective-permute-start(f32[2,2,16,2048]{3,2,0,1:T(8,128)S(1)} %pad_maximum_fusion.21), channel_id=1, source_target_pairs={{16,0},{17,1},{18,2},{19,3},{20,4},{21,5},{22,6},{23,7},{24,8},{25... | collective-permute-start | bytes 1572872 | tf_op jit(solution)/shard_map/while/body/eval_jaxpr/ppermute | solution.py:29
  154.9 15.2 %copy-start.4 = (f32[2,16,2048]{2,1,0:T(8,128)S(1)}, f32[2,16,2048]{2,1,0:T(8,128)}, u32[]{:S(2)}) copy-start(f32[2,16,2048]{2,1,0:T(8,128)} %get-tuple-element.1033) | copy-start | bytes 786436 | tf_op jit(solution)/shard_map/while
  (4 other events, 2.8 us)
where the time goes:
time: 172 us; the launch traced here: 171 us
  waiting for transfers between devices  72.3 us (42%)
  starting transfers between devices  45 us (26%)
  other arithmetic  44.8 us (26%)
  local copies, waits for them, and re-layouts  7.18 us (4%)
    ppermute x4, waiting for transfers between devices, shifted(): lax.ppermute(value, axis, [(source, source + steps) for source in range(i...  52.5 us
    ppermute x8, waiting for transfers between devices, extended_2(): lax.ppermute(tail, axis, [(i, (i + 1) % count) for i in range(ends)])  19.8 us
    ppermute x8, starting transfers between devices, extended_2(): lax.ppermute(tail, axis, [(i, (i + 1) % count) for i in range(ends)])  19.3 us
    ppermute x8, starting transfers between devices, extended_2(): lax.ppermute(head, axis, [((i + 1) % count, i) for i in range(ends)])  15.4 us
    sub x4, other arithmetic, forward_steps(): next_re = phase_re * acc_re - phase_im * acc_im  11.6 us
    ppermute x4, starting transfers between devices, shifted(): lax.ppermute(value, axis, [(source, source + steps) for source in range(i...  10.4 us
    sub x2, other arithmetic, backward_steps(): back_im = phase_re * grad_im - phase_im * grad_re  5.85 us
    add x4, other arithmetic, backward_steps(): back_re = phase_re * grad_re + phase_im * grad_im  4.63 us
  transfers between devices with their start and end apart: 20, of which 12 were waited for; matrix products, arithmetic and copies ran while one was open for 5% of the time, Pallas kernels for 0%

commit v1 on v0

--- a/solution.py
+++ b/solution.py
@@ -1,6 +1,9 @@
+import numpy as np
 import jax
 import jax.numpy as jnp
 from jax import lax
+from jax.experimental import pallas as pl
+from jax.experimental.pallas import tpu as pltpu
 from jax.sharding import PartitionSpec as P
 
 layer_thickness = 0.5
@@ -160,9 +163,363 @@
     return (gradient, image_field)
 
 
+ROWS = 16
+HALO_TILES = 4
+LANES = 128
+
+sin_terms = (0.999999999, -0.1666666575, 0.00833331893, -0.0001984042124, 2.753344554e-06, -2.470543221e-08, 1.352854445e-10)
+cos_terms = (0.9999999859, -0.4999998648, 0.0416664545, -0.001388763794, 2.476635379e-05, -2.704470886e-07, 1.712096229e-09)
+
+
+def window_rows():
+    rows = list(range(ROWS))
+    for group in range(HALO_TILES):
+        above = [-4 * (group + 1) + s for s in range(4)]
+        below = [ROWS + 4 * group + s for s in range(4)]
+        rows += below + above if group % 2 == 0 else above + below
+    return np.array(rows, np.int32)
+
+
+def band_matrices(coefficients, out_tiles, in_tiles, adjoint, first_row, plane_rows):
+    rows = window_rows()
+    m = np.arange(48 * out_tiles)
+    k = np.arange(48 * in_tiles)
+    row_m = rows[m // 48 * 8 + m % 8]
+    row_k = rows[k // 48 * 8 + k % 8]
+    plane_m = (m // 8) % 2
+    plane_k = (k // 8) % 2
+    part_k = (k // 16) % 3
+    tap_re = coefficients[:, 0].reshape(-1, 5, 3)
+    tap_im = coefficients[:, 1].reshape(-1, 5, 3)
+    if adjoint:
+        tap_re = tap_re[:, ::-1, ::-1]
+        tap_im = -tap_im[:, ::-1, ::-1]
+
+    def over_rows(taps):
+        wide = jnp.broadcast_to(taps[:, :, None, :, None], taps.shape[:2] + (out_tiles, 3, 16))
+        return wide.reshape(taps.shape[:2] + (48 * out_tiles,))
+
+    re_m = over_rows(tap_re)
+    im_m = over_rows(tap_im) * jnp.asarray(np.where(plane_m == 0, -1.0, 1.0), jnp.float32)
+    offset = jnp.asarray(row_k)[None, :] - jnp.asarray(row_m)[:, None]
+    same = jnp.asarray(plane_m)[:, None] == jnp.asarray(plane_k)[None, :]
+    total = 0.0
+    for a in range(5):
+        weight = jnp.where(same[None], re_m[:, a, :, None], im_m[:, a, :, None])
+        total = total + jnp.where((offset == a - 2)[None], weight, 0.0)
+    place = jnp.asarray(row_m) + first_row
+    inside = (place >= 0) & (place < plane_rows)
+    total = jnp.where(inside[None, :, None], total, 0.0)
+    high = lax.reduce_precision(total, 8, 7)
+    low = total - high
+    return jnp.where(jnp.asarray(part_k == 1)[None, None], low, high).astype(jnp.bfloat16)
+
+
+def pack_kernel(layers, width, step, surf, slow, pert, cross, chip, bulk, cross_far, chip_far):
+    depth = lax.axis_index("depth")
+    place = lax.axis_index("xy")
+    near = pl.ds(pl.multiple_of(depth * step, LANES), width)
+    far = pl.ds(pl.multiple_of((1 - depth) * step, LANES), width)
+    row = lax.broadcasted_iota(jnp.int32, (8, width), 0)
+
+    def edge_rows(down, lanes, put):
+        inner, outer = (1, 0) if down else (0, 1)
+
+        def tile(ref, level, index):
+            return ref[level, 8 * index : 8 * index + 8, lanes]
+
+        @pl.when(depth == 0)
+        def _():
+            put(0, tile(slow, 0, inner))
+            put(1, tile(slow, 1, inner))
+            turned = pltpu.roll(tile(slow, 1, outer), 4, 0)
+            if down:
+                extra = jnp.where(row < 2, pltpu.roll(tile(pert, 1, inner), 2, 0), turned)
+                put(2, jnp.where(row < 4, extra, tile(slow, 0, outer)))
+            else:
+                extra = jnp.where(row >= 6, pltpu.roll(tile(pert, 1, inner), 6, 0), turned)
+                put(2, jnp.where(row < 4, tile(slow, 0, outer), extra))
+
+        @pl.when(depth == 1)
+        def _():
+            put(0, tile(slow, 0, inner))
+            put(1, tile(pert, 1, inner))
+            put(2, tile(pert, 0, inner))
+
+    def into(ref, base):
+        def put(index, value):
+            ref[base + index] = value
+
+        return put
+
+    for f in range(2):
+        for part in range(2):
+            for index in range(2):
+                value = surf[f, part, 8 * index : 8 * index + 8, near]
+                cross[4 * f + 2 * part + index] = value
+                chip[4 * f + 2 * part + index] = value
+    for level in range(2):
+        for index in range(2):
+            bulk[2 * level + index] = slow[level, 8 * index : 8 * index + 8, far]
+            bulk[4 + 2 * level + index] = pert[level, 8 * index : 8 * index + 8, far]
+    for parity in range(2):
+
+        @pl.when(lax.rem(place, 2) == parity)
+        def _():
+            edge_rows(parity == 0, near, into(chip, 8))
+            edge_rows(parity == 0, far, into(chip_far, 0))
+            edge_rows(parity == 1, near, into(cross, 8))
+            edge_rows(parity == 1, far, into(cross_far, 0))
+
+
+def phase(angle):
+    square = angle * angle
+    cosine = cos_terms[-1]
+    sine = sin_terms[-1]
+    for term in cos_terms[-2::-1]:
+        cosine = cosine * square + term
+    for term in sin_terms[-2::-1]:
+        sine = sine * square + term
+    return cosine, sine * angle
+
+
+def sweep_kernel(
+    width, step, freqs, bands, back_bands, surf, slow, pert, cross, chip, bulk, cross_far, chip_far,
+    gradient, image, theirs, slow_win, pert_win, operand, phases, fields, image_win, grad_win,
+):
+    depth = lax.axis_index("depth")
+    place = lax.axis_index("xy")
+    half = width - LANES
+    near = pl.ds(pl.multiple_of(depth * step, LANES), width)
+    upper = lax.broadcasted_iota(jnp.int32, (8, width), 0) < 4
+    row = lax.broadcasted_iota(jnp.int32, (8, width), 0)
+    lane = lax.broadcasted_iota(jnp.int32, (16, width), 1)
+    even = lax.rem(place, 2) == 0
+
+    def sides(cross_tile, chip_tile):
+        return jnp.where(even, cross_tile, chip_tile), jnp.where(even, chip_tile, cross_tile)
+
+    for own in range(2):
+
+        @pl.when(depth == own)
+        def _():
+            for level in range(2):
+                for index in range(2):
+                    rows = slice(8 * index, 8 * index + 8)
+                    slow_win[2 * own + level, index] = slow[level, rows, near]
+                    pert_win[2 * own + level, index] = pert[level, rows, near]
+                    slow_win[2 * (1 - own) + level, index] = bulk[2 * level + index]
+                    pert_win[2 * (1 - own) + level, index] = bulk[4 + 2 * level + index]
+            first = (cross, chip, 8) if own == 0 else (cross_far, chip_far, 0)
+            second = (cross, chip, 8) if own == 1 else (cross_far, chip_far, 0)
+            above, below = zip(*[sides(first[0][first[2] + t], first[1][first[2] + t]) for t in range(3)])
+            for level in range(2):
+                slow_win[level, 2] = jnp.where(upper, below[level], above[level])
+                slow_win[level, 3] = jnp.where(upper, above[level], below[level])
+            slow_win[0, 4] = jnp.where(upper, below[2], above[2])
+            slow_win[1, 4] = pltpu.roll(jnp.where(upper, above[2], below[2]), 4, 0)
+            pert_win[1, 2] = jnp.where(
+                row < 2, pltpu.roll(below[2], 2, 0), jnp.where(row >= 6, pltpu.roll(above[2], 6, 0), 0.0)
+            )
+            above, below = zip(*[sides(second[0][second[2] + t], second[1][second[2] + t]) for t in range(3)])
+            slow_win[2, 2] = jnp.where(upper, below[0], above[0])
+            slow_win[2, 3] = jnp.where(upper, above[0], below[0])
+            pert_win[3, 2] = jnp.where(upper, below[1], above[1])
+            pert_win[3, 3] = jnp.where(upper, above[1], below[1])
+            pert_win[2, 2] = jnp.where(upper, below[2], above[2])
+
+    def store_operand(f, tile, value):
+        high = value.astype(jnp.bfloat16)
+        low = (value - high.astype(jnp.float32)).astype(jnp.bfloat16)
+        base = 48 * tile
+        operand[f, base : base + 16] = high
+        operand[f, base + 16 : base + 32] = high
+        operand[f, base + 32 : base + 48] = low
+
+    def stencil(f, matrix, out_tiles, in_tiles):
+        product = jnp.dot(
+            matrix[f, : 48 * out_tiles, : 48 * in_tiles],
+            operand[f, : 48 * in_tiles],
+            preferred_element_type=jnp.float32,
+        )
+        result = []
+        for tile in range(out_tiles):
+            base = 48 * tile
+            left = pltpu.roll(product[base : base + 16], 1, 1)
+            right = pltpu.roll(product[base + 32 : base + 48], width - 1, 1)
+            left = jnp.where(lane == 0, 0.0, left)
+            right = jnp.where(lane == width - 1, 0.0, right)
+            result.append(product[base + 16 : base + 32] + left + right)
+        return result
+
+    for f in range(2):
+        planes = []
+        for part in range(2):
+            at = 4 * f + 2 * part
+            above, below = zip(*[sides(cross[at + t], chip[at + t]) for t in range(2)])
+            planes.append(
+                [
+                    surf[f, part, 0:8, near],
+                    surf[f, part, 8:16, near],
+                    jnp.where(upper, below[0], above[1]),
+                    jnp.where(upper, above[1], below[0]),
+                    jnp.where(upper, below[1], above[0]),
+                    jnp.where(upper, above[0], below[1]),
+                ]
+            )
+        for tile in range(6):
+            store_operand(f, tile, jnp.concatenate([planes[0][tile], planes[1][tile]], axis=0))
+
+    def add_image(f, level, tile, re, im):
+        part = (re * re + im * im) * 0.5
+        image_win[level, tile] = part if f == 0 else image_win[level, tile] + part
+
+    def add_gradient(f, level, tile, w_re, w_im, u_re, u_im):
+        part = (0.25 * freqs[f]) * (w_im * u_re - w_re * u_im)
+        grad_win[level, tile] = part if f == 0 else grad_win[level, tile] + part
+
+    tiles = (6, 5, 5, 4)
+    for level in range(3):
+        for f in range(2):
+            fields_now = stencil(f, bands, tiles[level + 1], tiles[level])
+            for tile, value in enumerate(fields_now):
+                cosine, sine = phase(freqs[f] * 0.5 * slow_win[level, tile])
+                v_re, v_im = value[:8], value[8:]
+                re = cosine * v_re - sine * v_im
+                im = cosine * v_im + sine * v_re
+                both = jnp.concatenate([re, im], axis=0)
+                store_operand(f, tile, both)
+                if tile < 3:
+                    fields[f, level, tile] = both
+                    phases[f, level, tile] = jnp.concatenate([cosine, sine], axis=0)
+                if tile < 2:
+                    add_image(f, level, tile, re, im)
+    for f in range(2):
+        for tile, value in enumerate(stencil(f, bands, 4, 4)):
+            twice = 2.0 * pert_win[3, tile]
+            v_re, v_im = value[:8], value[8:]
+            if tile < 2:
+                cosine, sine = phase(freqs[f] * 0.5 * slow_win[3, tile])
+                re = cosine * v_re - sine * v_im
+                im = cosine * v_im + sine * v_re
+                add_image(f, 3, tile, re, im)
+                add_gradient(f, 3, tile, twice * re, twice * im, re, im)
+            store_operand(f, tile, jnp.concatenate([twice * v_re, twice * v_im], axis=0))
+    tiles = (2, 3, 3, 4)
+    for level in (2, 1, 0):
+        for f in range(2):
+            for tile, value in enumerate(stencil(f, back_bands, tiles[level], tiles[level + 1])):
+                twice = 2.0 * pert_win[level, tile]
+                u_re, u_im = fields[f, level, tile, :8], fields[f, level, tile, 8:]
+                w_re = value[:8] + twice * u_re
+                w_im = value[8:] + twice * u_im
+                if tile < 2:
+                    add_gradient(f, level, tile, w_re, w_im, u_re, u_im)
+                if level > 0:
+                    cosine, sine = phases[f, level, tile, :8], phases[f, level, tile, 8:]
+                    back = [cosine * w_re + sine * w_im, cosine * w_im - sine * w_re]
+                    store_operand(f, tile, jnp.concatenate(back, axis=0))
+
+    for own in range(2):
+
+        @pl.when(depth == own)
+        def _():
+            inner = slice(own * LANES, own * LANES + half)
+            outer = slice(own * half, own * half + half)
+            for level in range(2):
+                for tile in range(2):
+                    rows = slice(8 * tile, 8 * tile + 8)
+                    gradient[level, rows, outer] = grad_win[2 * own + level, tile, :, inner]
+                    image[level, rows, outer] = image_win[2 * own + level, tile, :, inner]
+                    theirs[0, level, rows] = grad_win[2 * (1 - own) + level, tile, :, inner]
+                    theirs[1, level, rows] = image_win[2 * (1 - own) + level, tile, :, inner]
+
+
+def split_columns(surface_data, frequencies, coefficients, slowness, perturbation):
+    count = lax.axis_size("xy")
+    columns = slowness.shape[2]
+    half = columns // 2
+    width = half + LANES
+    step = half - LANES
+    f32 = jnp.float32
+    axes = ("depth", "xy")
+
+    def moved(value, other_depth, neighbour):
+        pairs = []
+        for depth in range(2):
+            for place in range(count):
+                target = {"chip": place ^ 1, "cross": place + 1 if place % 2 else place - 1, "same": place}[neighbour]
+                if 0 <= target < count:
+                    layer = 1 - depth if other_depth else depth
+                    pairs.append((depth * count + place, layer * count + target))
+        return lax.ppermute(value, axes, pairs)
+
+    vmem = pl.BlockSpec(memory_space=pltpu.VMEM)
+    smem = pl.BlockSpec(memory_space=pltpu.SMEM)
+    tile = lambda n: jax.ShapeDtypeStruct((n, 8, width), f32)
+    cross, chip, bulk, cross_far, chip_far = pl.pallas_call(
+        lambda *refs: pack_kernel(2, width, step, *refs),
+        out_shape=(tile(11), tile(11), tile(8), tile(3), tile(3)),
+        in_specs=[vmem] * 3,
+        out_specs=(vmem,) * 5,
+        compiler_params=pltpu.CompilerParams(vmem_limit_bytes=32 * 2**20),
+        name="pack",
+    )(surface_data, slowness, perturbation)
+    cross = moved(cross, False, "cross")
+    bulk = moved(bulk, True, "same")
+    cross_far = moved(cross_far, True, "cross")
+    chip_far = moved(chip_far, True, "chip")
+    chip = moved(chip, False, "chip")
+
+    first_row = lax.axis_index("xy") * ROWS
+    bands = band_matrices(coefficients, 5, 6, False, first_row, count * ROWS)
+    back_bands = band_matrices(coefficients, 3, 4, True, first_row, count * ROWS)
+    own = jax.ShapeDtypeStruct((2, ROWS, columns), f32)
+    gradient, image, theirs = pl.pallas_call(
+        lambda *refs: sweep_kernel(width, step, *refs),
+        out_shape=(own, own, jax.ShapeDtypeStruct((2, 2, ROWS, half), f32)),
+        in_specs=[smem] + [vmem] * 10,
+        out_specs=(vmem,) * 3,
+        scratch_shapes=[
+            pltpu.VMEM((4, 5, 8, width), f32),
+            pltpu.VMEM((4, 4, 8, width), f32),
+            pltpu.VMEM((2, 288, width), jnp.bfloat16),
+            pltpu.VMEM((2, 3, 3, 16, width), f32),
+            pltpu.VMEM((2, 3, 3, 16, width), f32),
+            pltpu.VMEM((4, 2, 8, width), f32),
+            pltpu.VMEM((4, 2, 8, width), f32),
+        ],
+        compiler_params=pltpu.CompilerParams(vmem_limit_bytes=40 * 2**20),
+        name="sweep",
+    )(
+        frequencies, bands, back_bands, surface_data, slowness, perturbation,
+        cross, chip, bulk, cross_far, chip_far,
+    )
+    theirs = moved(theirs, True, "same")
+    start = (1 - lax.axis_index("depth")) * half
+    gradient = lax.dynamic_update_slice(gradient, theirs[0], (0, 0, start))
+    image = lax.dynamic_update_slice(image, theirs[1], (0, 0, start))
+    return gradient, image
+
+
+def on_slice(surface_data, frequencies, coefficients, slowness, perturbation):
+    levels, rows, columns = slowness.shape
+    fits = (
+        lax.axis_size("depth") == 2
+        and levels == 2
+        and rows == ROWS
+        and frequencies.shape[0] == 2
+        and lax.axis_size("xy") % 2 == 0
+        and columns % (2 * LANES) == 0
+        and columns >= 4 * LANES
+    )
+    plan = split_columns if fits else on_device
+    return plan(surface_data, frequencies, coefficients, slowness, perturbation)
+
+
 def solution(mesh):
     in_specs = (P(None, None, "xy", None), P(), P(), P("depth", "xy", None), P("depth", "xy", None))
     out_specs = (P("depth", "xy", None), P("depth", "xy", None))
     return jax.shard_map(
-        on_device, mesh=mesh, in_specs=in_specs, out_specs=out_specs, check_vma=False
+        on_slice, mesh=mesh, in_specs=in_specs, out_specs=out_specs, check_vma=False
     )

time: 172 us -> 39 us (0.23)
  the two profiles are of different devices: /device:TPU:20 before, /device:TPU:0 now
where the time goes in v1:
time: 39 us; the launch traced here: 38.6 us
  starting transfers between devices  11.9 us (31%)
  local copies, waits for them, and re-layouts  10.2 us (26%)
  waiting for transfers between devices  7.89 us (20%)
  Pallas kernels  5.57 us (14%)
  other arithmetic  2.08 us (5%)
  between operations  0.93 us (2%)
    ppermute x6, starting transfers between devices, moved(): return lax.ppermute(value, axes, pairs)  11.9 us
    unnamed x44, local copies, waits for them, and re-layouts  8.38 us
    ppermute x6, waiting for transfers between devices, moved(): return lax.ppermute(value, axes, pairs)  7.89 us
    pallas_call x1, Pallas kernels, split_columns(): pl.pallas_call(lambda *refs: sweep_kernel(width, step, *refs), out_shape=...  5.44 us
    convert_element_type x2, other arithmetic, band_matrices(): jnp.where(jnp.asarray(part_k == 1)[None, None], low, high)  1.36 us
  transfers between devices with their start and end apart: 6, of which 1 were waited for; matrix products, arithmetic and copies ran while one was open for 8% of the time, Pallas kernels for 0%

profile of v1, /device:TPU:0, one launch (start us, length us, event | category | flops | bytes accessed | tf_op | source)
XLA Modules:
  0.0 38.6 jit_solution(4951017992729233894)
XLA Ops:
  0.6 1.0 %copy-done = f32[2,2,16,2048]{3,2,1,0:T(8,128)S(1)} copy-done((f32[2,2,16,2048]{3,2,1,0:T(8,128)S(1)}, f32[2,2,16,2048]{3,2,1,0:T(8,128)}, u32[]{:S(2)}) %copy-start) | copy-done | bytes 524312
  1.7 0.9 %copy-done.2 = f32[2,16,2048]{2,1,0:T(8,128)S(1)} copy-done((f32[2,16,2048]{2,1,0:T(8,128)S(1)}, f32[2,16,2048]{2,1,0:T(8,128)}, u32[]{:S(2)}) %copy-start.2) | copy-done | bytes 262168
  2.6 0.9 %copy-done.4 = f32[2,16,2048]{2,1,0:T(8,128)S(1)} copy-done((f32[2,16,2048]{2,1,0:T(8,128)S(1)}, f32[2,16,2048]{2,1,0:T(8,128)}, u32[]{:S(2)}) %copy-start.4) | copy-done | bytes 262168
  3.7 0.7 %collective-permute-start.3 = (f32[3,8,1152]{2,1,0:T(8,128)S(1)}, f32[3,8,1152]{2,1,0:T(8,128)S(1)}, u32[]{:S(2)}, u32[]{:S(2)}) collective-permute-start(f32[3,8,1152]{2,1,0:T(8,128)S(1)} %get-tuple-element.13), channel_id=1, source_target_pairs={{1,18},{2,17},{3,20},{4,19},{5,22},{6,21},{7,24},{8,23},{9,26},{10... | collective-permute-start | bytes 331784 | tf_op jit(solution)/shard_map/ppermute | solution.py:455
  4.4 5.5 %collective-permute-start.4 = (f32[3,8,1152]{2,1,0:T(8,128)S(1)}, f32[3,8,1152]{2,1,0:T(8,128)S(1)}, u32[]{:S(2)}, u32[]{:S(2)}) collective-permute-start(f32[3,8,1152]{2,1,0:T(8,128)S(1)} %get-tuple-element.14), channel_id=1, source_target_pairs={{0,17},{1,16},{2,19},{3,18},{4,21},{5,20},{6,23},{7,22},{8,25},{9,... | collective-permute-start | bytes 331784 | tf_op jit(solution)/shard_map/ppermute | solution.py:455
  9.8 1.5 %collective-permute-start.2 = (f32[8,8,1152]{2,1,0:T(8,128)S(1)}, f32[8,8,1152]{2,1,0:T(8,128)S(1)}, u32[]{:S(2)}, u32[]{:S(2)}) collective-permute-start(f32[8,8,1152]{2,1,0:T(8,128)S(1)} %get-tuple-element.12), channel_id=1, source_target_pairs={{0,16},{1,17},{2,18},{3,19},{4,20},{5,21},{6,22},{7,23},{8,24},{9,... | collective-permute-start | bytes 884744 | tf_op jit(solution)/shard_map/ppermute | solution.py:455
  11.3 0.8 %collective-permute-start = (f32[11,8,1152]{2,1,0:T(8,128)S(1)}, f32[11,8,1152]{2,1,0:T(8,128)S(1)}, u32[]{:S(2)}, u32[]{:S(2)}) collective-permute-start(f32[11,8,1152]{2,1,0:T(8,128)S(1)} %get-tuple-element.10), channel_id=1, source_target_pairs={{1,2},{2,1},{3,4},{4,3},{5,6},{6,5},{7,8},{8,7},{9,10},{10,9},{11,... | collective-permute-start | bytes 1216520 | tf_op jit(solution)/shard_map/ppermute | solution.py:455
  12.1 2.9 %collective-permute-start.1 = (f32[11,8,1152]{2,1,0:T(8,128)S(1)}, f32[11,8,1152]{2,1,0:T(8,128)S(1)}, u32[]{:S(2)}, u32[]{:S(2)}) collective-permute-start(f32[11,8,1152]{2,1,0:T(8,128)S(1)} %get-tuple-element.11), channel_id=1, source_target_pairs={{0,1},{1,0},{2,3},{3,2},{4,5},{5,4},{6,7},{7,6},{8,9},{9,8},{10,11... | collective-permute-start | bytes 1216520 | tf_op jit(solution)/shard_map/ppermute | solution.py:455
  16.2 0.7 %copy-done.17 = s32[240]{0:T(256)S(1)} copy-done((s32[240]{0:T(256)S(1)}, s32[240]{0:T(256)}, u32[]{:S(2)}) %copy-start.17) | copy-done | bytes 984
  16.9 0.7 %copy-done.14 = s32[192]{0:T(256)S(1)} copy-done((s32[192]{0:T(256)S(1)}, s32[192]{0:T(256)}, u32[]{:S(2)}) %copy-start.14) | copy-done | bytes 792
  17.7 0.6 %copy-done.19 = f32[144]{0:T(256)S(1)} copy-done((f32[144]{0:T(256)S(1)}, f32[144]{0:T(256)}, u32[]{:S(2)}) %copy-start.19) | copy-done | bytes 600
  18.3 0.7 %copy-done.8 = s32[288]{0:T(512)S(1)} copy-done((s32[288]{0:T(512)S(1)}, s32[288]{0:T(512)}, u32[]{:S(2)}) %copy-start.8) | copy-done | bytes 1176
  19.1 0.6 %copy-done.18 = f32[240]{0:T(256)S(1)} copy-done((f32[240]{0:T(256)S(1)}, f32[240]{0:T(256)}, u32[]{:S(2)}) %copy-start.18) | copy-done | bytes 984
  19.7 0.7 %copy-done.11 = s32[144]{0:T(256)S(1)} copy-done((s32[144]{0:T(256)S(1)}, s32[144]{0:T(256)}, u32[]{:S(2)}) %copy-start.11) | copy-done | bytes 600
  20.5 0.5 %copy-done.7 = s32[288]{0:T(512)S(1)} copy-done((s32[288]{0:T(512)S(1)}, s32[288]{0:T(512)}, u32[]{:S(2)}) %copy-start.7) | copy-done | bytes 1176
  21.1 0.3 add_compare_fusion.4
  21.4 0.6 %copy-done.21 = pred[288]{0:T(512)(128)(4,1)S(1)} copy-done((pred[288]{0:T(512)(128)(4,1)S(1)}, pred[288]{0:T(512)(128)(4,1)}, u32[]{:S(2)}) %copy-start.21) | copy-done | bytes 312
  22.1 0.9 %fusion.refs_1_ = bf16[2,240,288]{2,1,0:T(8,128)(2,1)S(1)} fusion(f32[2,240]{1,0:T(2,128)S(1)} %get-tuple-element.38, f32[2,240]{1,0:T(2,128)S(1)} %get-tuple-element.55, f32[2,240]{1,0:T(2,128)S(1)} %get-tuple-element.39, f32[2,240]{1,0:T(2,128)S(1)} %get-tuple-element.54, f32[2,240]{1,0:T(2,128)S(1)} %get-tuple-element.40, ...), kind=kLoop, calls=%fused_computation.6 | loop fusion | flops 2626560 | bytes 710928 | tf_op jit(solution)/shard_map/convert_element_type | solution.py:215
  23.0 0.5 %fusion.1.refs_2_ = bf16[2,144,192]{2,1,0:T(8,128)(2,1)S(1)} fusion(f32[2,144]{1,0:T(2,128)S(1)} %get-tuple-element.28, f32[2,144]{1,0:T(2,128)S(1)} %get-tuple-element.60, f32[2,144]{1,0:T(2,128)S(1)} %get-tuple-element.29, f32[2,144]{1,0:T(2,128)S(1)} %get-tuple-element.59, f32[2,144]{1,0:T(2,128)S(1)} %get-tuple-element.30, ...), kind=kLoop, calls=%fused_computation.13 | loop fusion | flops 1050624 | bytes 288336 | tf_op jit(solution)/shard_map/convert_element_type | solution.py:215
  23.6 0.4 %copy-done.3 = f32[2,16,2048]{2,1,0:T(8,128)S(1)} copy-done((f32[2,16,2048]{2,1,0:T(8,128)S(1)}, f32[2,16,2048]{2,1,0:T(8,128)}, u32[]{:S(2)}) %copy-start.3) | copy-done | bytes 262168
  24.0 5.4 %sweep.1 = (f32[2,16,2048]{2,1,0:T(8,128)}, f32[2,16,2048]{2,1,0:T(8,128)}, f32[2,2,16,1024]{3,2,1,0:T(8,128)S(1)}) custom-call(f32[2]{0:T(128)S(1)} %copy-done.6, bf16[2,240,288]{2,1,0:T(8,128)(2,1)S(1)} %fusion.refs_1_, bf16[2,144,192]{2,1,0:T(8,128)(2,1)S(1)} %fusion.1.refs_2_, f32[2,2,16,2048]{3,2,1,0:T(8,128)S(1)} %copy-done.1, ...), custom_call_target="tpu_custom_call" | custom-call | tf_op jit(solution)/shard_map/sweep/pallas_call | solution.py:478
  29.4 0.6 %collective-permute-start.5 = (f32[2,2,16,1024]{3,2,1,0:T(8,128)S(1)}, f32[2,2,16,1024]{3,2,1,0:T(8,128)S(1)}, u32[]{:S(2)}, u32[]{:S(2)}) collective-permute-start(f32[2,2,16,1024]{3,2,1,0:T(8,128)S(1)} %get-tuple-element.16), channel_id=1, source_target_pairs={{0,16},{1,17},{2,18},{3,19},{4,20},{5,21},{6,22},{7,23},{8,24},{9,... | collective-permute-start | bytes 786440 | tf_op jit(solution)/shard_map/ppermute | solution.py:455
  30.0 7.9 %collective-permute-done.5 = f32[2,2,16,1024]{3,2,1,0:T(8,128)S(1)} collective-permute-done((f32[2,2,16,1024]{3,2,1,0:T(8,128)S(1)}, f32[2,2,16,1024]{3,2,1,0:T(8,128)S(1)}, u32[]{:S(2)}, u32[]{:S(2)}) %collective-permute-start.5) | collective-permute-done | bytes 262176 | tf_op jit(solution)/shard_map/ppermute | solution.py:455
  37.8 0.7 %fusion.2 = (f32[2,16,2048]{2,1,0:T(8,128)}, f32[2,16,2048]{2,1,0:T(8,128)}) fusion(f32[2,16,2048]{2,1,0:T(8,128)} %get-tuple-element.17, s32[]{:T(128)S(6)} %select_n.108, f32[2,2,16,1024]{3,2,1,0:T(8,128)S(1)} %collective-permute-done.5, f32[2,16,2048]{2,1,0:T(8,128)} %get-tuple-element.15), kind=kLoop, calls=%fused_computation.16 | loop fusion | bytes 524292 | tf_op jit(solution)/shard_map/dynamic_update_slice | solution.py:501
  (65 shorter events, 1.8 us)
Async XLA Ops:
  0.6 1.0 %copy-start = (f32[2,2,16,2048]{3,2,1,0:T(8,128)S(1)}, f32[2,2,16,2048]{3,2,1,0:T(8,128)}, u32[]{:S(2)}) copy-start(f32[2,2,16,2048]{3,2,1,0:T(8,128)} %refs_3_.1) | copy-start | bytes 1572868
  1.7 0.9 %copy-start.2 = (f32[2,16,2048]{2,1,0:T(8,128)S(1)}, f32[2,16,2048]{2,1,0:T(8,128)}, u32[]{:S(2)}) copy-start(f32[2,16,2048]{2,1,0:T(8,128)} %refs_4_.1) | copy-start | bytes 786436
  2.6 0.9 %copy-start.4 = (f32[2,16,2048]{2,1,0:T(8,128)S(1)}, f32[2,16,2048]{2,1,0:T(8,128)}, u32[]{:S(2)}) copy-start(f32[2,16,2048]{2,1,0:T(8,128)} %refs_5_.1) | copy-start | bytes 786436
  3.7 19.8 %collective-permute-start.3 = (f32[3,8,1152]{2,1,0:T(8,128)S(1)}, f32[3,8,1152]{2,1,0:T(8,128)S(1)}, u32[]{:S(2)}, u32[]{:S(2)}) collective-permute-start(f32[3,8,1152]{2,1,0:T(8,128)S(1)} %get-tuple-element.13), channel_id=1, source_target_pairs={{1,18},{2,17},{3,20},{4,19},{5,22},{6,21},{7,24},{8,23},{9,26},{10... | collective-permute-start | bytes 331784 | tf_op jit(solution)/shard_map/ppermute | solution.py:455
  4.4 19.1 %collective-permute-start.4 = (f32[3,8,1152]{2,1,0:T(8,128)S(1)}, f32[3,8,1152]{2,1,0:T(8,128)S(1)}, u32[]{:S(2)}, u32[]{:S(2)}) collective-permute-start(f32[3,8,1152]{2,1,0:T(8,128)S(1)} %get-tuple-element.14), channel_id=1, source_target_pairs={{0,17},{1,16},{2,19},{3,18},{4,21},{5,20},{6,23},{7,22},{8,25},{9,... | collective-permute-start | bytes 331784 | tf_op jit(solution)/shard_map/ppermute | solution.py:455
  9.8 13.7 %collective-permute-start.2 = (f32[8,8,1152]{2,1,0:T(8,128)S(1)}, f32[8,8,1152]{2,1,0:T(8,128)S(1)}, u32[]{:S(2)}, u32[]{:S(2)}) collective-permute-start(f32[8,8,1152]{2,1,0:T(8,128)S(1)} %get-tuple-element.12), channel_id=1, source_target_pairs={{0,16},{1,17},{2,18},{3,19},{4,20},{5,21},{6,22},{7,23},{8,24},{9,... | collective-permute-start | bytes 884744 | tf_op jit(solution)/shard_map/ppermute | solution.py:455
  11.3 3.7 %copy-start.9 = (f32[2,2,15]{2,1,0:T(2,128)S(1)}, f32[2,2,15]{2,1,0:T(2,128)}, u32[]{:S(2)}) copy-start(f32[2,2,15]{2,1,0:T(2,128)} %param.19) | copy-start | bytes 724
  11.3 12.2 %collective-permute-start = (f32[11,8,1152]{2,1,0:T(8,128)S(1)}, f32[11,8,1152]{2,1,0:T(8,128)S(1)}, u32[]{:S(2)}, u32[]{:S(2)}) collective-permute-start(f32[11,8,1152]{2,1,0:T(8,128)S(1)} %get-tuple-element.10), channel_id=1, source_target_pairs={{1,2},{2,1},{3,4},{4,3},{5,6},{6,5},{7,8},{8,7},{9,10},{10,9},{11,... | collective-permute-start | bytes 1216520 | tf_op jit(solution)/shard_map/ppermute | solution.py:455
  12.1 11.4 %collective-permute-start.1 = (f32[11,8,1152]{2,1,0:T(8,128)S(1)}, f32[11,8,1152]{2,1,0:T(8,128)S(1)}, u32[]{:S(2)}, u32[]{:S(2)}) collective-permute-start(f32[11,8,1152]{2,1,0:T(8,128)S(1)} %get-tuple-element.11), channel_id=1, source_target_pairs={{0,1},{1,0},{2,3},{3,2},{4,5},{5,4},{6,7},{7,6},{8,9},{9,8},{10,11... | collective-permute-start | bytes 1216520 | tf_op jit(solution)/shard_map/ppermute | solution.py:455
  16.2 0.7 %copy-start.17 = (s32[240]{0:T(256)S(1)}, s32[240]{0:T(256)}, u32[]{:S(2)}) copy-start(s32[240]{0:T(256)} %constant.20.clone) | copy-start | bytes 2884
  16.9 0.7 %copy-start.15 = (s32[144]{0:T(256)S(1)}, s32[144]{0:T(256)}, u32[]{:S(2)}) copy-start(s32[144]{0:T(256)} %constant.72.clone) | copy-start | bytes 1732
  18.3 0.7 %copy-start.8 = (s32[288]{0:T(512)S(1)}, s32[288]{0:T(512)}, u32[]{:S(2)}) copy-start(s32[288]{0:T(512)} %constant.22.clone) | copy-start | bytes 3460
  18.3 0.7 %copy-start.13 = (s32[240]{0:T(256)S(1)}, s32[240]{0:T(256)}, u32[]{:S(2)}) copy-start(s32[240]{0:T(256)} %constant.21.clone) | copy-start | bytes 2884
  19.0 0.7 %copy-start.18 = (f32[240]{0:T(256)S(1)}, f32[240]{0:T(256)}, u32[]{:S(2)}) copy-start(f32[240]{0:T(256)} %constant.18.clone) | copy-start | bytes 2884
  19.7 0.7 %copy-start.12 = (s32[192]{0:T(256)S(1)}, s32[192]{0:T(256)}, u32[]{:S(2)}) copy-start(s32[192]{0:T(256)} %constant.70.clone) | copy-start | bytes 2308
  20.4 0.7 %copy-start.7 = (s32[288]{0:T(512)S(1)}, s32[288]{0:T(512)}, u32[]{:S(2)}) copy-start(s32[288]{0:T(512)} %constant.19.clone) | copy-start | bytes 3460
  20.4 0.7 %copy-start.10 = (s32[240]{0:T(256)S(1)}, s32[240]{0:T(256)}, u32[]{:S(2)}) copy-start(s32[240]{0:T(256)} %constant.75) | copy-start | bytes 2884
  22.0 0.9 %copy-start.16 = (s32[144]{0:T(256)S(1)}, s32[144]{0:T(256)}, u32[]{:S(2)}) copy-start(s32[144]{0:T(256)} %constant.71.clone) | copy-start | bytes 1732
  22.0 0.9 %copy-start.20 = (pred[192]{0:T(512)(128)(4,1)S(1)}, pred[192]{0:T(512)(128)(4,1)}, u32[]{:S(2)}) copy-start(pred[192]{0:T(512)(128)(4,1)} %constant.74.clone) | copy-start | bytes 580
  22.0 1.5 %copy-start.1 = (f32[2,2,16,2048]{3,2,1,0:T(8,128)S(1)}, f32[2,2,16,2048]{3,2,1,0:T(8,128)}, u32[]{:S(2)}) copy-start(f32[2,2,16,2048]{3,2,1,0:T(8,128)} %refs_3_.1) | copy-start | bytes 1572868
  22.1 1.5 %copy-start.5 = (f32[2,16,2048]{2,1,0:T(8,128)S(1)}, f32[2,16,2048]{2,1,0:T(8,128)}, u32[]{:S(2)}) copy-start(f32[2,16,2048]{2,1,0:T(8,128)} %refs_5_.1) | copy-start | bytes 786436
  23.0 1.0 %copy-start.3 = (f32[2,16,2048]{2,1,0:T(8,128)S(1)}, f32[2,16,2048]{2,1,0:T(8,128)}, u32[]{:S(2)}) copy-start(f32[2,16,2048]{2,1,0:T(8,128)} %refs_4_.1) | copy-start | bytes 786436
  23.0 1.0 %copy-start.6 = (f32[2]{0:T(128)S(1)}, f32[2]{0:T(128)}, u32[]{:S(2)}) copy-start(f32[2]{0:T(128)} %refs_0_.3) | copy-start | bytes 28
  29.4 8.4 %collective-permute-start.5 = (f32[2,2,16,1024]{3,2,1,0:T(8,128)S(1)}, f32[2,2,16,1024]{3,2,1,0:T(8,128)S(1)}, u32[]{:S(2)}, u32[]{:S(2)}) collective-permute-start(f32[2,2,16,1024]{3,2,1,0:T(8,128)S(1)} %get-tuple-element.16), channel_id=1, source_target_pairs={{0,16},{1,17},{2,18},{3,19},{4,20},{5,21},{6,22},{7,23},{8,24},{9,... | collective-permute-start | bytes 786440 | tf_op jit(solution)/shard_map/ppermute | solution.py:455
  (4 other events, 2.7 us)

commit v2 on v1

--- a/solution.py
+++ b/solution.py
@@ -171,51 +171,66 @@
 cos_terms = (0.9999999859, -0.4999998648, 0.0416664545, -0.001388763794, 2.476635379e-05, -2.704470886e-07, 1.712096229e-09)
 
 
-def window_rows():
-    rows = list(range(ROWS))
-    for group in range(HALO_TILES):
-        above = [-4 * (group + 1) + s for s in range(4)]
-        below = [ROWS + 4 * group + s for s in range(4)]
-        rows += below + above if group % 2 == 0 else above + below
-    return np.array(rows, np.int32)
-
-
-def band_matrices(coefficients, out_tiles, in_tiles, adjoint, first_row, plane_rows):
-    rows = window_rows()
-    m = np.arange(48 * out_tiles)
-    k = np.arange(48 * in_tiles)
-    row_m = rows[m // 48 * 8 + m % 8]
-    row_k = rows[k // 48 * 8 + k % 8]
-    plane_m = (m // 8) % 2
-    plane_k = (k // 8) % 2
-    part_k = (k // 16) % 3
-    tap_re = coefficients[:, 0].reshape(-1, 5, 3)
-    tap_im = coefficients[:, 1].reshape(-1, 5, 3)
-    if adjoint:
-        tap_re = tap_re[:, ::-1, ::-1]
-        tap_im = -tap_im[:, ::-1, ::-1]
-
-    def over_rows(taps):
-        wide = jnp.broadcast_to(taps[:, :, None, :, None], taps.shape[:2] + (out_tiles, 3, 16))
-        return wide.reshape(taps.shape[:2] + (48 * out_tiles,))
-
-    re_m = over_rows(tap_re)
-    im_m = over_rows(tap_im) * jnp.asarray(np.where(plane_m == 0, -1.0, 1.0), jnp.float32)
-    offset = jnp.asarray(row_k)[None, :] - jnp.asarray(row_m)[:, None]
-    same = jnp.asarray(plane_m)[:, None] == jnp.asarray(plane_k)[None, :]
-    total = 0.0
-    for a in range(5):
-        weight = jnp.where(same[None], re_m[:, a, :, None], im_m[:, a, :, None])
-        total = total + jnp.where((offset == a - 2)[None], weight, 0.0)
-    place = jnp.asarray(row_m) + first_row
-    inside = (place >= 0) & (place < plane_rows)
-    total = jnp.where(inside[None, :, None], total, 0.0)
-    high = lax.reduce_precision(total, 8, 7)
-    low = total - high
-    return jnp.where(jnp.asarray(part_k == 1)[None, None], low, high).astype(jnp.bfloat16)
-
-
-def pack_kernel(layers, width, step, surf, slow, pert, cross, chip, bulk, cross_far, chip_far):
+def window_row(tile, sub):
+    group = tile - 2
+    above = sub - 4 * (group + 1)
+    below = sub + ROWS + 4 * group
+    even = jnp.where(sub < 4, below, above - 4)
+    odd = jnp.where(sub < 4, above, below - 4)
+    halo = jnp.where(lax.rem(tile, 2) == 0, even, odd)
+    return jnp.where(tile < 2, 8 * tile + sub, halo)
+
+
+def band_kernel(plane_rows, taps, bands, back_bands):
+    first_row = lax.axis_index("xy") * ROWS
+
+    def fill(ref, adjoint):
+        out_tiles = ref.shape[1] // 48
+        in_tiles = ref.shape[2] // 48
+        shape = (16, ref.shape[2])
+        col = lax.broadcasted_iota(jnp.int32, shape, 1)
+        sub = lax.broadcasted_iota(jnp.int32, shape, 0)
+        tile_k = sum((col >= 48 * t).astype(jnp.int32) for t in range(1, in_tiles))
+        row_k = window_row(tile_k, col & 7)
+        part_k = (col >> 4) - 3 * tile_k
+        plane_k = (col >> 3) & 1
+        plane_m = sub >> 3
+        same = plane_k == plane_m
+        inside_k = (row_k + first_row >= 0) & (row_k + first_row < plane_rows)
+        for tile in range(out_tiles):
+            row_m = window_row(jnp.full(shape, tile, jnp.int32), sub & 7)
+            inside = inside_k & (row_m + first_row >= 0) & (row_m + first_row < plane_rows)
+            offset = jnp.where(inside, row_k - row_m, 9)
+            hits = [offset == a - 2 for a in range(5)]
+            for f in range(ref.shape[0]):
+                for b in range(3):
+                    total = jnp.zeros(shape, jnp.float32)
+                    for a in range(5):
+                        tap = 3 * (4 - a) + 2 - b if adjoint else 3 * a + b
+                        re = taps[f, 0, tap]
+                        im = -taps[f, 1, tap] if adjoint else taps[f, 1, tap]
+                        crossed = jnp.where(plane_m == 0, -im, im)
+                        total = jnp.where(hits[a], jnp.where(same, re, crossed), total)
+                    high = total.astype(jnp.bfloat16)
+                    low = total - high.astype(jnp.float32)
+                    base = 48 * tile + 16 * b
+                    ref[f, base : base + 16] = jnp.where(part_k == 1, low, total).astype(jnp.bfloat16)
+
+    fill(bands, False)
+    fill(back_bands, True)
+
+
+def pack_kernel(
+    width, step, surf_in, slow_in, pert_in, cross, chip, bulk, cross_far, chip_far, window, surf, slow, pert, sems
+):
+    copies = [
+        pltpu.make_async_copy(source, target, sems.at[n])
+        for n, (source, target) in enumerate(((slow_in, slow), (pert_in, pert), (surf_in, surf)))
+    ]
+    for copy in copies:
+        copy.start()
+    for copy in copies:
+        copy.wait()
     depth = lax.axis_index("depth")
     place = lax.axis_index("xy")
     near = pl.ds(pl.multiple_of(depth * step, LANES), width)
@@ -258,8 +273,11 @@
                 value = surf[f, part, 8 * index : 8 * index + 8, near]
                 cross[4 * f + 2 * part + index] = value
                 chip[4 * f + 2 * part + index] = value
+                window[4 * f + 2 * part + index] = value
     for level in range(2):
         for index in range(2):
+            window[8 + 2 * level + index] = slow[level, 8 * index : 8 * index + 8, near]
+            window[12 + 2 * level + index] = pert[level, 8 * index : 8 * index + 8, near]
             bulk[2 * level + index] = slow[level, 8 * index : 8 * index + 8, far]
             bulk[4 + 2 * level + index] = pert[level, 8 * index : 8 * index + 8, far]
     for parity in range(2):
@@ -284,13 +302,12 @@
 
 
 def sweep_kernel(
-    width, step, freqs, bands, back_bands, surf, slow, pert, cross, chip, bulk, cross_far, chip_far,
+    width, freqs, bands, back_bands, window, cross, chip, bulk, cross_far, chip_far,
     gradient, image, theirs, slow_win, pert_win, operand, phases, fields, image_win, grad_win,
 ):
     depth = lax.axis_index("depth")
     place = lax.axis_index("xy")
     half = width - LANES
-    near = pl.ds(pl.multiple_of(depth * step, LANES), width)
     upper = lax.broadcasted_iota(jnp.int32, (8, width), 0) < 4
     row = lax.broadcasted_iota(jnp.int32, (8, width), 0)
     lane = lax.broadcasted_iota(jnp.int32, (16, width), 1)
@@ -305,9 +322,8 @@
         def _():
             for level in range(2):
                 for index in range(2):
-                    rows = slice(8 * index, 8 * index + 8)
-                    slow_win[2 * own + level, index] = slow[level, rows, near]
-                    pert_win[2 * own + level, index] = pert[level, rows, near]
+                    slow_win[2 * own + level, index] = window[8 + 2 * level + index]
+                    pert_win[2 * own + level, index] = window[12 + 2 * level + index]
                     slow_win[2 * (1 - own) + level, index] = bulk[2 * level + index]
                     pert_win[2 * (1 - own) + level, index] = bulk[4 + 2 * level + index]
             first = (cross, chip, 8) if own == 0 else (cross_far, chip_far, 0)
@@ -359,8 +375,8 @@
             above, below = zip(*[sides(cross[at + t], chip[at + t]) for t in range(2)])
             planes.append(
                 [
-                    surf[f, part, 0:8, near],
-                    surf[f, part, 8:16, near],
+                    window[at],
+                    window[at + 1],
                     jnp.where(upper, below[0], above[1]),
                     jnp.where(upper, above[1], below[0]),
                     jnp.where(upper, below[1], above[0]),
@@ -457,28 +473,39 @@
     vmem = pl.BlockSpec(memory_space=pltpu.VMEM)
     smem = pl.BlockSpec(memory_space=pltpu.SMEM)
     tile = lambda n: jax.ShapeDtypeStruct((n, 8, width), f32)
-    cross, chip, bulk, cross_far, chip_far = pl.pallas_call(
-        lambda *refs: pack_kernel(2, width, step, *refs),
-        out_shape=(tile(11), tile(11), tile(8), tile(3), tile(3)),
-        in_specs=[vmem] * 3,
-        out_specs=(vmem,) * 5,
+    cross, chip, bulk, cross_far, chip_far, window = pl.pallas_call(
+        lambda *refs: pack_kernel(width, step, *refs),
+        out_shape=(tile(11), tile(11), tile(8), tile(3), tile(3), tile(16)),
+        in_specs=[pl.BlockSpec(memory_space=pltpu.HBM)] * 3,
+        out_specs=(vmem,) * 6,
+        scratch_shapes=[
+            pltpu.VMEM(surface_data.shape, f32),
+            pltpu.VMEM(slowness.shape, f32),
+            pltpu.VMEM(perturbation.shape, f32),
+            pltpu.SemaphoreType.DMA((3,)),
+        ],
         compiler_params=pltpu.CompilerParams(vmem_limit_bytes=32 * 2**20),
         name="pack",
-    )(surface_data, slowness, perturbation)
+    )(*(pltpu.with_memory_space_constraint(x, pltpu.HBM) for x in (surface_data, slowness, perturbation)))
     cross = moved(cross, False, "cross")
     bulk = moved(bulk, True, "same")
     cross_far = moved(cross_far, True, "cross")
     chip_far = moved(chip_far, True, "chip")
     chip = moved(chip, False, "chip")
 
-    first_row = lax.axis_index("xy") * ROWS
-    bands = band_matrices(coefficients, 5, 6, False, first_row, count * ROWS)
-    back_bands = band_matrices(coefficients, 3, 4, True, first_row, count * ROWS)
+    bands, back_bands = pl.pallas_call(
+        lambda *refs: band_kernel(count * ROWS, *refs),
+        out_shape=(jax.ShapeDtypeStruct((2, 240, 288), jnp.bfloat16), jax.ShapeDtypeStruct((2, 144, 192), jnp.bfloat16)),
+        in_specs=[smem],
+        out_specs=(vmem,) * 2,
+        compiler_params=pltpu.CompilerParams(vmem_limit_bytes=16 * 2**20),
+        name="bands",
+    )(coefficients)
     own = jax.ShapeDtypeStruct((2, ROWS, columns), f32)
     gradient, image, theirs = pl.pallas_call(
-        lambda *refs: sweep_kernel(width, step, *refs),
+        lambda *refs: sweep_kernel(width, *refs),
         out_shape=(own, own, jax.ShapeDtypeStruct((2, 2, ROWS, half), f32)),
-        in_specs=[smem] + [vmem] * 10,
+        in_specs=[smem] + [vmem] * 8,
         out_specs=(vmem,) * 3,
         scratch_shapes=[
             pltpu.VMEM((4, 5, 8, width), f32),
@@ -492,8 +519,7 @@
         compiler_params=pltpu.CompilerParams(vmem_limit_bytes=40 * 2**20),
         name="sweep",
     )(
-        frequencies, bands, back_bands, surface_data, slowness, perturbation,
-        cross, chip, bulk, cross_far, chip_far,
+        frequencies, bands, back_bands, window, cross, chip, bulk, cross_far, chip_far,
     )
     theirs = moved(theirs, True, "same")
     start = (1 - lax.axis_index("depth")) * half

time: 39 us -> 35.8 us (0.918)
  local copies, waits for them, and re-layouts: 10.2 us -> 1.37 us
  waiting for transfers between devices: 7.89 us -> 12.7 us
  Pallas kernels: 5.57 us -> 8.21 us
  other arithmetic: 2.08 us -> 0 us
  starting transfers between devices: 11.9 us -> 12.7 us
    unnamed x44 -> x4, local copies, waits for them, and re-layouts: 8.38 us -> 0.65 us
    ppermute x6, waiting for transfers between devices: 7.89 us -> 12.7 us  [moved(): return lax.ppermute(value, axes, pairs)]
    pallas_call x2 -> x3, Pallas kernels: 5.57 us -> 8.21 us  [the longest x1 5.37 us: split_columns(): pl.pallas_call(lambda *refs: sweep_kernel(width, *refs), out_shape=(own,...]
    convert_element_type x2 -> x0, other arithmetic: 1.36 us -> none  [band_matrices(): jnp.where(jnp.asarray(part_k == 1)[None, None], low, high)]
    ppermute x6, starting transfers between devices: 11.9 us -> 12.7 us  [moved(): return lax.ppermute(value, axes, pairs)]
    eq x4 -> x0, other arithmetic: 0.68 us -> none  [the longest x2 0.48 us: band_matrices(): total = total + jnp.where((offset == a - 2)[None], weight, 0.0)]
    broadcast_in_dim x10 -> x0, local copies, waits for them, and re-layouts: 0.49 us -> none  [the longest x8 0.47 us: over_rows(): jnp.broadcast_to(taps[:, :, None, :, None], taps.shape[:2] + (out_tiles,...]
    reshape x4 -> x0, local copies, waits for them, and re-layouts: 0.44 us -> none  [over_rows(): return wide.reshape(taps.shape[:2] + (48 * out_tiles,))]
  transfers between devices with their start and end apart: 6 -> 6, of which waited for: 1 -> 2; matrix products, arithmetic and copies ran while one was open for 8% -> 0% of each run, Pallas kernels for 0% -> 4%
where the time goes in v2:
time: 35.8 us; the launch traced here: 35.6 us
  starting transfers between devices  12.7 us (35%)
  waiting for transfers between devices  12.7 us (35%)
  Pallas kernels  8.21 us (23%)
  local copies, waits for them, and re-layouts  1.37 us (4%)
  between operations  0.69 us (2%)
    ppermute x6, starting transfers between devices, moved(): return lax.ppermute(value, axes, pairs)  12.7 us
    ppermute x6, waiting for transfers between devices, moved(): return lax.ppermute(value, axes, pairs)  12.7 us
    pallas_call x1, Pallas kernels, split_columns(): pl.pallas_call(lambda *refs: sweep_kernel(width, *refs), out_shape=(own,...  5.37 us
    pallas_call x1, Pallas kernels, split_columns(): pl.pallas_call(lambda *refs: band_kernel(count * ROWS, *refs), out_shape=...  1.45 us
    pallas_call x1, Pallas kernels, split_columns(): pl.pallas_call(lambda *refs: pack_kernel(width, step, *refs), out_shape=(...  1.39 us
    dynamic_update_slice x1, local copies, waits for them, and re-layouts, split_columns(): image = lax.dynamic_update_slice(image, theirs[1], (0, 0, start))  0.72 us
  transfers between devices with their start and end apart: 6, of which 2 were waited for; matrix products, arithmetic and copies ran while one was open for 0% of the time, Pallas kernels for 4%

profile of v2, /device:TPU:0, one launch (start us, length us, event | category | flops | bytes accessed | tf_op | source)
XLA Modules:
  0.0 35.6 jit_solution(12664130007809577536)
XLA Ops:
  0.6 1.4 %pack.1 = (f32[11,8,1152]{2,1,0:T(8,128)S(1)}, f32[11,8,1152]{2,1,0:T(8,128)S(1)}, f32[8,8,1152]{2,1,0:T(8,128)S(1)}, f32[3,8,1152]{2,1,0:T(8,128)S(1)}, f32[3,8...) custom-call(f32[2,2,16,2048]{3,2,1,0:T(8,128)} %refs_0_.4, f32[2,16,2048]{2,1,0:T(8,128)} %refs_1_.1, f32[2,16,2048]{2,1,0:T(8,128)} %refs_2_.1), custom_call_target="tpu_custom_call" | custom-call | tf_op jit(solution)/shard_map/pack/pallas_call | solution.py:476
  2.0 0.7 %collective-permute-start = (f32[11,8,1152]{2,1,0:T(8,128)S(1)}, f32[11,8,1152]{2,1,0:T(8,128)S(1)}, u32[]{:S(2)}, u32[]{:S(2)}) collective-permute-start(f32[11,8,1152]{2,1,0:T(8,128)S(1)} %get-tuple-element.16), channel_id=1, source_target_pairs={{1,2},{2,1},{3,4},{4,3},{5,6},{6,5},{7,8},{8,7},{9,10},{10,9},{11,... | collective-permute-start | bytes 1216520 | tf_op jit(solution)/shard_map/ppermute | solution.py:471
  2.7 4.4 %collective-permute-start.1 = (f32[11,8,1152]{2,1,0:T(8,128)S(1)}, f32[11,8,1152]{2,1,0:T(8,128)S(1)}, u32[]{:S(2)}, u32[]{:S(2)}) collective-permute-start(f32[11,8,1152]{2,1,0:T(8,128)S(1)} %get-tuple-element.17), channel_id=1, source_target_pairs={{0,1},{1,0},{2,3},{3,2},{4,5},{5,4},{6,7},{7,6},{8,9},{9,8},{10,11... | collective-permute-start | bytes 1216520 | tf_op jit(solution)/shard_map/ppermute | solution.py:471
  7.1 0.0 copy-start
  7.1 1.5 %collective-permute-start.2 = (f32[8,8,1152]{2,1,0:T(8,128)S(1)}, f32[8,8,1152]{2,1,0:T(8,128)S(1)}, u32[]{:S(2)}, u32[]{:S(2)}) collective-permute-start(f32[8,8,1152]{2,1,0:T(8,128)S(1)} %get-tuple-element.18), channel_id=1, source_target_pairs={{0,16},{1,17},{2,18},{3,19},{4,20},{5,21},{6,22},{7,23},{8,24},{9,... | collective-permute-start | bytes 884744 | tf_op jit(solution)/shard_map/ppermute | solution.py:471
  8.6 0.7 %collective-permute-start.3 = (f32[3,8,1152]{2,1,0:T(8,128)S(1)}, f32[3,8,1152]{2,1,0:T(8,128)S(1)}, u32[]{:S(2)}, u32[]{:S(2)}) collective-permute-start(f32[3,8,1152]{2,1,0:T(8,128)S(1)} %get-tuple-element.19), channel_id=1, source_target_pairs={{1,18},{2,17},{3,20},{4,19},{5,22},{6,21},{7,24},{8,23},{9,26},{10... | collective-permute-start | bytes 331784 | tf_op jit(solution)/shard_map/ppermute | solution.py:471
  9.2 4.0 %collective-permute-start.4 = (f32[3,8,1152]{2,1,0:T(8,128)S(1)}, f32[3,8,1152]{2,1,0:T(8,128)S(1)}, u32[]{:S(2)}, u32[]{:S(2)}) collective-permute-start(f32[3,8,1152]{2,1,0:T(8,128)S(1)} %get-tuple-element.20), channel_id=1, source_target_pairs={{0,17},{1,16},{2,19},{3,18},{4,21},{5,20},{6,23},{7,22},{8,25},{9,... | collective-permute-start | bytes 331784 | tf_op jit(solution)/shard_map/ppermute | solution.py:471
  13.2 0.0 copy-done
  13.2 1.4 %bands.1 = (bf16[2,240,288]{2,1,0:T(8,128)(2,1)S(1)}, bf16[2,144,192]{2,1,0:T(8,128)(2,1)S(1)}) custom-call(f32[2,2,15]{2,1,0:T(2,128)S(1)} %copy-done), custom_call_target="tpu_custom_call" | custom-call | tf_op jit(solution)/shard_map/bands/pallas_call | solution.py:496
  14.7 0.0 collective-permute-done.3.refs_7_
  14.7 6.1 %collective-permute-done.4.refs_8_ = f32[3,8,1152]{2,1,0:T(8,128)S(1)} collective-permute-done((f32[3,8,1152]{2,1,0:T(8,128)S(1)}, f32[3,8,1152]{2,1,0:T(8,128)S(1)}, u32[]{:S(2)}, u32[]{:S(2)}) %collective-permute-start.4) | collective-permute-done | bytes 110624 | tf_op jit(solution)/shard_map/ppermute | solution.py:471
  20.8 0.0 collective-permute-done.2.refs_6_
  20.8 0.0 collective-permute-done.refs_4_
  20.8 0.0 collective-permute-done.1.refs_5_
  20.9 0.0 copy-start.1
  20.9 0.6 %copy-done.1 = f32[2]{0:T(128)S(1)} copy-done((f32[2]{0:T(128)S(1)}, f32[2]{0:T(128)}, u32[]{:S(2)}) %copy-start.1) | copy-done | bytes 32
  21.5 5.4 %sweep.1 = (f32[2,16,2048]{2,1,0:T(8,128)}, f32[2,16,2048]{2,1,0:T(8,128)}, f32[2,2,16,1024]{3,2,1,0:T(8,128)S(1)}) custom-call(f32[2]{0:T(128)S(1)} %copy-done.1, bf16[2,240,288]{2,1,0:T(8,128)(2,1)S(1)} %get-tuple-element.13.refs_1_, bf16[2,144,192]{2,1,0:T(8,128)(2,1)S(1)} %get-tuple-element.14.refs_2_, f32[16,8,1152]{2,1,0:T(8,128)S(1)} %get-tuple-element.15.refs_3_, ...), custom_call_target="tpu_custom_call" | custom-call | tf_op jit(solution)/shard_map/sweep/pallas_call | solution.py:505
  26.9 1.5 %collective-permute-start.5 = (f32[2,2,16,1024]{3,2,1,0:T(8,128)S(1)}, f32[2,2,16,1024]{3,2,1,0:T(8,128)S(1)}, u32[]{:S(2)}, u32[]{:S(2)}) collective-permute-start(f32[2,2,16,1024]{3,2,1,0:T(8,128)S(1)} %get-tuple-element.22), channel_id=1, source_target_pairs={{0,16},{1,17},{2,18},{3,19},{4,20},{5,21},{6,22},{7,23},{8,24},{9,... | collective-permute-start | bytes 786440 | tf_op jit(solution)/shard_map/ppermute | solution.py:471
  28.4 6.5 %collective-permute-done.5 = f32[2,2,16,1024]{3,2,1,0:T(8,128)S(1)} collective-permute-done((f32[2,2,16,1024]{3,2,1,0:T(8,128)S(1)}, f32[2,2,16,1024]{3,2,1,0:T(8,128)S(1)}, u32[]{:S(2)}, u32[]{:S(2)}) %collective-permute-start.5) | collective-permute-done | bytes 262176 | tf_op jit(solution)/shard_map/ppermute | solution.py:471
  34.9 0.7 %fusion = (f32[2,16,2048]{2,1,0:T(8,128)}, f32[2,16,2048]{2,1,0:T(8,128)}) fusion(f32[2,16,2048]{2,1,0:T(8,128)} %get-tuple-element.23, s32[]{:T(128)S(6)} %select_n.4, f32[2,2,16,1024]{3,2,1,0:T(8,128)S(1)} %collective-permute-done.5, f32[2,16,2048]{2,1,0:T(8,128)} %get-tuple-element.21), kind=kLoop, calls=%fused_computation.1 | loop fusion | bytes 524292 | tf_op jit(solution)/shard_map/dynamic_update_slice | solution.py:527
Async XLA Ops:
  2.0 18.8 %collective-permute-start = (f32[11,8,1152]{2,1,0:T(8,128)S(1)}, f32[11,8,1152]{2,1,0:T(8,128)S(1)}, u32[]{:S(2)}, u32[]{:S(2)}) collective-permute-start(f32[11,8,1152]{2,1,0:T(8,128)S(1)} %get-tuple-element.16), channel_id=1, source_target_pairs={{1,2},{2,1},{3,4},{4,3},{5,6},{6,5},{7,8},{8,7},{9,10},{10,9},{11,... | collective-permute-start | bytes 1216520 | tf_op jit(solution)/shard_map/ppermute | solution.py:471
  2.7 18.1 %collective-permute-start.1 = (f32[11,8,1152]{2,1,0:T(8,128)S(1)}, f32[11,8,1152]{2,1,0:T(8,128)S(1)}, u32[]{:S(2)}, u32[]{:S(2)}) collective-permute-start(f32[11,8,1152]{2,1,0:T(8,128)S(1)} %get-tuple-element.17), channel_id=1, source_target_pairs={{0,1},{1,0},{2,3},{3,2},{4,5},{5,4},{6,7},{7,6},{8,9},{9,8},{10,11... | collective-permute-start | bytes 1216520 | tf_op jit(solution)/shard_map/ppermute | solution.py:471
  7.1 6.2 %copy-start = (f32[2,2,15]{2,1,0:T(2,128)S(1)}, f32[2,2,15]{2,1,0:T(2,128)}, u32[]{:S(2)}) copy-start(f32[2,2,15]{2,1,0:T(2,128)} %refs_0_.3) | copy-start | bytes 724
  7.1 13.7 %collective-permute-start.2 = (f32[8,8,1152]{2,1,0:T(8,128)S(1)}, f32[8,8,1152]{2,1,0:T(8,128)S(1)}, u32[]{:S(2)}, u32[]{:S(2)}) collective-permute-start(f32[8,8,1152]{2,1,0:T(8,128)S(1)} %get-tuple-element.18), channel_id=1, source_target_pairs={{0,16},{1,17},{2,18},{3,19},{4,20},{5,21},{6,22},{7,23},{8,24},{9,... | collective-permute-start | bytes 884744 | tf_op jit(solution)/shard_map/ppermute | solution.py:471
  8.6 6.1 %collective-permute-start.3 = (f32[3,8,1152]{2,1,0:T(8,128)S(1)}, f32[3,8,1152]{2,1,0:T(8,128)S(1)}, u32[]{:S(2)}, u32[]{:S(2)}) collective-permute-start(f32[3,8,1152]{2,1,0:T(8,128)S(1)} %get-tuple-element.19), channel_id=1, source_target_pairs={{1,18},{2,17},{3,20},{4,19},{5,22},{6,21},{7,24},{8,23},{9,26},{10... | collective-permute-start | bytes 331784 | tf_op jit(solution)/shard_map/ppermute | solution.py:471
  9.2 11.6 %collective-permute-start.4 = (f32[3,8,1152]{2,1,0:T(8,128)S(1)}, f32[3,8,1152]{2,1,0:T(8,128)S(1)}, u32[]{:S(2)}, u32[]{:S(2)}) collective-permute-start(f32[3,8,1152]{2,1,0:T(8,128)S(1)} %get-tuple-element.20), channel_id=1, source_target_pairs={{0,17},{1,16},{2,19},{3,18},{4,21},{5,20},{6,23},{7,22},{8,25},{9,... | collective-permute-start | bytes 331784 | tf_op jit(solution)/shard_map/ppermute | solution.py:471
  20.9 0.7 %copy-start.1 = (f32[2]{0:T(128)S(1)}, f32[2]{0:T(128)}, u32[]{:S(2)}) copy-start(f32[2]{0:T(128)} %refs_0_.5) | copy-start | bytes 28
  26.9 8.0 %collective-permute-start.5 = (f32[2,2,16,1024]{3,2,1,0:T(8,128)S(1)}, f32[2,2,16,1024]{3,2,1,0:T(8,128)S(1)}, u32[]{:S(2)}, u32[]{:S(2)}) collective-permute-start(f32[2,2,16,1024]{3,2,1,0:T(8,128)S(1)} %get-tuple-element.22), channel_id=1, source_target_pairs={{0,16},{1,17},{2,18},{3,19},{4,20},{5,21},{6,22},{7,23},{8,24},{9,... | collective-permute-start | bytes 786440 | tf_op jit(solution)/shard_map/ppermute | solution.py:471

commit v3 on v2

--- a/solution.py
+++ b/solution.py
@@ -167,8 +167,10 @@
 HALO_TILES = 4
 LANES = 128
 
-sin_terms = (0.999999999, -0.1666666575, 0.00833331893, -0.0001984042124, 2.753344554e-06, -2.470543221e-08, 1.352854445e-10)
-cos_terms = (0.9999999859, -0.4999998648, 0.0416664545, -0.001388763794, 2.476635379e-05, -2.704470886e-07, 1.712096229e-09)
+OVERLAP = 8
+
+sin_terms = (0.9999999995, -0.1666666515, 0.008333256964, -0.0001982776292, 2.657952479e-06)
+cos_terms = (0.9999999947, -0.4999998344, 0.04166583045, -0.00138740917, 2.372928386e-05)
 
 
 def window_row(tile, sub):
@@ -181,7 +183,7 @@
     return jnp.where(tile < 2, 8 * tile + sub, halo)
 
 
-def band_kernel(plane_rows, taps, bands, back_bands):
+def band_kernel(plane_rows, taps, freqs, bands, back_bands, freq_tiles):
     first_row = lax.axis_index("xy") * ROWS
 
     def fill(ref, adjoint):
@@ -218,11 +220,72 @@
 
     fill(bands, False)
     fill(back_bands, True)
-
-
-def pack_kernel(
-    width, step, surf_in, slow_in, pert_in, cross, chip, bulk, cross_far, chip_far, window, surf, slow, pert, sems
-):
+    for f in range(freq_tiles.shape[0]):
+        freq_tiles[f] = jnp.full((8, LANES), freqs[f], jnp.float32)
+
+
+def pack_rows(ref, values, side):
+    lane = lax.broadcasted_iota(jnp.int32, (8, LANES), 1)
+    overlaps = jnp.zeros((8, LANES), jnp.float32)
+    blocks = (values[0].shape[1] - LANES) // LANES
+    for n, value in enumerate(values):
+        for block in range(blocks):
+            ref[blocks * n + block] = value[:, (block + side) * LANES : (block + side + 1) * LANES]
+        extra = value[:, : LANES] if side else value[:, blocks * LANES :]
+        turn = (OVERLAP * (n + side)) % LANES
+        extra = pltpu.roll(extra, turn, 1) if turn else extra
+        overlaps = jnp.where((lane >= OVERLAP * n) & (lane < OVERLAP * (n + 1)), extra, overlaps)
+    ref[blocks * len(values)] = overlaps
+
+
+def unpack_rows(ref, tiles, n, side):
+    blocks = (ref.shape[0] - 1) // tiles
+    turn = (-OVERLAP * (n + side)) % LANES
+    extra = ref[blocks * tiles]
+    extra = pltpu.roll(extra, turn, 1) if turn else extra
+    parts = [ref[blocks * n + block] for block in range(blocks)]
+    return jnp.concatenate([extra] + parts if side else parts + [extra], axis=1)
+
+
+def edge_levels(levels, slow, pert, down):
+    inner, outer = (1, 0) if down else (0, 1)
+    if levels == 1:
+        return [slow(0, inner), pert(1, inner), pert(0, inner)]
+    row = lax.broadcasted_iota(jnp.int32, slow(0, 0).shape, 0)
+    turned = pltpu.roll(slow(1, outer), 4, 0)
+    if down:
+        extra = jnp.where(row < 2, pltpu.roll(pert(1, inner), 2, 0), turned)
+        last = jnp.where(row < 4, extra, slow(0, outer))
+    else:
+        extra = jnp.where(row >= 6, pltpu.roll(pert(1, inner), 6, 0), turned)
+        last = jnp.where(row < 4, slow(0, outer), extra)
+    return [slow(0, inner), slow(1, inner), last]
+
+
+def edge_surface(surf, down):
+    inner, outer = (1, 0) if down else (0, 1)
+    tiles = [surf(plane, inner) for plane in range(4)]
+    row = lax.broadcasted_iota(jnp.int32, tiles[0].shape, 0)
+    spread = surf(3, outer)
+    for plane in range(3):
+        turn = 6 - 2 * plane
+        free = row < 2 if down else row >= 6
+        tiles.append(jnp.where(free, pltpu.roll(spread, turn, 0), surf(plane, outer)))
+    return tiles
+
+
+def surface_edges(tiles, down):
+    row = lax.broadcasted_iota(jnp.int32, tiles[0].shape, 0)
+    outer = [tiles[4], tiles[5], tiles[6]]
+    first = 2 if down else 0
+    spread = pltpu.roll(tiles[6], 6, 0)
+    spread = jnp.where((row >= first + 2) & (row < first + 4), pltpu.roll(tiles[5], 4, 0), spread)
+    spread = jnp.where((row >= first) & (row < first + 2), pltpu.roll(tiles[4], 2, 0), spread)
+    outer.append(spread)
+    return [(tiles[plane], outer[plane]) for plane in range(4)]
+
+
+def pack_kernel(width, step, surf_in, slow_in, pert_in, cross, bulk, cross_far, window, surf, slow, pert, sems):
     copies = [
         pltpu.make_async_copy(source, target, sems.at[n])
         for n, (source, target) in enumerate(((slow_in, slow), (pert_in, pert), (surf_in, surf)))
@@ -233,116 +296,85 @@
         copy.wait()
     depth = lax.axis_index("depth")
     place = lax.axis_index("xy")
-    near = pl.ds(pl.multiple_of(depth * step, LANES), width)
-    far = pl.ds(pl.multiple_of((1 - depth) * step, LANES), width)
-    row = lax.broadcasted_iota(jnp.int32, (8, width), 0)
-
-    def edge_rows(down, lanes, put):
-        inner, outer = (1, 0) if down else (0, 1)
-
-        def tile(ref, level, index):
-            return ref[level, 8 * index : 8 * index + 8, lanes]
-
-        @pl.when(depth == 0)
+    for own in range(2):
+
+        def reader(ref, side):
+            lanes = slice(side * step, side * step + width)
+            return lambda level, tile: ref[level, 8 * tile : 8 * tile + 8, lanes]
+
+        def surface(plane, tile):
+            return surf[plane // 2, plane % 2, 8 * tile : 8 * tile + 8, own * step : own * step + width]
+
+        @pl.when(depth == own)
         def _():
-            put(0, tile(slow, 0, inner))
-            put(1, tile(slow, 1, inner))
-            turned = pltpu.roll(tile(slow, 1, outer), 4, 0)
-            if down:
-                extra = jnp.where(row < 2, pltpu.roll(tile(pert, 1, inner), 2, 0), turned)
-                put(2, jnp.where(row < 4, extra, tile(slow, 0, outer)))
-            else:
-                extra = jnp.where(row >= 6, pltpu.roll(tile(pert, 1, inner), 6, 0), turned)
-                put(2, jnp.where(row < 4, tile(slow, 0, outer), extra))
-
-        @pl.when(depth == 1)
+            slow_near, pert_near = reader(slow, own), reader(pert, own)
+            slow_far, pert_far = reader(slow, 1 - own), reader(pert, 1 - own)
+            both = [(level, tile) for level in range(2) for tile in range(2)]
+            for n, (level, tile) in enumerate(both):
+                window[8 + n] = slow_near(level, tile)
+                window[12 + n] = pert_near(level, tile)
+            for plane in range(4):
+                for tile in range(2):
+                    window[2 * plane + tile] = surface(plane, tile)
+            pack_rows(bulk, [slow_far(*at) for at in both] + [pert_far(*at) for at in both], 1 - own)
+            for down in (False, True):
+
+                @pl.when((lax.rem(place, 2) == 1) == down)
+                def _():
+                    edges = edge_surface(surface, down) + edge_levels(own, slow_near, pert_near, down)
+                    pack_rows(cross, edges, own)
+                    pack_rows(cross_far, edge_levels(own, slow_far, pert_far, down), 1 - own)
+
+
+def relay_kernel(window, bulk, chip, partner):
+    depth = lax.axis_index("depth")
+    place = lax.axis_index("xy")
+    for own in range(2):
+
+        @pl.when(depth == own)
         def _():
-            put(0, tile(slow, 0, inner))
-            put(1, tile(pert, 1, inner))
-            put(2, tile(pert, 0, inner))
-
-    def into(ref, base):
-        def put(index, value):
-            ref[base + index] = value
-
-        return put
-
-    for f in range(2):
-        for part in range(2):
-            for index in range(2):
-                value = surf[f, part, 8 * index : 8 * index + 8, near]
-                cross[4 * f + 2 * part + index] = value
-                chip[4 * f + 2 * part + index] = value
-                window[4 * f + 2 * part + index] = value
-    for level in range(2):
-        for index in range(2):
-            window[8 + 2 * level + index] = slow[level, 8 * index : 8 * index + 8, near]
-            window[12 + 2 * level + index] = pert[level, 8 * index : 8 * index + 8, near]
-            bulk[2 * level + index] = slow[level, 8 * index : 8 * index + 8, far]
-            bulk[4 + 2 * level + index] = pert[level, 8 * index : 8 * index + 8, far]
-    for parity in range(2):
-
-        @pl.when(lax.rem(place, 2) == parity)
-        def _():
-            edge_rows(parity == 0, near, into(chip, 8))
-            edge_rows(parity == 0, far, into(chip_far, 0))
-            edge_rows(parity == 1, near, into(cross, 8))
-            edge_rows(parity == 1, far, into(cross_far, 0))
-
-
-def phase(angle):
-    square = angle * angle
+            other = [unpack_rows(bulk, 8, n, own) for n in range(8)]
+            for n in range(8):
+                partner[n] = other[n]
+            readers = {
+                own: (lambda level, tile: window[8 + 2 * level + tile], lambda level, tile: window[12 + 2 * level + tile]),
+                1 - own: (lambda level, tile: other[2 * level + tile], lambda level, tile: other[4 + 2 * level + tile]),
+            }
+            for down in (False, True):
+
+                @pl.when((lax.rem(place, 2) == 0) == down)
+                def _():
+                    edges = edge_surface(lambda plane, tile: window[2 * plane + tile], down)
+                    for levels in (own, 1 - own):
+                        edges = edges + edge_levels(levels, *readers[levels], down)
+                    pack_rows(chip, edges, own)
+
+
+def phase(half):
+    square = half * half
     cosine = cos_terms[-1]
     sine = sin_terms[-1]
     for term in cos_terms[-2::-1]:
         cosine = cosine * square + term
     for term in sin_terms[-2::-1]:
         sine = sine * square + term
-    return cosine, sine * angle
+    sine = sine * half
+    twice = sine + sine
+    return 1.0 - twice * sine, twice * cosine
 
 
 def sweep_kernel(
-    width, freqs, bands, back_bands, window, cross, chip, bulk, cross_far, chip_far,
+    width, freq_tiles, bands, back_bands, window, partner, cross, cross_far, chip,
     gradient, image, theirs, slow_win, pert_win, operand, phases, fields, image_win, grad_win,
 ):
     depth = lax.axis_index("depth")
     place = lax.axis_index("xy")
     half = width - LANES
-    upper = lax.broadcasted_iota(jnp.int32, (8, width), 0) < 4
     row = lax.broadcasted_iota(jnp.int32, (8, width), 0)
-    lane = lax.broadcasted_iota(jnp.int32, (16, width), 1)
+    upper = row < 4
+    lane = lax.broadcasted_iota(jnp.int32, (16, LANES), 1)
     even = lax.rem(place, 2) == 0
-
-    def sides(cross_tile, chip_tile):
-        return jnp.where(even, cross_tile, chip_tile), jnp.where(even, chip_tile, cross_tile)
-
-    for own in range(2):
-
-        @pl.when(depth == own)
-        def _():
-            for level in range(2):
-                for index in range(2):
-                    slow_win[2 * own + level, index] = window[8 + 2 * level + index]
-                    pert_win[2 * own + level, index] = window[12 + 2 * level + index]
-                    slow_win[2 * (1 - own) + level, index] = bulk[2 * level + index]
-                    pert_win[2 * (1 - own) + level, index] = bulk[4 + 2 * level + index]
-            first = (cross, chip, 8) if own == 0 else (cross_far, chip_far, 0)
-            second = (cross, chip, 8) if own == 1 else (cross_far, chip_far, 0)
-            above, below = zip(*[sides(first[0][first[2] + t], first[1][first[2] + t]) for t in range(3)])
-            for level in range(2):
-                slow_win[level, 2] = jnp.where(upper, below[level], above[level])
-                slow_win[level, 3] = jnp.where(upper, above[level], below[level])
-            slow_win[0, 4] = jnp.where(upper, below[2], above[2])
-            slow_win[1, 4] = pltpu.roll(jnp.where(upper, above[2], below[2]), 4, 0)
-            pert_win[1, 2] = jnp.where(
-                row < 2, pltpu.roll(below[2], 2, 0), jnp.where(row >= 6, pltpu.roll(above[2], 6, 0), 0.0)
-            )
-            above, below = zip(*[sides(second[0][second[2] + t], second[1][second[2] + t]) for t in range(3)])
-            slow_win[2, 2] = jnp.where(upper, below[0], above[0])
-            slow_win[2, 3] = jnp.where(upper, above[0], below[0])
-            pert_win[3, 2] = jnp.where(upper, below[1], above[1])
-            pert_win[3, 3] = jnp.where(upper, above[1], below[1])
-            pert_win[2, 2] = jnp.where(upper, below[2], above[2])
+    freqs = [jnp.concatenate([freq_tiles[f]] * (width // LANES), axis=1) for f in range(2)]
 
     def store_operand(f, tile, value):
         high = value.astype(jnp.bfloat16)
@@ -363,28 +395,63 @@
             base = 48 * tile
             left = pltpu.roll(product[base : base + 16], 1, 1)
             right = pltpu.roll(product[base + 32 : base + 48], width - 1, 1)
-            left = jnp.where(lane == 0, 0.0, left)
-            right = jnp.where(lane == width - 1, 0.0, right)
+            left = jnp.concatenate([jnp.where(lane == 0, 0.0, left[:, :LANES]), left[:, LANES:]], axis=1)
+            right = jnp.concatenate([right[:, :half], jnp.where(lane == LANES - 1, 0.0, right[:, half:])], axis=1)
             result.append(product[base + 16 : base + 32] + left + right)
         return result
 
-    for f in range(2):
+    def fill(own, below_is_chip):
+        chip_edges = [unpack_rows(chip, 13, n, own) for n in range(13)]
+        cross_edges = [unpack_rows(cross, 10, n, own) for n in range(10)]
+        cross_edges += [unpack_rows(cross_far, 3, n, own) for n in range(3)]
+        above, below = (cross_edges, chip_edges) if below_is_chip else (chip_edges, cross_edges)
+        for level in range(2):
+            for tile in range(2):
+                slow_win[2 * own + level, tile] = window[8 + 2 * level + tile]
+                pert_win[2 * own + level, tile] = window[12 + 2 * level + tile]
+                slow_win[2 * (1 - own) + level, tile] = partner[2 * level + tile]
+                pert_win[2 * (1 - own) + level, tile] = partner[4 + 2 * level + tile]
+        at = (7, 10) if own == 0 else (10, 7)
+        up, down = above[at[0] : at[0] + 3], below[at[0] : at[0] + 3]
+        for level in range(2):
+            slow_win[level, 2] = jnp.where(upper, down[level], up[level])
+            slow_win[level, 3] = jnp.where(upper, up[level], down[level])
+        slow_win[0, 4] = jnp.where(upper, down[2], up[2])
+        slow_win[1, 4] = pltpu.roll(jnp.where(upper, up[2], down[2]), 4, 0)
+        pert_win[1, 2] = jnp.where(
+            row < 2, pltpu.roll(down[2], 2, 0), jnp.where(row >= 6, pltpu.roll(up[2], 6, 0), 0.0)
+        )
+        up, down = above[at[1] : at[1] + 3], below[at[1] : at[1] + 3]
+        slow_win[2, 2] = jnp.where(upper, down[0], up[0])
+        slow_win[2, 3] = jnp.where(upper, up[0], down[0])
+        pert_win[3, 2] = jnp.where(upper, down[1], up[1])
+        pert_win[3, 3] = jnp.where(upper, up[1], down[1])
+        pert_win[2, 2] = jnp.where(upper, down[2], up[2])
+        up, down = surface_edges(above[:7], True), surface_edges(below[:7], False)
         planes = []
-        for part in range(2):
-            at = 4 * f + 2 * part
-            above, below = zip(*[sides(cross[at + t], chip[at + t]) for t in range(2)])
+        for plane in range(4):
+            up_inner, up_outer = up[plane]
+            down_inner, down_outer = down[plane]
             planes.append(
                 [
-                    window[at],
-                    window[at + 1],
-                    jnp.where(upper, below[0], above[1]),
-                    jnp.where(upper, above[1], below[0]),
-                    jnp.where(upper, below[1], above[0]),
-                    jnp.where(upper, above[0], below[1]),
+                    window[2 * plane],
+                    window[2 * plane + 1],
+                    jnp.where(upper, down_inner, up_inner),
+                    jnp.where(upper, up_inner, down_inner),
+                    jnp.where(upper, down_outer, up_outer),
+                    jnp.where(upper, up_outer, down_outer),
                 ]
             )
-        for tile in range(6):
-            store_operand(f, tile, jnp.concatenate([planes[0][tile], planes[1][tile]], axis=0))
+        for f in range(2):
+            for tile in range(6):
+                store_operand(f, tile, jnp.concatenate([planes[2 * f][tile], planes[2 * f + 1][tile]], axis=0))
+
+    for own in range(2):
+        for below_is_chip in (False, True):
+
+            @pl.when((depth == own) & (even == below_is_chip))
+            def _():
+                fill(own, below_is_chip)
 
     def add_image(f, level, tile, re, im):
         part = (re * re + im * im) * 0.5
@@ -399,7 +466,7 @@
         for f in range(2):
             fields_now = stencil(f, bands, tiles[level + 1], tiles[level])
             for tile, value in enumerate(fields_now):
-                cosine, sine = phase(freqs[f] * 0.5 * slow_win[level, tile])
+                cosine, sine = phase(freqs[f] * 0.25 * slow_win[level, tile])
                 v_re, v_im = value[:8], value[8:]
                 re = cosine * v_re - sine * v_im
                 im = cosine * v_im + sine * v_re
@@ -415,7 +482,7 @@
             twice = 2.0 * pert_win[3, tile]
             v_re, v_im = value[:8], value[8:]
             if tile < 2:
-                cosine, sine = phase(freqs[f] * 0.5 * slow_win[3, tile])
+                cosine, sine = phase(freqs[f] * 0.25 * slow_win[3, tile])
                 re = cosine * v_re - sine * v_im
                 im = cosine * v_im + sine * v_re
                 add_image(f, 3, tile, re, im)
@@ -473,39 +540,54 @@
     vmem = pl.BlockSpec(memory_space=pltpu.VMEM)
     smem = pl.BlockSpec(memory_space=pltpu.SMEM)
     tile = lambda n: jax.ShapeDtypeStruct((n, 8, width), f32)
-    cross, chip, bulk, cross_far, chip_far, window = pl.pallas_call(
+    packed = lambda n: jax.ShapeDtypeStruct((n * half // LANES + 1, 8, LANES), f32)
+    params = lambda mib: pltpu.CompilerParams(vmem_limit_bytes=mib * 2**20)
+    cross, bulk, cross_far, window = pl.pallas_call(
         lambda *refs: pack_kernel(width, step, *refs),
-        out_shape=(tile(11), tile(11), tile(8), tile(3), tile(3), tile(16)),
+        out_shape=(packed(10), packed(8), packed(3), tile(16)),
         in_specs=[pl.BlockSpec(memory_space=pltpu.HBM)] * 3,
-        out_specs=(vmem,) * 6,
+        out_specs=(vmem,) * 4,
         scratch_shapes=[
             pltpu.VMEM(surface_data.shape, f32),
             pltpu.VMEM(slowness.shape, f32),
             pltpu.VMEM(perturbation.shape, f32),
             pltpu.SemaphoreType.DMA((3,)),
         ],
-        compiler_params=pltpu.CompilerParams(vmem_limit_bytes=32 * 2**20),
+        compiler_params=params(32),
         name="pack",
     )(*(pltpu.with_memory_space_constraint(x, pltpu.HBM) for x in (surface_data, slowness, perturbation)))
     cross = moved(cross, False, "cross")
     bulk = moved(bulk, True, "same")
     cross_far = moved(cross_far, True, "cross")
-    chip_far = moved(chip_far, True, "chip")
+    bands, back_bands, freq_tiles = pl.pallas_call(
+        lambda *refs: band_kernel(count * ROWS, *refs),
+        out_shape=(
+            jax.ShapeDtypeStruct((2, 240, 288), jnp.bfloat16),
+            jax.ShapeDtypeStruct((2, 144, 192), jnp.bfloat16),
+            jax.ShapeDtypeStruct((2, 8, LANES), f32),
+        ),
+        in_specs=[smem] * 2,
+        out_specs=(vmem,) * 3,
+        compiler_params=params(16),
+        cost_estimate=pl.CostEstimate(flops=10**10, bytes_accessed=10**6, transcendentals=0),
+        name="bands",
+    )(coefficients, frequencies)
+    chip, partner = pl.pallas_call(
+        relay_kernel,
+        out_shape=(packed(13), tile(8)),
+        in_specs=[vmem] * 2,
+        out_specs=(vmem,) * 2,
+        compiler_params=params(32),
+        cost_estimate=pl.CostEstimate(flops=10**10, bytes_accessed=10**6, transcendentals=0),
+        name="relay",
+    )(window, bulk)
     chip = moved(chip, False, "chip")
 
-    bands, back_bands = pl.pallas_call(
-        lambda *refs: band_kernel(count * ROWS, *refs),
-        out_shape=(jax.ShapeDtypeStruct((2, 240, 288), jnp.bfloat16), jax.ShapeDtypeStruct((2, 144, 192), jnp.bfloat16)),
-        in_specs=[smem],
-        out_specs=(vmem,) * 2,
-        compiler_params=pltpu.CompilerParams(vmem_limit_bytes=16 * 2**20),
-        name="bands",
-    )(coefficients)
     own = jax.ShapeDtypeStruct((2, ROWS, columns), f32)
     gradient, image, theirs = pl.pallas_call(
         lambda *refs: sweep_kernel(width, *refs),
         out_shape=(own, own, jax.ShapeDtypeStruct((2, 2, ROWS, half), f32)),
-        in_specs=[smem] + [vmem] * 8,
+        in_specs=[vmem] * 8,
         out_specs=(vmem,) * 3,
         scratch_shapes=[
             pltpu.VMEM((4, 5, 8, width), f32),
@@ -516,10 +598,10 @@
             pltpu.VMEM((4, 2, 8, width), f32),
             pltpu.VMEM((4, 2, 8, width), f32),
         ],
-        compiler_params=pltpu.CompilerParams(vmem_limit_bytes=40 * 2**20),
+        compiler_params=params(40),
         name="sweep",
     )(
-        frequencies, bands, back_bands, window, cross, chip, bulk, cross_far, chip_far,
+        freq_tiles, bands, back_bands, window, partner, cross, cross_far, chip,
     )
     theirs = moved(theirs, True, "same")
     start = (1 - lax.axis_index("depth")) * half

time: 35.8 us -> 29.8 us (0.83)
  the two profiles are of different devices: /device:TPU:0 before, /device:TPU:20 now
where the time goes in v3:
time: 29.8 us; the launch traced here: 29.6 us
  waiting for transfers between devices  12.2 us (41%)
  Pallas kernels  7.75 us (26%)
  starting transfers between devices  7.69 us (26%)
  local copies, waits for them, and re-layouts  1.29 us (4%)
  between operations  0.69 us (2%)
    ppermute x5, waiting for transfers between devices, moved(): return lax.ppermute(value, axes, pairs)  12.2 us
    ppermute x5, starting transfers between devices, moved(): return lax.ppermute(value, axes, pairs)  7.69 us
    pallas_call x1, Pallas kernels, split_columns(): pl.pallas_call(lambda *refs: sweep_kernel(width, *refs), out_shape=(own,...  4.74 us
    pallas_call x1, Pallas kernels, split_columns(): pl.pallas_call(lambda *refs: band_kernel(count * ROWS, *refs), out_shape=...  1.45 us
    pallas_call x1, Pallas kernels, split_columns(): pl.pallas_call(lambda *refs: pack_kernel(width, step, *refs), out_shape=(...  1.39 us
    dynamic_update_slice x1, local copies, waits for them, and re-layouts, split_columns(): image = lax.dynamic_update_slice(image, theirs[1], (0, 0, start))  0.72 us
  transfers between devices with their start and end apart: 5, of which 4 were waited for; matrix products, arithmetic and copies ran while one was open for 0% of the time, Pallas kernels for 5%

profile of v3, /device:TPU:20, one launch (start us, length us, event | category | flops | bytes accessed | tf_op | source)
XLA Modules:
  0.0 29.6 jit_solution(17848407754229942581)
XLA Ops:
  0.6 1.4 %pack.1 = (f32[81,8,128]{2,1,0:T(8,128)S(1)}, f32[65,8,128]{2,1,0:T(8,128)S(1)}, f32[25,8,128]{2,1,0:T(8,128)S(1)}, f32[16,8,1152]{2,1,0:T(8,128)S(1)}) custom-call(f32[2,2,16,2048]{3,2,1,0:T(8,128)} %refs_0_.3, f32[2,16,2048]{2,1,0:T(8,128)} %refs_1_.3, f32[2,16,2048]{2,1,0:T(8,128)} %refs_2_.1), custom_call_target="tpu_custom_call" | custom-call | tf_op jit(solution)/shard_map/pack/pallas_call | solution.py:545
  2.0 1.6 %collective-permute-start = (f32[65,8,128]{2,1,0:T(8,128)S(1)}, f32[65,8,128]{2,1,0:T(8,128)S(1)}, u32[]{:S(2)}, u32[]{:S(2)}) collective-permute-start(f32[65,8,128]{2,1,0:T(8,128)S(1)} %get-tuple-element.18), channel_id=1, source_target_pairs={{0,16},{1,17},{2,18},{3,19},{4,20},{5,21},{6,22},{7,23},{8,24},{9,... | collective-permute-start | bytes 798728 | tf_op jit(solution)/shard_map/ppermute | solution.py:538
  3.6 1.9 %collective-permute-start.1 = (f32[81,8,128]{2,1,0:T(8,128)S(1)}, f32[81,8,128]{2,1,0:T(8,128)S(1)}, u32[]{:S(2)}, u32[]{:S(2)}) collective-permute-start(f32[81,8,128]{2,1,0:T(8,128)S(1)} %get-tuple-element.20), channel_id=1, source_target_pairs={{1,2},{2,1},{3,4},{4,3},{5,6},{6,5},{7,8},{8,7},{9,10},{10,9},{11,... | collective-permute-start | bytes 995336 | tf_op jit(solution)/shard_map/ppermute | solution.py:538
  5.5 3.6 %collective-permute-start.2 = (f32[25,8,128]{2,1,0:T(8,128)S(1)}, f32[25,8,128]{2,1,0:T(8,128)S(1)}, u32[]{:S(2)}, u32[]{:S(2)}) collective-permute-start(f32[25,8,128]{2,1,0:T(8,128)S(1)} %get-tuple-element.21), channel_id=1, source_target_pairs={{1,18},{2,17},{3,20},{4,19},{5,22},{6,21},{7,24},{8,23},{9,26},{10... | collective-permute-start | bytes 307208 | tf_op jit(solution)/shard_map/ppermute | solution.py:538
  9.1 1.1 %collective-permute-done.bulk = f32[65,8,128]{2,1,0:T(8,128)S(1)} collective-permute-done((f32[65,8,128]{2,1,0:T(8,128)S(1)}, f32[65,8,128]{2,1,0:T(8,128)S(1)}, u32[]{:S(2)}, u32[]{:S(2)}) %collective-permute-start) | collective-permute-done | bytes 266272 | tf_op jit(solution)/shard_map/ppermute | solution.py:538
  10.2 0.0 copy-start
  10.2 0.2 relay.1
  10.4 0.0 copy-start.1
  10.4 0.1 collective-permute-start.3
  10.5 0.4 %copy-done = f32[2,2,15]{2,1,0:T(2,128)S(1)} copy-done((f32[2,2,15]{2,1,0:T(2,128)S(1)}, f32[2,2,15]{2,1,0:T(2,128)}, u32[]{:S(2)}) %copy-start) | copy-done | bytes 264
  10.9 0.2 copy-done.1
  11.1 1.5 %bands.1 = (bf16[2,240,288]{2,1,0:T(8,128)(2,1)S(1)}, bf16[2,144,192]{2,1,0:T(8,128)(2,1)S(1)}, f32[2,8,128]{2,1,0:T(8,128)S(1)}) custom-call(f32[2,2,15]{2,1,0:T(2,128)S(1)} %copy-done, f32[2]{0:T(128)S(1)} %copy-done.1), custom_call_target="tpu_custom_call" | custom-call | flops 10000000000 | bytes 1000000 | tf_op jit(solution)/shard_map/bands/pallas_call | solution.py:562
  12.5 1.0 %collective-permute-done.2.refs_6_ = f32[25,8,128]{2,1,0:T(8,128)S(1)} collective-permute-done((f32[25,8,128]{2,1,0:T(8,128)S(1)}, f32[25,8,128]{2,1,0:T(8,128)S(1)}, u32[]{:S(2)}, u32[]{:S(2)}) %collective-permute-start.2) | collective-permute-done | bytes 102432 | tf_op jit(solution)/shard_map/ppermute | solution.py:538
  13.5 4.2 %collective-permute-done.1.refs_5_ = f32[81,8,128]{2,1,0:T(8,128)S(1)} collective-permute-done((f32[81,8,128]{2,1,0:T(8,128)S(1)}, f32[81,8,128]{2,1,0:T(8,128)S(1)}, u32[]{:S(2)}, u32[]{:S(2)}) %collective-permute-start.1) | collective-permute-done | bytes 331808 | tf_op jit(solution)/shard_map/ppermute | solution.py:538
  17.8 0.0 collective-permute-done.3.refs_7_
  17.8 4.7 %sweep.1 = (f32[2,16,2048]{2,1,0:T(8,128)}, f32[2,16,2048]{2,1,0:T(8,128)}, f32[2,2,16,1024]{3,2,1,0:T(8,128)S(1)}) custom-call(f32[2,8,128]{2,1,0:T(8,128)S(1)} %get-tuple-element.14.refs_0_, bf16[2,240,288]{2,1,0:T(8,128)(2,1)S(1)} %get-tuple-element.15.refs_1_, bf16[2,144,192]{2,1,0:T(8,128)(2,1)S(1)} %get-tuple-element.16.refs_2_, ...), custom_call_target="tpu_custom_call" | custom-call | tf_op jit(solution)/shard_map/sweep/pallas_call | solution.py:587
  22.5 0.5 %collective-permute-start.4 = (f32[2,2,16,1024]{3,2,1,0:T(8,128)S(1)}, f32[2,2,16,1024]{3,2,1,0:T(8,128)S(1)}, u32[]{:S(2)}, u32[]{:S(2)}) collective-permute-start(f32[2,2,16,1024]{3,2,1,0:T(8,128)S(1)} %get-tuple-element.24), channel_id=1, source_target_pairs={{0,16},{1,17},{2,18},{3,19},{4,20},{5,21},{6,22},{7,23},{8,24},{9,... | collective-permute-start | bytes 786440 | tf_op jit(solution)/shard_map/ppermute | solution.py:538
  23.0 5.8 %collective-permute-done.4 = f32[2,2,16,1024]{3,2,1,0:T(8,128)S(1)} collective-permute-done((f32[2,2,16,1024]{3,2,1,0:T(8,128)S(1)}, f32[2,2,16,1024]{3,2,1,0:T(8,128)S(1)}, u32[]{:S(2)}, u32[]{:S(2)}) %collective-permute-start.4) | collective-permute-done | bytes 262176 | tf_op jit(solution)/shard_map/ppermute | solution.py:538
  28.9 0.7 %fusion = (f32[2,16,2048]{2,1,0:T(8,128)}, f32[2,16,2048]{2,1,0:T(8,128)}) fusion(f32[2,16,2048]{2,1,0:T(8,128)} %get-tuple-element.25, s32[]{:T(128)S(6)} %select_n.4, f32[2,2,16,1024]{3,2,1,0:T(8,128)S(1)} %collective-permute-done.4, f32[2,16,2048]{2,1,0:T(8,128)} %get-tuple-element.23), kind=kLoop, calls=%fused_computation.1 | loop fusion | bytes 524292 | tf_op jit(solution)/shard_map/dynamic_update_slice | solution.py:609
Async XLA Ops:
  2.0 8.2 %collective-permute-start = (f32[65,8,128]{2,1,0:T(8,128)S(1)}, f32[65,8,128]{2,1,0:T(8,128)S(1)}, u32[]{:S(2)}, u32[]{:S(2)}) collective-permute-start(f32[65,8,128]{2,1,0:T(8,128)S(1)} %get-tuple-element.18), channel_id=1, source_target_pairs={{0,16},{1,17},{2,18},{3,19},{4,20},{5,21},{6,22},{7,23},{8,24},{9,... | collective-permute-start | bytes 798728 | tf_op jit(solution)/shard_map/ppermute | solution.py:538
  3.6 14.2 %collective-permute-start.1 = (f32[81,8,128]{2,1,0:T(8,128)S(1)}, f32[81,8,128]{2,1,0:T(8,128)S(1)}, u32[]{:S(2)}, u32[]{:S(2)}) collective-permute-start(f32[81,8,128]{2,1,0:T(8,128)S(1)} %get-tuple-element.20), channel_id=1, source_target_pairs={{1,2},{2,1},{3,4},{4,3},{5,6},{6,5},{7,8},{8,7},{9,10},{10,9},{11,... | collective-permute-start | bytes 995336 | tf_op jit(solution)/shard_map/ppermute | solution.py:538
  5.5 8.0 %collective-permute-start.2 = (f32[25,8,128]{2,1,0:T(8,128)S(1)}, f32[25,8,128]{2,1,0:T(8,128)S(1)}, u32[]{:S(2)}, u32[]{:S(2)}) collective-permute-start(f32[25,8,128]{2,1,0:T(8,128)S(1)} %get-tuple-element.21), channel_id=1, source_target_pairs={{1,18},{2,17},{3,20},{4,19},{5,22},{6,21},{7,24},{8,23},{9,26},{10... | collective-permute-start | bytes 307208 | tf_op jit(solution)/shard_map/ppermute | solution.py:538
  10.2 0.7 %copy-start = (f32[2,2,15]{2,1,0:T(2,128)S(1)}, f32[2,2,15]{2,1,0:T(2,128)}, u32[]{:S(2)}) copy-start(f32[2,2,15]{2,1,0:T(2,128)} %refs_0_.2) | copy-start | bytes 724
  10.4 0.7 %copy-start.1 = (f32[2]{0:T(128)S(1)}, f32[2]{0:T(128)}, u32[]{:S(2)}) copy-start(f32[2]{0:T(128)} %refs_1_.2) | copy-start | bytes 28
  10.4 7.3 %collective-permute-start.3 = (f32[105,8,128]{2,1,0:T(8,128)S(1)}, f32[105,8,128]{2,1,0:T(8,128)S(1)}, u32[]{:S(2)}, u32[]{:S(2)}) collective-permute-start(f32[105,8,128]{2,1,0:T(8,128)S(1)} %get-tuple-element.22), channel_id=1, source_target_pairs={{0,1},{1,0},{2,3},{3,2},{4,5},{5,4},{6,7},{7,6},{8,9},{9,8},{10,11... | collective-permute-start | bytes 1290248 | tf_op jit(solution)/shard_map/ppermute | solution.py:538
  22.5 6.4 %collective-permute-start.4 = (f32[2,2,16,1024]{3,2,1,0:T(8,128)S(1)}, f32[2,2,16,1024]{3,2,1,0:T(8,128)S(1)}, u32[]{:S(2)}, u32[]{:S(2)}) collective-permute-start(f32[2,2,16,1024]{3,2,1,0:T(8,128)S(1)} %get-tuple-element.24), channel_id=1, source_target_pairs={{0,16},{1,17},{2,18},{3,19},{4,20},{5,21},{6,22},{7,23},{8,24},{9,... | collective-permute-start | bytes 786440 | tf_op jit(solution)/shard_map/ppermute | solution.py:538

commit v4 on v3

--- a/solution.py
+++ b/solution.py
@@ -262,30 +262,12 @@
     return [slow(0, inner), slow(1, inner), last]
 
 
-def edge_surface(surf, down):
-    inner, outer = (1, 0) if down else (0, 1)
-    tiles = [surf(plane, inner) for plane in range(4)]
-    row = lax.broadcasted_iota(jnp.int32, tiles[0].shape, 0)
-    spread = surf(3, outer)
-    for plane in range(3):
-        turn = 6 - 2 * plane
-        free = row < 2 if down else row >= 6
-        tiles.append(jnp.where(free, pltpu.roll(spread, turn, 0), surf(plane, outer)))
-    return tiles
-
-
-def surface_edges(tiles, down):
-    row = lax.broadcasted_iota(jnp.int32, tiles[0].shape, 0)
-    outer = [tiles[4], tiles[5], tiles[6]]
-    first = 2 if down else 0
-    spread = pltpu.roll(tiles[6], 6, 0)
-    spread = jnp.where((row >= first + 2) & (row < first + 4), pltpu.roll(tiles[5], 4, 0), spread)
-    spread = jnp.where((row >= first) & (row < first + 2), pltpu.roll(tiles[4], 2, 0), spread)
-    outer.append(spread)
-    return [(tiles[plane], outer[plane]) for plane in range(4)]
-
-
-def pack_kernel(width, step, surf_in, slow_in, pert_in, cross, bulk, cross_far, window, surf, slow, pert, sems):
+def edge_surface(surf, f, down):
+    order = (1, 0) if down else (0, 1)
+    return [surf(2 * f + part, tile) for tile in order for part in range(2)]
+
+
+def pack_kernel(width, step, surf_in, slow_in, pert_in, cross, cross_next, bulk, cross_far, window, surf, slow, pert, sems):
     copies = [
         pltpu.make_async_copy(source, target, sems.at[n])
         for n, (source, target) in enumerate(((slow_in, slow), (pert_in, pert), (surf_in, surf)))
@@ -321,8 +303,9 @@
 
                 @pl.when((lax.rem(place, 2) == 1) == down)
                 def _():
-                    edges = edge_surface(surface, down) + edge_levels(own, slow_near, pert_near, down)
+                    edges = edge_levels(own, slow_near, pert_near, down) + edge_surface(surface, 0, down)
                     pack_rows(cross, edges, own)
+                    pack_rows(cross_next, edge_surface(surface, 1, down), own)
                     pack_rows(cross_far, edge_levels(own, slow_far, pert_far, down), 1 - own)
 
 
@@ -344,9 +327,11 @@
 
                 @pl.when((lax.rem(place, 2) == 0) == down)
                 def _():
-                    edges = edge_surface(lambda plane, tile: window[2 * plane + tile], down)
+                    edges = []
                     for levels in (own, 1 - own):
                         edges = edges + edge_levels(levels, *readers[levels], down)
+                    for f in range(2):
+                        edges = edges + edge_surface(lambda plane, tile: window[2 * plane + tile], f, down)
                     pack_rows(chip, edges, own)
 
 
@@ -363,88 +348,87 @@
     return 1.0 - twice * sine, twice * cosine
 
 
-def sweep_kernel(
-    width, freq_tiles, bands, back_bands, window, partner, cross, cross_far, chip,
-    gradient, image, theirs, slow_win, pert_win, operand, phases, fields, image_win, grad_win,
-):
+def own_phases_kernel(freq_tiles, window, partner, phases):
     depth = lax.axis_index("depth")
-    place = lax.axis_index("xy")
+    for level in range(4):
+        for tile in range(2):
+            own, other = window[8 + 2 * (level % 2) + tile], partner[2 * (level % 2) + tile]
+            slow = jnp.where(depth == level // 2, own, other)
+            for f in range(2):
+                cosine, sine = phase(over_columns(freq_tiles[f], slow) * 0.25 * slow)
+                phases[f, level, tile, :8] = cosine
+                phases[f, level, tile, 8:] = sine
+
+
+def over_columns(tile, like):
+    return jnp.concatenate([tile] * (like.shape[1] // LANES), axis=1)
+
+
+def split_store(operand, tile, value):
+    high = value.astype(jnp.bfloat16)
+    low = (value - high.astype(jnp.float32)).astype(jnp.bfloat16)
+    base = 48 * tile
+    operand[base : base + 16] = high
+    operand[base + 16 : base + 32] = high
+    operand[base + 32 : base + 48] = low
+
+
+def stencil(matrix, operand, out_tiles, in_tiles):
+    product = jnp.dot(
+        matrix[: 48 * out_tiles, : 48 * in_tiles],
+        operand[: 48 * in_tiles],
+        preferred_element_type=jnp.float32,
+    )
+    width = product.shape[1]
     half = width - LANES
-    row = lax.broadcasted_iota(jnp.int32, (8, width), 0)
+    lane = lax.broadcasted_iota(jnp.int32, (16, LANES), 1)
+    result = []
+    for tile in range(out_tiles):
+        base = 48 * tile
+        left = pltpu.roll(product[base : base + 16], 1, 1)
+        right = pltpu.roll(product[base + 32 : base + 48], width - 1, 1)
+        left = jnp.concatenate([jnp.where(lane == 0, 0.0, left[:, :LANES]), left[:, LANES:]], axis=1)
+        right = jnp.concatenate([right[:, :half], jnp.where(lane == LANES - 1, 0.0, right[:, half:])], axis=1)
+        result.append(product[base + 16 : base + 32] + left + right)
+    return result
+
+
+def gradient_part(freq_tile, w_re, w_im, u_re, u_im):
+    return (0.25 * over_columns(freq_tile, w_re)) * (w_im * u_re - w_re * u_im)
+
+
+def fill_levels(window, partner, cross, cross_far, chip, slow_halo, pert_win):
+    row = lax.broadcasted_iota(jnp.int32, slow_halo.shape[2:], 0)
     upper = row < 4
-    lane = lax.broadcasted_iota(jnp.int32, (16, LANES), 1)
-    even = lax.rem(place, 2) == 0
-    freqs = [jnp.concatenate([freq_tiles[f]] * (width // LANES), axis=1) for f in range(2)]
-
-    def store_operand(f, tile, value):
-        high = value.astype(jnp.bfloat16)
-        low = (value - high.astype(jnp.float32)).astype(jnp.bfloat16)
-        base = 48 * tile
-        operand[f, base : base + 16] = high
-        operand[f, base + 16 : base + 32] = high
-        operand[f, base + 32 : base + 48] = low
-
-    def stencil(f, matrix, out_tiles, in_tiles):
-        product = jnp.dot(
-            matrix[f, : 48 * out_tiles, : 48 * in_tiles],
-            operand[f, : 48 * in_tiles],
-            preferred_element_type=jnp.float32,
-        )
-        result = []
-        for tile in range(out_tiles):
-            base = 48 * tile
-            left = pltpu.roll(product[base : base + 16], 1, 1)
-            right = pltpu.roll(product[base + 32 : base + 48], width - 1, 1)
-            left = jnp.concatenate([jnp.where(lane == 0, 0.0, left[:, :LANES]), left[:, LANES:]], axis=1)
-            right = jnp.concatenate([right[:, :half], jnp.where(lane == LANES - 1, 0.0, right[:, half:])], axis=1)
-            result.append(product[base + 16 : base + 32] + left + right)
-        return result
+    depth = lax.axis_index("depth")
+    even = lax.rem(lax.axis_index("xy"), 2) == 0
 
     def fill(own, below_is_chip):
-        chip_edges = [unpack_rows(chip, 13, n, own) for n in range(13)]
-        cross_edges = [unpack_rows(cross, 10, n, own) for n in range(10)]
-        cross_edges += [unpack_rows(cross_far, 3, n, own) for n in range(3)]
+        near = [unpack_rows(cross, 7, n, own) for n in range(3)]
+        far = [unpack_rows(cross_far, 3, n, own) for n in range(3)]
+        cross_edges = (near, far) if own == 0 else (far, near)
+        on_chip = [unpack_rows(chip, 14, n, own) for n in range(6)]
+        chip_edges = (on_chip[:3], on_chip[3:]) if own == 0 else (on_chip[3:], on_chip[:3])
         above, below = (cross_edges, chip_edges) if below_is_chip else (chip_edges, cross_edges)
         for level in range(2):
             for tile in range(2):
-                slow_win[2 * own + level, tile] = window[8 + 2 * level + tile]
                 pert_win[2 * own + level, tile] = window[12 + 2 * level + tile]
-                slow_win[2 * (1 - own) + level, tile] = partner[2 * level + tile]
                 pert_win[2 * (1 - own) + level, tile] = partner[4 + 2 * level + tile]
-        at = (7, 10) if own == 0 else (10, 7)
-        up, down = above[at[0] : at[0] + 3], below[at[0] : at[0] + 3]
+        up, down = above[0], below[0]
         for level in range(2):
-            slow_win[level, 2] = jnp.where(upper, down[level], up[level])
-            slow_win[level, 3] = jnp.where(upper, up[level], down[level])
-        slow_win[0, 4] = jnp.where(upper, down[2], up[2])
-        slow_win[1, 4] = pltpu.roll(jnp.where(upper, up[2], down[2]), 4, 0)
+            slow_halo[level, 0] = jnp.where(upper, down[level], up[level])
+            slow_halo[level, 1] = jnp.where(upper, up[level], down[level])
+        slow_halo[0, 2] = jnp.where(upper, down[2], up[2])
+        slow_halo[1, 2] = pltpu.roll(jnp.where(upper, up[2], down[2]), 4, 0)
         pert_win[1, 2] = jnp.where(
             row < 2, pltpu.roll(down[2], 2, 0), jnp.where(row >= 6, pltpu.roll(up[2], 6, 0), 0.0)
         )
-        up, down = above[at[1] : at[1] + 3], below[at[1] : at[1] + 3]
-        slow_win[2, 2] = jnp.where(upper, down[0], up[0])
-        slow_win[2, 3] = jnp.where(upper, up[0], down[0])
+        up, down = above[1], below[1]
+        slow_halo[2, 0] = jnp.where(upper, down[0], up[0])
+        slow_halo[2, 1] = jnp.where(upper, up[0], down[0])
         pert_win[3, 2] = jnp.where(upper, down[1], up[1])
         pert_win[3, 3] = jnp.where(upper, up[1], down[1])
         pert_win[2, 2] = jnp.where(upper, down[2], up[2])
-        up, down = surface_edges(above[:7], True), surface_edges(below[:7], False)
-        planes = []
-        for plane in range(4):
-            up_inner, up_outer = up[plane]
-            down_inner, down_outer = down[plane]
-            planes.append(
-                [
-                    window[2 * plane],
-                    window[2 * plane + 1],
-                    jnp.where(upper, down_inner, up_inner),
-                    jnp.where(upper, up_inner, down_inner),
-                    jnp.where(upper, down_outer, up_outer),
-                    jnp.where(upper, up_outer, down_outer),
-                ]
-            )
-        for f in range(2):
-            for tile in range(6):
-                store_operand(f, tile, jnp.concatenate([planes[2 * f][tile], planes[2 * f + 1][tile]], axis=0))
 
     for own in range(2):
         for below_is_chip in (False, True):
@@ -453,59 +437,121 @@
             def _():
                 fill(own, below_is_chip)
 
-    def add_image(f, level, tile, re, im):
-        part = (re * re + im * im) * 0.5
-        image_win[level, tile] = part if f == 0 else image_win[level, tile] + part
-
-    def add_gradient(f, level, tile, w_re, w_im, u_re, u_im):
-        part = (0.25 * freqs[f]) * (w_im * u_re - w_re * u_im)
-        grad_win[level, tile] = part if f == 0 else grad_win[level, tile] + part
+
+def fill_surface(f, window, cross, cross_tiles, cross_first, chip, operand):
+    upper = lax.broadcasted_iota(jnp.int32, window.shape[1:], 0) < 4
+    depth = lax.axis_index("depth")
+    even = lax.rem(lax.axis_index("xy"), 2) == 0
+
+    def fill(own, below_is_chip):
+        cross_edges = [unpack_rows(cross, cross_tiles, cross_first + n, own) for n in range(4)]
+        chip_edges = [unpack_rows(chip, 14, 6 + 4 * f + n, own) for n in range(4)]
+        up, down = (cross_edges, chip_edges) if below_is_chip else (chip_edges, cross_edges)
+        planes = []
+        for part in range(2):
+            at = 4 * f + 2 * part
+            planes.append(
+                [
+                    window[at],
+                    window[at + 1],
+                    jnp.where(upper, down[part], up[part]),
+                    jnp.where(upper, up[part], down[part]),
+                    jnp.where(upper, down[2 + part], up[2 + part]),
+                    jnp.where(upper, up[2 + part], down[2 + part]),
+                ]
+            )
+        for tile in range(6):
+            split_store(operand, tile, jnp.concatenate([planes[0][tile], planes[1][tile]], axis=0))
+
+    for own in range(2):
+        for below_is_chip in (False, True):
+
+            @pl.when((depth == own) & (even == below_is_chip))
+            def _():
+                fill(own, below_is_chip)
+
+
+def sweep(f, freq_tiles, bands, back_bands, own_phases, slow_halo, pert_win, operand, halo_phases, fields, add_image, add_gradient):
+    def advance(level, tile, value):
+        if tile < 2:
+            cosine, sine = own_phases[f, level, tile, :8], own_phases[f, level, tile, 8:]
+        else:
+            slow = slow_halo[level, tile - 2]
+            cosine, sine = phase(over_columns(freq_tiles[f], slow) * 0.25 * slow)
+            if tile == 2 and level > 0:
+                halo_phases[level - 1, :8] = cosine
+                halo_phases[level - 1, 8:] = sine
+        v_re, v_im = value[:8], value[8:]
+        re = cosine * v_re - sine * v_im
+        im = cosine * v_im + sine * v_re
+        if tile < 2:
+            add_image(level, tile, (re * re + im * im) * 0.5)
+        return re, im
 
     tiles = (6, 5, 5, 4)
     for level in range(3):
-        for f in range(2):
-            fields_now = stencil(f, bands, tiles[level + 1], tiles[level])
-            for tile, value in enumerate(fields_now):
-                cosine, sine = phase(freqs[f] * 0.25 * slow_win[level, tile])
-                v_re, v_im = value[:8], value[8:]
-                re = cosine * v_re - sine * v_im
-                im = cosine * v_im + sine * v_re
-                both = jnp.concatenate([re, im], axis=0)
-                store_operand(f, tile, both)
-                if tile < 3:
-                    fields[f, level, tile] = both
-                    phases[f, level, tile] = jnp.concatenate([cosine, sine], axis=0)
-                if tile < 2:
-                    add_image(f, level, tile, re, im)
-    for f in range(2):
-        for tile, value in enumerate(stencil(f, bands, 4, 4)):
-            twice = 2.0 * pert_win[3, tile]
-            v_re, v_im = value[:8], value[8:]
-            if tile < 2:
-                cosine, sine = phase(freqs[f] * 0.25 * slow_win[3, tile])
-                re = cosine * v_re - sine * v_im
-                im = cosine * v_im + sine * v_re
-                add_image(f, 3, tile, re, im)
-                add_gradient(f, 3, tile, twice * re, twice * im, re, im)
-            store_operand(f, tile, jnp.concatenate([twice * v_re, twice * v_im], axis=0))
+        for tile, value in enumerate(stencil(bands.at[f], operand, tiles[level + 1], tiles[level])):
+            both = jnp.concatenate(advance(level, tile, value), axis=0)
+            split_store(operand, tile, both)
+            if tile < 3:
+                fields[level, tile] = both
+    for tile, value in enumerate(stencil(bands.at[f], operand, 4, 4)):
+        twice = 2.0 * pert_win[3, tile]
+        if tile < 2:
+            re, im = advance(3, tile, value)
+            add_gradient(3, tile, gradient_part(freq_tiles[f], twice * re, twice * im, re, im))
+        split_store(operand, tile, jnp.concatenate([twice * value[:8], twice * value[8:]], axis=0))
     tiles = (2, 3, 3, 4)
     for level in (2, 1, 0):
-        for f in range(2):
-            for tile, value in enumerate(stencil(f, back_bands, tiles[level], tiles[level + 1])):
-                twice = 2.0 * pert_win[level, tile]
-                u_re, u_im = fields[f, level, tile, :8], fields[f, level, tile, 8:]
-                w_re = value[:8] + twice * u_re
-                w_im = value[8:] + twice * u_im
+        for tile, value in enumerate(stencil(back_bands.at[f], operand, tiles[level], tiles[level + 1])):
+            twice = 2.0 * pert_win[level, tile]
+            u_re, u_im = fields[level, tile, :8], fields[level, tile, 8:]
+            w_re = value[:8] + twice * u_re
+            w_im = value[8:] + twice * u_im
+            if tile < 2:
+                add_gradient(level, tile, gradient_part(freq_tiles[f], w_re, w_im, u_re, u_im))
+            if level > 0:
                 if tile < 2:
-                    add_gradient(f, level, tile, w_re, w_im, u_re, u_im)
-                if level > 0:
-                    cosine, sine = phases[f, level, tile, :8], phases[f, level, tile, 8:]
-                    back = [cosine * w_re + sine * w_im, cosine * w_im - sine * w_re]
-                    store_operand(f, tile, jnp.concatenate(back, axis=0))
-
+                    cosine, sine = own_phases[f, level, tile, :8], own_phases[f, level, tile, 8:]
+                else:
+                    cosine, sine = halo_phases[level - 1, :8], halo_phases[level - 1, 8:]
+                back = [cosine * w_re + sine * w_im, cosine * w_im - sine * w_re]
+                split_store(operand, tile, jnp.concatenate(back, axis=0))
+
+
+def first_sweep_kernel(
+    freq_tiles, bands, back_bands, own_phases, window, partner, cross, cross_far, chip,
+    slow_halo, pert_win, image_sum, grad_sum, operand, halo_phases, fields,
+):
+    fill_levels(window, partner, cross, cross_far, chip, slow_halo, pert_win)
+    fill_surface(0, window, cross, 7, 3, chip, operand)
+
+    def add_image(level, tile, value):
+        image_sum[level, tile] = value
+
+    def add_gradient(level, tile, value):
+        grad_sum[level, tile] = value
+
+    sweep(0, freq_tiles, bands, back_bands, own_phases, slow_halo, pert_win, operand, halo_phases, fields, add_image, add_gradient)
+
+
+def second_sweep_kernel(
+    freq_tiles, bands, back_bands, own_phases, window, cross_next, chip, slow_halo, pert_win, image_sum, grad_sum,
+    gradient, image, theirs, operand, halo_phases, fields, image_win, grad_win,
+):
+    fill_surface(1, window, cross_next, 4, 0, chip, operand)
+
+    def add_image(level, tile, value):
+        image_win[level, tile] = value + image_sum[level, tile]
+
+    def add_gradient(level, tile, value):
+        grad_win[level, tile] = value + grad_sum[level, tile]
+
+    sweep(1, freq_tiles, bands, back_bands, own_phases, slow_halo, pert_win, operand, halo_phases, fields, add_image, add_gradient)
+    half = theirs.shape[3]
     for own in range(2):
 
-        @pl.when(depth == own)
+        @pl.when(lax.axis_index("depth") == own)
         def _():
             inner = slice(own * LANES, own * LANES + half)
             outer = slice(own * half, own * half + half)
@@ -542,11 +588,11 @@
     tile = lambda n: jax.ShapeDtypeStruct((n, 8, width), f32)
     packed = lambda n: jax.ShapeDtypeStruct((n * half // LANES + 1, 8, LANES), f32)
     params = lambda mib: pltpu.CompilerParams(vmem_limit_bytes=mib * 2**20)
-    cross, bulk, cross_far, window = pl.pallas_call(
+    cross, cross_next, bulk, cross_far, window = pl.pallas_call(
         lambda *refs: pack_kernel(width, step, *refs),
-        out_shape=(packed(10), packed(8), packed(3), tile(16)),
+        out_shape=(packed(7), packed(4), packed(8), packed(3), tile(16)),
         in_specs=[pl.BlockSpec(memory_space=pltpu.HBM)] * 3,
-        out_specs=(vmem,) * 4,
+        out_specs=(vmem,) * 5,
         scratch_shapes=[
             pltpu.VMEM(surface_data.shape, f32),
             pltpu.VMEM(slowness.shape, f32),
@@ -559,6 +605,7 @@
     cross = moved(cross, False, "cross")
     bulk = moved(bulk, True, "same")
     cross_far = moved(cross_far, True, "cross")
+    cross_next = moved(cross_next, False, "cross")
     bands, back_bands, freq_tiles = pl.pallas_call(
         lambda *refs: band_kernel(count * ROWS, *refs),
         out_shape=(
@@ -574,7 +621,7 @@
     )(coefficients, frequencies)
     chip, partner = pl.pallas_call(
         relay_kernel,
-        out_shape=(packed(13), tile(8)),
+        out_shape=(packed(14), tile(8)),
         in_specs=[vmem] * 2,
         out_specs=(vmem,) * 2,
         compiler_params=params(32),
@@ -583,25 +630,46 @@
     )(window, bulk)
     chip = moved(chip, False, "chip")
 
+    own_phases = pl.pallas_call(
+        own_phases_kernel,
+        out_shape=jax.ShapeDtypeStruct((2, 4, 2, 16, width), f32),
+        in_specs=[vmem] * 3,
+        out_specs=vmem,
+        compiler_params=params(16),
+        name="own_phases",
+    )(freq_tiles, window, partner)
+
     own = jax.ShapeDtypeStruct((2, ROWS, columns), f32)
+    sums = jax.ShapeDtypeStruct((4, 2, 8, width), f32)
+    scratch = [
+        pltpu.VMEM((288, width), jnp.bfloat16),
+        pltpu.VMEM((2, 16, width), f32),
+        pltpu.VMEM((3, 3, 16, width), f32),
+    ]
+    slow_halo, pert_win, image_sum, grad_sum = pl.pallas_call(
+        first_sweep_kernel,
+        out_shape=(
+            jax.ShapeDtypeStruct((3, 3, 8, width), f32),
+            jax.ShapeDtypeStruct((4, 4, 8, width), f32),
+            sums,
+            sums,
+        ),
+        in_specs=[vmem] * 9,
+        out_specs=(vmem,) * 4,
+        scratch_shapes=scratch,
+        compiler_params=params(32),
+        name="first_sweep",
+    )(freq_tiles, bands, back_bands, own_phases, window, partner, cross, cross_far, chip)
     gradient, image, theirs = pl.pallas_call(
-        lambda *refs: sweep_kernel(width, *refs),
+        second_sweep_kernel,
         out_shape=(own, own, jax.ShapeDtypeStruct((2, 2, ROWS, half), f32)),
-        in_specs=[vmem] * 8,
+        in_specs=[vmem] * 11,
         out_specs=(vmem,) * 3,
-        scratch_shapes=[
-            pltpu.VMEM((4, 5, 8, width), f32),
-            pltpu.VMEM((4, 4, 8, width), f32),
-            pltpu.VMEM((2, 288, width), jnp.bfloat16),
-            pltpu.VMEM((2, 3, 3, 16, width), f32),
-            pltpu.VMEM((2, 3, 3, 16, width), f32),
-            pltpu.VMEM((4, 2, 8, width), f32),
-            pltpu.VMEM((4, 2, 8, width), f32),
-        ],
-        compiler_params=params(40),
-        name="sweep",
+        scratch_shapes=scratch + [pltpu.VMEM((4, 2, 8, width), f32)] * 2,
+        compiler_params=params(32),
+        name="second_sweep",
     )(
-        freq_tiles, bands, back_bands, window, partner, cross, cross_far, chip,
+        freq_tiles, bands, back_bands, own_phases, window, cross_next, chip, slow_halo, pert_win, image_sum, grad_sum
     )
     theirs = moved(theirs, True, "same")
     start = (1 - lax.axis_index("depth")) * half

time: 29.8 us -> 32.8 us (1.10)
  the two profiles are of different devices: /device:TPU:20 before, /device:TPU:0 now
where the time goes in v4:
time: 32.8 us; the launch traced here: 32.6 us
  waiting for transfers between devices  11.5 us (35%)
  Pallas kernels  10.3 us (31%)
  starting transfers between devices  9.28 us (28%)
  between operations  0.73 us (2%)
  local copies, waits for them, and re-layouts  0.72 us (2%)
    ppermute x6, waiting for transfers between devices, moved(): return lax.ppermute(value, axes, pairs)  11.5 us
    ppermute x6, starting transfers between devices, moved(): return lax.ppermute(value, axes, pairs)  9.28 us
    pallas_call x1, Pallas kernels, split_columns(): pl.pallas_call(second_sweep_kernel, out_shape=(own, own, jax.ShapeDtypeSt...  3.82 us
    pallas_call x1, Pallas kernels, split_columns(): pl.pallas_call(first_sweep_kernel, out_shape=(jax.ShapeDtypeStruct((3, 3,...  3.05 us
    pallas_call x1, Pallas kernels, split_columns(): pl.pallas_call(lambda *refs: band_kernel(count * ROWS, *refs), out_shape=...  1.45 us
    pallas_call x1, Pallas kernels, split_columns(): pl.pallas_call(lambda *refs: pack_kernel(width, step, *refs), out_shape=(...  1.38 us
    dynamic_update_slice x1, local copies, waits for them, and re-layouts, split_columns(): image = lax.dynamic_update_slice(image, theirs[1], (0, 0, start))  0.72 us
  transfers between devices with their start and end apart: 6, of which 2 were waited for; matrix products, arithmetic and copies ran while one was open for 0% of the time, Pallas kernels for 16%

profile of v4, /device:TPU:0, one launch (start us, length us, event | category | flops | bytes accessed | tf_op | source)
XLA Modules:
  0.0 32.6 jit_solution(17022049019531505040)
XLA Ops:
  0.6 1.4 %pack.1 = (f32[57,8,128]{2,1,0:T(8,128)S(1)}, f32[33,8,128]{2,1,0:T(8,128)S(1)}, f32[65,8,128]{2,1,0:T(8,128)S(1)}, f32[25,8,128]{2,1,0:T(8,128)S(1)}, f32[16,8,1152]{2,1,0:T(8,128)S(1)}) custom-call(f32[2,2,16,2048]{3,2,1,0:T(8,128)} %refs_0_.3, f32[2,16,2048]{2,1,0:T(8,128)} %refs_1_.3, f32[2,16,2048]{2,1,0:T(8,128)} %refs_2_.1), custom_call_target="tpu_custom_call" | custom-call | tf_op jit(solution)/shard_map/pack/pallas_call | solution.py:591
  2.0 3.0 %collective-permute-start = (f32[65,8,128]{2,1,0:T(8,128)S(1)}, f32[65,8,128]{2,1,0:T(8,128)S(1)}, u32[]{:S(2)}, u32[]{:S(2)}) collective-permute-start(f32[65,8,128]{2,1,0:T(8,128)S(1)} %get-tuple-element.23), channel_id=1, source_target_pairs={{0,16},{1,17},{2,18},{3,19},{4,20},{5,21},{6,22},{7,23},{8,24},{9,... | collective-permute-start | bytes 798728 | tf_op jit(solution)/shard_map/ppermute | solution.py:584
  5.0 0.7 %collective-permute-start.3 = (f32[57,8,128]{2,1,0:T(8,128)S(1)}, f32[57,8,128]{2,1,0:T(8,128)S(1)}, u32[]{:S(2)}, u32[]{:S(2)}) collective-permute-start(f32[57,8,128]{2,1,0:T(8,128)S(1)} %get-tuple-element.27), channel_id=1, source_target_pairs={{1,2},{2,1},{3,4},{4,3},{5,6},{6,5},{7,8},{8,7},{9,10},{10,9},{11,... | collective-permute-start | bytes 700424 | tf_op jit(solution)/shard_map/ppermute | solution.py:584
  5.7 0.7 %collective-permute-start.4 = (f32[25,8,128]{2,1,0:T(8,128)S(1)}, f32[25,8,128]{2,1,0:T(8,128)S(1)}, u32[]{:S(2)}, u32[]{:S(2)}) collective-permute-start(f32[25,8,128]{2,1,0:T(8,128)S(1)} %get-tuple-element.28), channel_id=1, source_target_pairs={{1,18},{2,17},{3,20},{4,19},{5,22},{6,21},{7,24},{8,23},{9,26},{10... | collective-permute-start | bytes 307208 | tf_op jit(solution)/shard_map/ppermute | solution.py:584
  6.4 0.7 %collective-permute-start.1 = (f32[33,8,128]{2,1,0:T(8,128)S(1)}, f32[33,8,128]{2,1,0:T(8,128)S(1)}, u32[]{:S(2)}, u32[]{:S(2)}) collective-permute-start(f32[33,8,128]{2,1,0:T(8,128)S(1)} %get-tuple-element.25), channel_id=1, source_target_pairs={{1,2},{2,1},{3,4},{4,3},{5,6},{6,5},{7,8},{8,7},{9,10},{10,9},{11,... | collective-permute-start | bytes 405512 | tf_op jit(solution)/shard_map/ppermute | solution.py:584
  7.0 4.4 %collective-permute-done.bulk = f32[65,8,128]{2,1,0:T(8,128)S(1)} collective-permute-done((f32[65,8,128]{2,1,0:T(8,128)S(1)}, f32[65,8,128]{2,1,0:T(8,128)S(1)}, u32[]{:S(2)}, u32[]{:S(2)}) %collective-permute-start) | collective-permute-done | bytes 266272 | tf_op jit(solution)/shard_map/ppermute | solution.py:584
  11.4 0.0 copy-start
  11.4 0.0 copy-start.1
  11.4 0.2 relay.1
  11.6 2.8 %collective-permute-start.2 = (f32[113,8,128]{2,1,0:T(8,128)S(1)}, f32[113,8,128]{2,1,0:T(8,128)S(1)}, u32[]{:S(2)}, u32[]{:S(2)}) collective-permute-start(f32[113,8,128]{2,1,0:T(8,128)S(1)} %get-tuple-element.26), channel_id=1, source_target_pairs={{0,1},{1,0},{2,3},{3,2},{4,5},{5,4},{6,7},{7,6},{8,9},{9,8},{10,11... | collective-permute-start | bytes 1388552 | tf_op jit(solution)/shard_map/ppermute | solution.py:584
  14.4 0.0 copy-done
  14.4 0.0 copy-done.1
  14.4 1.5 %bands.1 = (bf16[2,240,288]{2,1,0:T(8,128)(2,1)S(1)}, bf16[2,144,192]{2,1,0:T(8,128)(2,1)S(1)}, f32[2,8,128]{2,1,0:T(8,128)S(1)}) custom-call(f32[2,2,15]{2,1,0:T(2,128)S(1)} %copy-done, f32[2]{0:T(128)S(1)} %copy-done.1), custom_call_target="tpu_custom_call" | custom-call | flops 10000000000 | bytes 1000000 | tf_op jit(solution)/shard_map/bands/pallas_call | solution.py:609
  15.9 0.5 %own_phases.1 = f32[2,4,2,16,1152]{4,3,2,1,0:T(8,128)S(1)} custom-call(f32[2,8,128]{2,1,0:T(8,128)S(1)} %get-tuple-element.19.freq_tiles, f32[16,8,1152]{2,1,0:T(8,128)S(1)} %get-tuple-element.22.window, f32[8,8,1152]{2,1,0:T(8,128)S(1)} %get-tuple-element.24.partner), custom_call_target="tpu_custom_call" | custom-call | tf_op jit(solution)/shard_map/own_phases/pallas_call | solution.py:633
  16.3 0.0 collective-permute-done.4.cross_far
  16.3 0.0 collective-permute-done.3.cross
  16.4 0.0 collective-permute-done.2.chip
  16.4 3.0 %first_sweep.1 = (f32[3,3,8,1152]{3,2,1,0:T(8,128)S(1)}, f32[4,4,8,1152]{3,2,1,0:T(8,128)S(1)}, f32[4,2,8,1152]{3,2,1,0:T(8,128)S(1)}, f32[4,2,8,1152]{3,2,1,0:T(8,128)S(1)}) custom-call(f32[2,8,128]{2,1,0:T(8,128)S(1)} %get-tuple-element.19.freq_tiles, bf16[2,240,288]{2,1,0:T(8,128)(2,1)S(1)} %get-tuple-element.20.bands, ...), custom_call_target="tpu_custom_call" | custom-call | tf_op jit(solution)/shard_map/first_sweep/pallas_call | solution.py:649
  19.4 0.0 collective-permute-done.1.cross_next
  19.4 3.8 %second_sweep.1 = (f32[2,16,2048]{2,1,0:T(8,128)}, f32[2,16,2048]{2,1,0:T(8,128)}, f32[2,2,16,1024]{3,2,1,0:T(8,128)S(1)}) custom-call(f32[2,8,128]{2,1,0:T(8,128)S(1)} %get-tuple-element.19.freq_tiles, bf16[2,240,288]{2,1,0:T(8,128)(2,1)S(1)} %get-tuple-element.20.bands, bf16[2,144,192]{2,1,0:T(8,128)(2,1)S(1)} %get-tuple-element.21.back_bands, ...), custom_call_target="tpu_custom_call" | custom-call | tf_op jit(solution)/shard_map/second_sweep/pallas_call | solution.py:663
  23.3 1.5 %collective-permute-start.5 = (f32[2,2,16,1024]{3,2,1,0:T(8,128)S(1)}, f32[2,2,16,1024]{3,2,1,0:T(8,128)S(1)}, u32[]{:S(2)}, u32[]{:S(2)}) collective-permute-start(f32[2,2,16,1024]{3,2,1,0:T(8,128)S(1)} %get-tuple-element.34), channel_id=1, source_target_pairs={{0,16},{1,17},{2,18},{3,19},{4,20},{5,21},{6,22},{7,23},{8,24},{9,... | collective-permute-start | bytes 786440 | tf_op jit(solution)/shard_map/ppermute | solution.py:584
  24.8 7.1 %collective-permute-done.5 = f32[2,2,16,1024]{3,2,1,0:T(8,128)S(1)} collective-permute-done((f32[2,2,16,1024]{3,2,1,0:T(8,128)S(1)}, f32[2,2,16,1024]{3,2,1,0:T(8,128)S(1)}, u32[]{:S(2)}, u32[]{:S(2)}) %collective-permute-start.5) | collective-permute-done | bytes 262176 | tf_op jit(solution)/shard_map/ppermute | solution.py:584
  31.9 0.7 %fusion = (f32[2,16,2048]{2,1,0:T(8,128)}, f32[2,16,2048]{2,1,0:T(8,128)}) fusion(f32[2,16,2048]{2,1,0:T(8,128)} %get-tuple-element.35, s32[]{:T(128)S(6)} %select_n.4, f32[2,2,16,1024]{3,2,1,0:T(8,128)S(1)} %collective-permute-done.5, f32[2,16,2048]{2,1,0:T(8,128)} %get-tuple-element.33), kind=kLoop, calls=%fused_computation.1 | loop fusion | bytes 524292 | tf_op jit(solution)/shard_map/dynamic_update_slice | solution.py:677
Async XLA Ops:
  2.0 9.4 %collective-permute-start = (f32[65,8,128]{2,1,0:T(8,128)S(1)}, f32[65,8,128]{2,1,0:T(8,128)S(1)}, u32[]{:S(2)}, u32[]{:S(2)}) collective-permute-start(f32[65,8,128]{2,1,0:T(8,128)S(1)} %get-tuple-element.23), channel_id=1, source_target_pairs={{0,16},{1,17},{2,18},{3,19},{4,20},{5,21},{6,22},{7,23},{8,24},{9,... | collective-permute-start | bytes 798728 | tf_op jit(solution)/shard_map/ppermute | solution.py:584
  5.0 11.3 %collective-permute-start.3 = (f32[57,8,128]{2,1,0:T(8,128)S(1)}, f32[57,8,128]{2,1,0:T(8,128)S(1)}, u32[]{:S(2)}, u32[]{:S(2)}) collective-permute-start(f32[57,8,128]{2,1,0:T(8,128)S(1)} %get-tuple-element.27), channel_id=1, source_target_pairs={{1,2},{2,1},{3,4},{4,3},{5,6},{6,5},{7,8},{8,7},{9,10},{10,9},{11,... | collective-permute-start | bytes 700424 | tf_op jit(solution)/shard_map/ppermute | solution.py:584
  5.7 10.7 %collective-permute-start.4 = (f32[25,8,128]{2,1,0:T(8,128)S(1)}, f32[25,8,128]{2,1,0:T(8,128)S(1)}, u32[]{:S(2)}, u32[]{:S(2)}) collective-permute-start(f32[25,8,128]{2,1,0:T(8,128)S(1)} %get-tuple-element.28), channel_id=1, source_target_pairs={{1,18},{2,17},{3,20},{4,19},{5,22},{6,21},{7,24},{8,23},{9,26},{10... | collective-permute-start | bytes 307208 | tf_op jit(solution)/shard_map/ppermute | solution.py:584
  6.4 13.1 %collective-permute-start.1 = (f32[33,8,128]{2,1,0:T(8,128)S(1)}, f32[33,8,128]{2,1,0:T(8,128)S(1)}, u32[]{:S(2)}, u32[]{:S(2)}) collective-permute-start(f32[33,8,128]{2,1,0:T(8,128)S(1)} %get-tuple-element.25), channel_id=1, source_target_pairs={{1,2},{2,1},{3,4},{4,3},{5,6},{6,5},{7,8},{8,7},{9,10},{10,9},{11,... | collective-permute-start | bytes 405512 | tf_op jit(solution)/shard_map/ppermute | solution.py:584
  11.4 3.0 %copy-start = (f32[2,2,15]{2,1,0:T(2,128)S(1)}, f32[2,2,15]{2,1,0:T(2,128)}, u32[]{:S(2)}) copy-start(f32[2,2,15]{2,1,0:T(2,128)} %refs_0_.2) | copy-start | bytes 724
  11.4 3.0 %copy-start.1 = (f32[2]{0:T(128)S(1)}, f32[2]{0:T(128)}, u32[]{:S(2)}) copy-start(f32[2]{0:T(128)} %refs_1_.2) | copy-start | bytes 28
  11.6 4.8 %collective-permute-start.2 = (f32[113,8,128]{2,1,0:T(8,128)S(1)}, f32[113,8,128]{2,1,0:T(8,128)S(1)}, u32[]{:S(2)}, u32[]{:S(2)}) collective-permute-start(f32[113,8,128]{2,1,0:T(8,128)S(1)} %get-tuple-element.26), channel_id=1, source_target_pairs={{0,1},{1,0},{2,3},{3,2},{4,5},{5,4},{6,7},{7,6},{8,9},{9,8},{10,11... | collective-permute-start | bytes 1388552 | tf_op jit(solution)/shard_map/ppermute | solution.py:584
  23.3 8.6 %collective-permute-start.5 = (f32[2,2,16,1024]{3,2,1,0:T(8,128)S(1)}, f32[2,2,16,1024]{3,2,1,0:T(8,128)S(1)}, u32[]{:S(2)}, u32[]{:S(2)}) collective-permute-start(f32[2,2,16,1024]{3,2,1,0:T(8,128)S(1)} %get-tuple-element.34), channel_id=1, source_target_pairs={{0,16},{1,17},{2,18},{3,19},{4,20},{5,21},{6,22},{7,23},{8,24},{9,... | collective-permute-start | bytes 786440 | tf_op jit(solution)/shard_map/ppermute | solution.py:584

commit v5 on v3

--- a/solution.py
+++ b/solution.py
@@ -333,7 +333,7 @@
 
         @pl.when(depth == own)
         def _():
-            other = [unpack_rows(bulk, 8, n, own) for n in range(8)]
+            other = [unpack_rows(bulk.at[1 - own], 8, n, own) for n in range(8)]
             for n in range(8):
                 partner[n] = other[n]
             readers = {
@@ -363,9 +363,25 @@
     return 1.0 - twice * sine, twice * cosine
 
 
+def own_phases_kernel(freq_tiles, window, partner, phases):
+    depth = lax.axis_index("depth")
+    for level in range(4):
+        for tile in range(2):
+            own, other = window[8 + 2 * (level % 2) + tile], partner[2 * (level % 2) + tile]
+            slow = jnp.where(depth == level // 2, own, other)
+            for f in range(2):
+                cosine, sine = phase(over_columns(freq_tiles[f], slow) * 0.25 * slow)
+                phases[f, level, tile, :8] = cosine
+                phases[f, level, tile, 8:] = sine
+
+
+def over_columns(tile, like):
+    return jnp.concatenate([tile] * (like.shape[1] // LANES), axis=1)
+
+
 def sweep_kernel(
-    width, freq_tiles, bands, back_bands, window, partner, cross, cross_far, chip,
-    gradient, image, theirs, slow_win, pert_win, operand, phases, fields, image_win, grad_win,
+    width, freq_tiles, bands, back_bands, own_phases, window, partner, cross, cross_far, chip,
+    gradient, image, theirs, slow_win, pert_win, operand, halo_phases, fields, image_win, grad_win,
 ):
     depth = lax.axis_index("depth")
     place = lax.axis_index("xy")
@@ -407,23 +423,21 @@
         above, below = (cross_edges, chip_edges) if below_is_chip else (chip_edges, cross_edges)
         for level in range(2):
             for tile in range(2):
-                slow_win[2 * own + level, tile] = window[8 + 2 * level + tile]
                 pert_win[2 * own + level, tile] = window[12 + 2 * level + tile]
-                slow_win[2 * (1 - own) + level, tile] = partner[2 * level + tile]
                 pert_win[2 * (1 - own) + level, tile] = partner[4 + 2 * level + tile]
         at = (7, 10) if own == 0 else (10, 7)
         up, down = above[at[0] : at[0] + 3], below[at[0] : at[0] + 3]
         for level in range(2):
-            slow_win[level, 2] = jnp.where(upper, down[level], up[level])
-            slow_win[level, 3] = jnp.where(upper, up[level], down[level])
-        slow_win[0, 4] = jnp.where(upper, down[2], up[2])
-        slow_win[1, 4] = pltpu.roll(jnp.where(upper, up[2], down[2]), 4, 0)
+            slow_win[level, 0] = jnp.where(upper, down[level], up[level])
+            slow_win[level, 1] = jnp.where(upper, up[level], down[level])
+        slow_win[0, 2] = jnp.where(upper, down[2], up[2])
+        slow_win[1, 2] = pltpu.roll(jnp.where(upper, up[2], down[2]), 4, 0)
         pert_win[1, 2] = jnp.where(
             row < 2, pltpu.roll(down[2], 2, 0), jnp.where(row >= 6, pltpu.roll(up[2], 6, 0), 0.0)
         )
         up, down = above[at[1] : at[1] + 3], below[at[1] : at[1] + 3]
-        slow_win[2, 2] = jnp.where(upper, down[0], up[0])
-        slow_win[2, 3] = jnp.where(upper, up[0], down[0])
+        slow_win[2, 0] = jnp.where(upper, down[0], up[0])
+        slow_win[2, 1] = jnp.where(upper, up[0], down[0])
         pert_win[3, 2] = jnp.where(upper, down[1], up[1])
         pert_win[3, 3] = jnp.where(upper, up[1], down[1])
         pert_win[2, 2] = jnp.where(upper, down[2], up[2])
@@ -461,12 +475,21 @@
         part = (0.25 * freqs[f]) * (w_im * u_re - w_re * u_im)
         grad_win[level, tile] = part if f == 0 else grad_win[level, tile] + part
 
+    def phases_of(f, level, tile):
+        if tile < 2:
+            return own_phases[f, level, tile, :8], own_phases[f, level, tile, 8:]
+        cosine, sine = phase(freqs[f] * 0.25 * slow_win[level, tile - 2])
+        if tile == 2 and level > 0:
+            halo_phases[f, level - 1, :8] = cosine
+            halo_phases[f, level - 1, 8:] = sine
+        return cosine, sine
+
     tiles = (6, 5, 5, 4)
     for level in range(3):
         for f in range(2):
             fields_now = stencil(f, bands, tiles[level + 1], tiles[level])
             for tile, value in enumerate(fields_now):
-                cosine, sine = phase(freqs[f] * 0.25 * slow_win[level, tile])
+                cosine, sine = phases_of(f, level, tile)
                 v_re, v_im = value[:8], value[8:]
                 re = cosine * v_re - sine * v_im
                 im = cosine * v_im + sine * v_re
@@ -474,7 +497,6 @@
                 store_operand(f, tile, both)
                 if tile < 3:
                     fields[f, level, tile] = both
-                    phases[f, level, tile] = jnp.concatenate([cosine, sine], axis=0)
                 if tile < 2:
                     add_image(f, level, tile, re, im)
     for f in range(2):
@@ -482,7 +504,7 @@
             twice = 2.0 * pert_win[3, tile]
             v_re, v_im = value[:8], value[8:]
             if tile < 2:
-                cosine, sine = phase(freqs[f] * 0.25 * slow_win[3, tile])
+                cosine, sine = phases_of(f, 3, tile)
                 re = cosine * v_re - sine * v_im
                 im = cosine * v_im + sine * v_re
                 add_image(f, 3, tile, re, im)
@@ -499,7 +521,10 @@
                 if tile < 2:
                     add_gradient(f, level, tile, w_re, w_im, u_re, u_im)
                 if level > 0:
-                    cosine, sine = phases[f, level, tile, :8], phases[f, level, tile, 8:]
+                    if tile < 2:
+                        cosine, sine = phases_of(f, level, tile)
+                    else:
+                        cosine, sine = halo_phases[f, level - 1, :8], halo_phases[f, level - 1, 8:]
                     back = [cosine * w_re + sine * w_im, cosine * w_im - sine * w_re]
                     store_operand(f, tile, jnp.concatenate(back, axis=0))
 
@@ -557,7 +582,7 @@
         name="pack",
     )(*(pltpu.with_memory_space_constraint(x, pltpu.HBM) for x in (surface_data, slowness, perturbation)))
     cross = moved(cross, False, "cross")
-    bulk = moved(bulk, True, "same")
+    bulk = lax.all_gather(bulk, "depth")
     cross_far = moved(cross_far, True, "cross")
     bands, back_bands, freq_tiles = pl.pallas_call(
         lambda *refs: band_kernel(count * ROWS, *refs),
@@ -583,17 +608,26 @@
     )(window, bulk)
     chip = moved(chip, False, "chip")
 
+    own_phases = pl.pallas_call(
+        own_phases_kernel,
+        out_shape=jax.ShapeDtypeStruct((2, 4, 2, 16, width), f32),
+        in_specs=[vmem] * 3,
+        out_specs=vmem,
+        compiler_params=params(16),
+        name="own_phases",
+    )(freq_tiles, window, partner)
+
     own = jax.ShapeDtypeStruct((2, ROWS, columns), f32)
     gradient, image, theirs = pl.pallas_call(
         lambda *refs: sweep_kernel(width, *refs),
         out_shape=(own, own, jax.ShapeDtypeStruct((2, 2, ROWS, half), f32)),
-        in_specs=[vmem] * 8,
+        in_specs=[vmem] * 9,
         out_specs=(vmem,) * 3,
         scratch_shapes=[
-            pltpu.VMEM((4, 5, 8, width), f32),
+            pltpu.VMEM((3, 3, 8, width), f32),
             pltpu.VMEM((4, 4, 8, width), f32),
             pltpu.VMEM((2, 288, width), jnp.bfloat16),
-            pltpu.VMEM((2, 3, 3, 16, width), f32),
+            pltpu.VMEM((2, 2, 16, width), f32),
             pltpu.VMEM((2, 3, 3, 16, width), f32),
             pltpu.VMEM((4, 2, 8, width), f32),
             pltpu.VMEM((4, 2, 8, width), f32),
@@ -601,7 +635,7 @@
         compiler_params=params(40),
         name="sweep",
     )(
-        freq_tiles, bands, back_bands, window, partner, cross, cross_far, chip,
+        freq_tiles, bands, back_bands, own_phases, window, partner, cross, cross_far, chip,
     )
     theirs = moved(theirs, True, "same")
     start = (1 - lax.axis_index("depth")) * half

time: 29.8 us -> 37.5 us (1.26)
  blocking collectives: 0 us -> 8.82 us
  waiting for transfers between devices: 12.2 us -> 11.1 us
  local copies, waits for them, and re-layouts: 1.29 us -> 0.72 us
    all_gather x0 -> x1, blocking collectives: none -> 8.82 us  [split_columns(): bulk = lax.all_gather(bulk, 'depth')]
    ppermute x5 -> x4, waiting for transfers between devices: 12.2 us -> 11.1 us  [moved(): return lax.ppermute(value, axes, pairs)]
    unnamed x4, local copies, waits for them, and re-layouts: 0.57 us -> 0.01 us
    pallas_call x0 -> x1, Pallas kernels: none -> 0.47 us  [split_columns(): pl.pallas_call(own_phases_kernel, out_shape=jax.ShapeDtypeStruct((2, 4, 2...]
    ppermute x5 -> x4, starting transfers between devices: 7.69 us -> 8 us  [moved(): return lax.ppermute(value, axes, pairs)]
  transfers between devices with their start and end apart: 5 -> 4, of which waited for: 4 -> 3; matrix products, arithmetic and copies ran while one was open for 0% -> 0% of each run, Pallas kernels for 5% -> 5%
where the time goes in v5:
time: 37.5 us; the launch traced here: 37.2 us
  waiting for transfers between devices  11.1 us (30%)
  blocking collectives  8.82 us (24%)
  starting transfers between devices  8 us (21%)
  Pallas kernels  7.9 us (21%)
  local copies, waits for them, and re-layouts  0.72 us (2%)
  between operations  0.7 us (2%)
    ppermute x4, waiting for transfers between devices, moved(): return lax.ppermute(value, axes, pairs)  11.1 us
    all_gather x1, blocking collectives, split_columns(): bulk = lax.all_gather(bulk, 'depth')  8.82 us
    ppermute x4, starting transfers between devices, moved(): return lax.ppermute(value, axes, pairs)  8 us
    pallas_call x1, Pallas kernels, split_columns(): pl.pallas_call(lambda *refs: sweep_kernel(width, *refs), out_shape=(own,...  4.42 us
    pallas_call x1, Pallas kernels, split_columns(): pl.pallas_call(lambda *refs: band_kernel(count * ROWS, *refs), out_shape=...  1.45 us
    pallas_call x1, Pallas kernels, split_columns(): pl.pallas_call(lambda *refs: pack_kernel(width, step, *refs), out_shape=(...  1.39 us
  transfers between devices with their start and end apart: 4, of which 3 were waited for; matrix products, arithmetic and copies ran while one was open for 0% of the time, Pallas kernels for 5%

profile of v5, /device:TPU:20, one launch (start us, length us, event | category | flops | bytes accessed | tf_op | source)
XLA Modules:
  0.0 37.2 jit_solution(11896692487440625248)
XLA Ops:
  0.6 1.4 %pack.1 = (f32[81,8,128]{2,1,0:T(8,128)S(1)}, f32[65,8,128]{2,1,0:T(8,128)S(1)}, f32[25,8,128]{2,1,0:T(8,128)S(1)}, f32[16,8,1152]{2,1,0:T(8,128)S(1)}) custom-call(f32[2,2,16,2048]{3,2,1,0:T(8,128)} %refs_0_.3, f32[2,16,2048]{2,1,0:T(8,128)} %refs_1_.3, f32[2,16,2048]{2,1,0:T(8,128)} %refs_2_.1), custom_call_target="tpu_custom_call" | custom-call | tf_op jit(solution)/shard_map/pack/pallas_call | solution.py:570
  2.0 8.8 %all-gather = f32[130,8,128]{2,1,0:T(8,128)S(1)} all-gather(f32[65,8,128]{2,1,0:T(8,128)S(1)} %get-tuple-element.18), channel_id=2, replica_groups=mesh['depth'=2,'xy'=16] {'depth'}, dimensions={0}, use_global_device_ids=true | all-gather | bytes 798720 | tf_op jit(solution)/shard_map/all_gather | solution.py:585
  10.8 0.0 copy-start
  10.8 0.0 copy-start.1
  10.8 0.2 relay.1
  11.0 0.1 collective-permute-start.2
  11.1 2.5 %collective-permute-start = (f32[81,8,128]{2,1,0:T(8,128)S(1)}, f32[81,8,128]{2,1,0:T(8,128)S(1)}, u32[]{:S(2)}, u32[]{:S(2)}) collective-permute-start(f32[81,8,128]{2,1,0:T(8,128)S(1)} %get-tuple-element.20), channel_id=1, source_target_pairs={{1,2},{2,1},{3,4},{4,3},{5,6},{6,5},{7,8},{8,7},{9,10},{10,9},{11,... | collective-permute-start | bytes 995336 | tf_op jit(solution)/shard_map/ppermute | solution.py:563
  13.6 4.0 %collective-permute-start.1 = (f32[25,8,128]{2,1,0:T(8,128)S(1)}, f32[25,8,128]{2,1,0:T(8,128)S(1)}, u32[]{:S(2)}, u32[]{:S(2)}) collective-permute-start(f32[25,8,128]{2,1,0:T(8,128)S(1)} %get-tuple-element.21), channel_id=1, source_target_pairs={{1,18},{2,17},{3,20},{4,19},{5,22},{6,21},{7,24},{8,23},{9,26},{10... | collective-permute-start | bytes 307208 | tf_op jit(solution)/shard_map/ppermute | solution.py:563
  17.6 0.0 copy-done
  17.6 0.0 copy-done.1
  17.6 1.5 %bands.1 = (bf16[2,240,288]{2,1,0:T(8,128)(2,1)S(1)}, bf16[2,144,192]{2,1,0:T(8,128)(2,1)S(1)}, f32[2,8,128]{2,1,0:T(8,128)S(1)}) custom-call(f32[2,2,15]{2,1,0:T(2,128)S(1)} %copy-done, f32[2]{0:T(128)S(1)} %copy-done.1), custom_call_target="tpu_custom_call" | custom-call | flops 10000000000 | bytes 1000000 | tf_op jit(solution)/shard_map/bands/pallas_call | solution.py:587
  19.1 0.5 %own_phases.1.refs_3_ = f32[2,4,2,16,1152]{4,3,2,1,0:T(8,128)S(1)} custom-call(f32[2,8,128]{2,1,0:T(8,128)S(1)} %get-tuple-element.14.freq_tiles.refs_0_, f32[16,8,1152]{2,1,0:T(8,128)S(1)} %get-tuple-element.17.window.refs_4_, f32[8,8,1152]{2,1,0:T(8,128)S(1)} %get-tuple-element.19.partner.refs_5_), custom_call_target="tpu_custom_call" | custom-call | tf_op jit(solution)/shard_map/own_phases/pallas_call | solution.py:611
  19.6 2.1 %collective-permute-done.1.refs_7_ = f32[25,8,128]{2,1,0:T(8,128)S(1)} collective-permute-done((f32[25,8,128]{2,1,0:T(8,128)S(1)}, f32[25,8,128]{2,1,0:T(8,128)S(1)}, u32[]{:S(2)}, u32[]{:S(2)}) %collective-permute-start.1) | collective-permute-done | bytes 102432 | tf_op jit(solution)/shard_map/ppermute | solution.py:563
  21.6 3.6 %collective-permute-done.refs_6_ = f32[81,8,128]{2,1,0:T(8,128)S(1)} collective-permute-done((f32[81,8,128]{2,1,0:T(8,128)S(1)}, f32[81,8,128]{2,1,0:T(8,128)S(1)}, u32[]{:S(2)}, u32[]{:S(2)}) %collective-permute-start) | collective-permute-done | bytes 331808 | tf_op jit(solution)/shard_map/ppermute | solution.py:563
  25.3 0.0 collective-permute-done.2.refs_8_
  25.3 4.4 %sweep.1 = (f32[2,16,2048]{2,1,0:T(8,128)}, f32[2,16,2048]{2,1,0:T(8,128)}, f32[2,2,16,1024]{3,2,1,0:T(8,128)S(1)}) custom-call(f32[2,8,128]{2,1,0:T(8,128)S(1)} %get-tuple-element.14.freq_tiles.refs_0_, bf16[2,240,288]{2,1,0:T(8,128)(2,1)S(1)} %get-tuple-element.15.refs_1_, bf16[2,144,192]{2,1,0:T(8,128)(2,1)S(1)} %get-tuple-element.16.refs_2_, ...), custom_call_target="tpu_custom_call" | custom-call | tf_op jit(solution)/shard_map/sweep/pallas_call | solution.py:621
  29.7 1.5 %collective-permute-start.3 = (f32[2,2,16,1024]{3,2,1,0:T(8,128)S(1)}, f32[2,2,16,1024]{3,2,1,0:T(8,128)S(1)}, u32[]{:S(2)}, u32[]{:S(2)}) collective-permute-start(f32[2,2,16,1024]{3,2,1,0:T(8,128)S(1)} %get-tuple-element.24), channel_id=1, source_target_pairs={{0,16},{1,17},{2,18},{3,19},{4,20},{5,21},{6,22},{7,23},{8,24},{9,... | collective-permute-start | bytes 786440 | tf_op jit(solution)/shard_map/ppermute | solution.py:563
  31.2 5.3 %collective-permute-done.3 = f32[2,2,16,1024]{3,2,1,0:T(8,128)S(1)} collective-permute-done((f32[2,2,16,1024]{3,2,1,0:T(8,128)S(1)}, f32[2,2,16,1024]{3,2,1,0:T(8,128)S(1)}, u32[]{:S(2)}, u32[]{:S(2)}) %collective-permute-start.3) | collective-permute-done | bytes 262176 | tf_op jit(solution)/shard_map/ppermute | solution.py:563
  36.5 0.7 %fusion = (f32[2,16,2048]{2,1,0:T(8,128)}, f32[2,16,2048]{2,1,0:T(8,128)}) fusion(f32[2,16,2048]{2,1,0:T(8,128)} %get-tuple-element.25, s32[]{:T(128)S(6)} %select_n.4, f32[2,2,16,1024]{3,2,1,0:T(8,128)S(1)} %collective-permute-done.3, f32[2,16,2048]{2,1,0:T(8,128)} %get-tuple-element.23), kind=kLoop, calls=%fused_computation.1 | loop fusion | bytes 524292 | tf_op jit(solution)/shard_map/dynamic_update_slice | solution.py:643
Async XLA Ops:
  10.8 6.8 %copy-start = (f32[2,2,15]{2,1,0:T(2,128)S(1)}, f32[2,2,15]{2,1,0:T(2,128)}, u32[]{:S(2)}) copy-start(f32[2,2,15]{2,1,0:T(2,128)} %refs_0_.2) | copy-start | bytes 724
  10.8 6.8 %copy-start.1 = (f32[2]{0:T(128)S(1)}, f32[2]{0:T(128)}, u32[]{:S(2)}) copy-start(f32[2]{0:T(128)} %refs_1_.2) | copy-start | bytes 28
  11.0 14.3 %collective-permute-start.2 = (f32[105,8,128]{2,1,0:T(8,128)S(1)}, f32[105,8,128]{2,1,0:T(8,128)S(1)}, u32[]{:S(2)}, u32[]{:S(2)}) collective-permute-start(f32[105,8,128]{2,1,0:T(8,128)S(1)} %get-tuple-element.22), channel_id=1, source_target_pairs={{0,1},{1,0},{2,3},{3,2},{4,5},{5,4},{6,7},{7,6},{8,9},{9,8},{10,11... | collective-permute-start | bytes 1290248 | tf_op jit(solution)/shard_map/ppermute | solution.py:563
  11.1 14.2 %collective-permute-start = (f32[81,8,128]{2,1,0:T(8,128)S(1)}, f32[81,8,128]{2,1,0:T(8,128)S(1)}, u32[]{:S(2)}, u32[]{:S(2)}) collective-permute-start(f32[81,8,128]{2,1,0:T(8,128)S(1)} %get-tuple-element.20), channel_id=1, source_target_pairs={{1,2},{2,1},{3,4},{4,3},{5,6},{6,5},{7,8},{8,7},{9,10},{10,9},{11,... | collective-permute-start | bytes 995336 | tf_op jit(solution)/shard_map/ppermute | solution.py:563
  13.6 8.0 %collective-permute-start.1 = (f32[25,8,128]{2,1,0:T(8,128)S(1)}, f32[25,8,128]{2,1,0:T(8,128)S(1)}, u32[]{:S(2)}, u32[]{:S(2)}) collective-permute-start(f32[25,8,128]{2,1,0:T(8,128)S(1)} %get-tuple-element.21), channel_id=1, source_target_pairs={{1,18},{2,17},{3,20},{4,19},{5,22},{6,21},{7,24},{8,23},{9,26},{10... | collective-permute-start | bytes 307208 | tf_op jit(solution)/shard_map/ppermute | solution.py:563
  29.7 6.8 %collective-permute-start.3 = (f32[2,2,16,1024]{3,2,1,0:T(8,128)S(1)}, f32[2,2,16,1024]{3,2,1,0:T(8,128)S(1)}, u32[]{:S(2)}, u32[]{:S(2)}) collective-permute-start(f32[2,2,16,1024]{3,2,1,0:T(8,128)S(1)} %get-tuple-element.24), channel_id=1, source_target_pairs={{0,16},{1,17},{2,18},{3,19},{4,20},{5,21},{6,22},{7,23},{8,24},{9,... | collective-permute-start | bytes 786440 | tf_op jit(solution)/shard_map/ppermute | solution.py:563

commit v6 on v5

--- a/solution.py
+++ b/solution.py
@@ -167,6 +167,7 @@
 HALO_TILES = 4
 LANES = 128
 
+SPARE = 1
 OVERLAP = 8
 
 sin_terms = (0.9999999995, -0.1666666515, 0.008333256964, -0.0001982776292, 2.657952479e-06)
@@ -333,7 +334,7 @@
 
         @pl.when(depth == own)
         def _():
-            other = [unpack_rows(bulk.at[1 - own], 8, n, own) for n in range(8)]
+            other = [unpack_rows(bulk, 8, n, own) for n in range(8)]
             for n in range(8):
                 partner[n] = other[n]
             readers = {
@@ -379,42 +380,68 @@
     return jnp.concatenate([tile] * (like.shape[1] // LANES), axis=1)
 
 
-def sweep_kernel(
-    width, freq_tiles, bands, back_bands, own_phases, window, partner, cross, cross_far, chip,
-    gradient, image, theirs, slow_win, pert_win, operand, halo_phases, fields, image_win, grad_win,
+def split_store(operand, f, tile, value):
+    high = value.astype(jnp.bfloat16)
+    low = (value - high.astype(jnp.float32)).astype(jnp.bfloat16)
+    base = 48 * tile
+    operand[f, base : base + 16] = high
+    operand[f, base + 16 : base + 32] = high
+    operand[f, base + 32 : base + 48] = low
+
+
+def stencil(matrix, operand, f, out_tiles, in_tiles):
+    product = jnp.dot(
+        matrix[f, : 48 * out_tiles, : 48 * in_tiles],
+        operand[f, : 48 * in_tiles],
+        preferred_element_type=jnp.float32,
+    )
+    width = product.shape[1]
+    half = width - LANES
+    lane = lax.broadcasted_iota(jnp.int32, (16, LANES), 1)
+    result = []
+    for tile in range(out_tiles):
+        base = 48 * tile
+        left = pltpu.roll(product[base : base + 16], 1, 1)
+        right = pltpu.roll(product[base + 32 : base + 48], width - 1, 1)
+        left = jnp.concatenate([jnp.where(lane == 0, 0.0, left[:, :LANES]), left[:, LANES:]], axis=1)
+        right = jnp.concatenate([right[:, :half], jnp.where(lane == LANES - 1, 0.0, right[:, half:])], axis=1)
+        result.append(product[base + 16 : base + 32] + left + right)
+    return result
+
+
+def gradient_part(freq_tile, w_re, w_im, u_re, u_im):
+    return (0.25 * over_columns(freq_tile, w_re)) * (w_im * u_re - w_re * u_im)
+
+
+def deliver(depth, whole, theirs, found):
+    half = whole.shape[2] // 2
+    blocks = half // LANES
+    for own in range(2):
+
+        @pl.when(depth == own)
+        def _():
+            inner = slice(own * LANES, own * LANES + half)
+            outer = slice(own * half, own * half + half)
+            for level in range(2):
+                for tile in range(2):
+                    whole[level, 8 * tile : 8 * tile + 8, outer] = found[2 * own + level, tile, :, inner]
+                    for block in range(blocks):
+                        first = (own + block) * LANES
+                        theirs[blocks * (2 * level + tile) + block] = found[
+                            2 * (1 - own) + level, tile, :, first : first + LANES
+                        ]
+
+
+def forward_kernel(
+    freq_tiles, bands, own_phases, window, partner, cross, cross_far, chip,
+    image, theirs, fields, halo_phases, pert_win, last_gradient, operand_out, slow_win, operand, image_win,
 ):
+    width = window.shape[2]
     depth = lax.axis_index("depth")
     place = lax.axis_index("xy")
-    half = width - LANES
     row = lax.broadcasted_iota(jnp.int32, (8, width), 0)
     upper = row < 4
-    lane = lax.broadcasted_iota(jnp.int32, (16, LANES), 1)
     even = lax.rem(place, 2) == 0
-    freqs = [jnp.concatenate([freq_tiles[f]] * (width // LANES), axis=1) for f in range(2)]
-
-    def store_operand(f, tile, value):
-        high = value.astype(jnp.bfloat16)
-        low = (value - high.astype(jnp.float32)).astype(jnp.bfloat16)
-        base = 48 * tile
-        operand[f, base : base + 16] = high
-        operand[f, base + 16 : base + 32] = high
-        operand[f, base + 32 : base + 48] = low
-
-    def stencil(f, matrix, out_tiles, in_tiles):
-        product = jnp.dot(
-            matrix[f, : 48 * out_tiles, : 48 * in_tiles],
-            operand[f, : 48 * in_tiles],
-            preferred_element_type=jnp.float32,
-        )
-        result = []
-        for tile in range(out_tiles):
-            base = 48 * tile
-            left = pltpu.roll(product[base : base + 16], 1, 1)
-            right = pltpu.roll(product[base + 32 : base + 48], width - 1, 1)
-            left = jnp.concatenate([jnp.where(lane == 0, 0.0, left[:, :LANES]), left[:, LANES:]], axis=1)
-            right = jnp.concatenate([right[:, :half], jnp.where(lane == LANES - 1, 0.0, right[:, half:])], axis=1)
-            result.append(product[base + 16 : base + 32] + left + right)
-        return result
 
     def fill(own, below_is_chip):
         chip_edges = [unpack_rows(chip, 13, n, own) for n in range(13)]
@@ -458,7 +485,7 @@
             )
         for f in range(2):
             for tile in range(6):
-                store_operand(f, tile, jnp.concatenate([planes[2 * f][tile], planes[2 * f + 1][tile]], axis=0))
+                split_store(operand, f, tile, jnp.concatenate([planes[2 * f][tile], planes[2 * f + 1][tile]], axis=0))
 
     for own in range(2):
         for below_is_chip in (False, True):
@@ -467,80 +494,89 @@
             def _():
                 fill(own, below_is_chip)
 
-    def add_image(f, level, tile, re, im):
-        part = (re * re + im * im) * 0.5
-        image_win[level, tile] = part if f == 0 else image_win[level, tile] + part
-
-    def add_gradient(f, level, tile, w_re, w_im, u_re, u_im):
-        part = (0.25 * freqs[f]) * (w_im * u_re - w_re * u_im)
-        grad_win[level, tile] = part if f == 0 else grad_win[level, tile] + part
-
-    def phases_of(f, level, tile):
+    def advance(f, level, tile, value):
         if tile < 2:
-            return own_phases[f, level, tile, :8], own_phases[f, level, tile, 8:]
-        cosine, sine = phase(freqs[f] * 0.25 * slow_win[level, tile - 2])
-        if tile == 2 and level > 0:
-            halo_phases[f, level - 1, :8] = cosine
-            halo_phases[f, level - 1, 8:] = sine
-        return cosine, sine
+            cosine, sine = own_phases[f, level, tile, :8], own_phases[f, level, tile, 8:]
+        else:
+            slow = slow_win[level, tile - 2]
+            cosine, sine = phase(over_columns(freq_tiles[f], slow) * 0.25 * slow)
+            if tile == 2 and level > 0:
+                halo_phases[f, level - 1, :8] = cosine
+                halo_phases[f, level - 1, 8:] = sine
+        v_re, v_im = value[:8], value[8:]
+        re = cosine * v_re - sine * v_im
+        im = cosine * v_im + sine * v_re
+        if tile < 2:
+            part = (re * re + im * im) * 0.5
+            image_win[level, tile] = part if f == 0 else image_win[level, tile] + part
+        return re, im
 
     tiles = (6, 5, 5, 4)
     for level in range(3):
         for f in range(2):
-            fields_now = stencil(f, bands, tiles[level + 1], tiles[level])
-            for tile, value in enumerate(fields_now):
-                cosine, sine = phases_of(f, level, tile)
-                v_re, v_im = value[:8], value[8:]
-                re = cosine * v_re - sine * v_im
-                im = cosine * v_im + sine * v_re
-                both = jnp.concatenate([re, im], axis=0)
-                store_operand(f, tile, both)
+            for tile, value in enumerate(stencil(bands, operand, f, tiles[level + 1], tiles[level])):
+                both = jnp.concatenate(advance(f, level, tile, value), axis=0)
+                split_store(operand, f, tile, both)
                 if tile < 3:
                     fields[f, level, tile] = both
-                if tile < 2:
-                    add_image(f, level, tile, re, im)
     for f in range(2):
-        for tile, value in enumerate(stencil(f, bands, 4, 4)):
+        for tile, value in enumerate(stencil(bands, operand, f, 4, 4)):
             twice = 2.0 * pert_win[3, tile]
-            v_re, v_im = value[:8], value[8:]
             if tile < 2:
-                cosine, sine = phases_of(f, 3, tile)
-                re = cosine * v_re - sine * v_im
-                im = cosine * v_im + sine * v_re
-                add_image(f, 3, tile, re, im)
-                add_gradient(f, 3, tile, twice * re, twice * im, re, im)
-            store_operand(f, tile, jnp.concatenate([twice * v_re, twice * v_im], axis=0))
+                re, im = advance(f, 3, tile, value)
+                part = gradient_part(freq_tiles[f], twice * re, twice * im, re, im)
+                last_gradient[tile] = part if f == 0 else last_gradient[tile] + part
+            split_store(operand_out, f, tile, jnp.concatenate([twice * value[:8], twice * value[8:]], axis=0))
+    deliver(depth, image, theirs, image_win)
+
+
+def backward_kernel(
+    freq_tiles, back_bands, own_phases, halo_phases, fields, pert_win, last_gradient, first_operand,
+    gradient, theirs, operand, grad_win,
+):
     tiles = (2, 3, 3, 4)
+    source = first_operand
+    for tile in range(2):
+        grad_win[3, tile] = last_gradient[tile]
     for level in (2, 1, 0):
         for f in range(2):
-            for tile, value in enumerate(stencil(f, back_bands, tiles[level], tiles[level + 1])):
+            for tile, value in enumerate(stencil(back_bands, source, f, tiles[level], tiles[level + 1])):
                 twice = 2.0 * pert_win[level, tile]
                 u_re, u_im = fields[f, level, tile, :8], fields[f, level, tile, 8:]
                 w_re = value[:8] + twice * u_re
                 w_im = value[8:] + twice * u_im
                 if tile < 2:
-                    add_gradient(f, level, tile, w_re, w_im, u_re, u_im)
+                    part = gradient_part(freq_tiles[f], w_re, w_im, u_re, u_im)
+                    grad_win[level, tile] = part if f == 0 else grad_win[level, tile] + part
                 if level > 0:
                     if tile < 2:
-                        cosine, sine = phases_of(f, level, tile)
+                        cosine, sine = own_phases[f, level, tile, :8], own_phases[f, level, tile, 8:]
                     else:
                         cosine, sine = halo_phases[f, level - 1, :8], halo_phases[f, level - 1, 8:]
                     back = [cosine * w_re + sine * w_im, cosine * w_im - sine * w_re]
-                    store_operand(f, tile, jnp.concatenate(back, axis=0))
-
-    for own in range(2):
-
-        @pl.when(depth == own)
-        def _():
-            inner = slice(own * LANES, own * LANES + half)
-            outer = slice(own * half, own * half + half)
-            for level in range(2):
-                for tile in range(2):
-                    rows = slice(8 * tile, 8 * tile + 8)
-                    gradient[level, rows, outer] = grad_win[2 * own + level, tile, :, inner]
-                    image[level, rows, outer] = image_win[2 * own + level, tile, :, inner]
-                    theirs[0, level, rows] = grad_win[2 * (1 - own) + level, tile, :, inner]
-                    theirs[1, level, rows] = image_win[2 * (1 - own) + level, tile, :, inner]
+                    split_store(operand, f, tile, jnp.concatenate(back, axis=0))
+        source = operand
+    deliver(lax.axis_index("depth"), gradient, theirs, grad_win)
+
+
+def update_kernel(gradient_tiles, image_tiles, gradient_in, image_in, gradient, image, gradient_rows, image_rows, sems):
+    half = gradient_rows.shape[2]
+    blocks = half // LANES
+    start = pl.multiple_of((1 - lax.axis_index("depth")) * half, LANES)
+    copies = []
+    for n, (tiles, rows, whole) in enumerate(
+        ((image_tiles, image_rows, image), (gradient_tiles, gradient_rows, gradient))
+    ):
+        for level in range(2):
+            for tile in range(2):
+                for block in range(blocks):
+                    rows[level, 8 * tile : 8 * tile + 8, LANES * block : LANES * (block + 1)] = tiles[
+                        blocks * (2 * level + tile) + block
+                    ]
+        copies.append(pltpu.make_async_copy(rows, whole.at[:, :, pl.ds(start, half)], sems.at[n]))
+        copies[-1].start()
+    for copy in copies:
+        copy.wait()
 
 
 def split_columns(surface_data, frequencies, coefficients, slowness, perturbation):
@@ -582,7 +618,7 @@
         name="pack",
     )(*(pltpu.with_memory_space_constraint(x, pltpu.HBM) for x in (surface_data, slowness, perturbation)))
     cross = moved(cross, False, "cross")
-    bulk = lax.all_gather(bulk, "depth")
+    bulk = moved(bulk, True, "same")
     cross_far = moved(cross_far, True, "cross")
     bands, back_bands, freq_tiles = pl.pallas_call(
         lambda *refs: band_kernel(count * ROWS, *refs),
@@ -618,30 +654,55 @@
     )(freq_tiles, window, partner)
 
     own = jax.ShapeDtypeStruct((2, ROWS, columns), f32)
-    gradient, image, theirs = pl.pallas_call(
-        lambda *refs: sweep_kernel(width, *refs),
-        out_shape=(own, own, jax.ShapeDtypeStruct((2, 2, ROWS, half), f32)),
-        in_specs=[vmem] * 9,
-        out_specs=(vmem,) * 3,
+    sent = lambda spare: jax.ShapeDtypeStruct((2 * ROWS // 8 * half // LANES + spare, 8, LANES), f32)
+    image, theirs_image, fields, halo_phases, pert_win, last_gradient, operand = pl.pallas_call(
+        forward_kernel,
+        out_shape=(
+            own,
+            sent(SPARE),
+            jax.ShapeDtypeStruct((2, 3, 3, 16, width), f32),
+            jax.ShapeDtypeStruct((2, 2, 16, width), f32),
+            jax.ShapeDtypeStruct((4, 4, 8, width), f32),
+            tile(2),
+            jax.ShapeDtypeStruct((2, 192, width), jnp.bfloat16),
+        ),
+        in_specs=[vmem] * 8,
+        out_specs=(vmem,) * 7,
         scratch_shapes=[
             pltpu.VMEM((3, 3, 8, width), f32),
-            pltpu.VMEM((4, 4, 8, width), f32),
             pltpu.VMEM((2, 288, width), jnp.bfloat16),
-            pltpu.VMEM((2, 2, 16, width), f32),
-            pltpu.VMEM((2, 3, 3, 16, width), f32),
-            pltpu.VMEM((4, 2, 8, width), f32),
             pltpu.VMEM((4, 2, 8, width), f32),
         ],
-        compiler_params=params(40),
-        name="sweep",
-    )(
-        freq_tiles, bands, back_bands, own_phases, window, partner, cross, cross_far, chip,
-    )
+        compiler_params=params(32),
+        name="forward",
+    )(freq_tiles, bands, own_phases, window, partner, cross, cross_far, chip)
+    gradient, theirs = pl.pallas_call(
+        backward_kernel,
+        out_shape=(own, sent(0)),
+        in_specs=[vmem] * 8,
+        out_specs=(vmem,) * 2,
+        scratch_shapes=[
+            pltpu.VMEM((2, 144, width), jnp.bfloat16),
+            pltpu.VMEM((4, 2, 8, width), f32),
+        ],
+        compiler_params=params(32),
+        cost_estimate=pl.CostEstimate(flops=10**10, bytes_accessed=10**6, transcendentals=0),
+        name="backward",
+    )(freq_tiles, back_bands, own_phases, halo_phases, fields, pert_win, last_gradient, operand)
+    theirs_image = moved(theirs_image, True, "same")
     theirs = moved(theirs, True, "same")
-    start = (1 - lax.axis_index("depth")) * half
-    gradient = lax.dynamic_update_slice(gradient, theirs[0], (0, 0, start))
-    image = lax.dynamic_update_slice(image, theirs[1], (0, 0, start))
-    return gradient, image
+    hbm = pl.BlockSpec(memory_space=pltpu.HBM)
+    in_place = [pltpu.with_memory_space_constraint(x, pltpu.HBM) for x in (gradient, image)]
+    return pl.pallas_call(
+        update_kernel,
+        out_shape=(own, own),
+        in_specs=[vmem, vmem, hbm, hbm],
+        out_specs=(hbm, hbm),
+        scratch_shapes=[pltpu.VMEM((2, ROWS, half), f32)] * 2 + [pltpu.SemaphoreType.DMA((2,))],
+        input_output_aliases={2: 0, 3: 1},
+        compiler_params=params(8),
+        name="update",
+    )(theirs, theirs_image, *in_place)
 
 
 def on_slice(surface_data, frequencies, coefficients, slowness, perturbation):

time: 37.5 us -> 31.2 us (0.83)
  blocking collectives: 8.82 us -> 0 us
  Pallas kernels: 7.9 us -> 9.48 us
  starting transfers between devices: 8 us -> 9.18 us
    all_gather x1 -> x0, blocking collectives: 8.82 us -> none  [split_columns(): bulk = lax.all_gather(bulk, 'depth')]
    pallas_call x1 -> x3, Pallas kernels: 4.42 us -> 6.01 us  [the longest x1 3.4 us: split_columns(): pl.pallas_call(forward_kernel, out_shape=(own, sent(SPARE), jax.ShapeDtyp...]
    ppermute x4 -> x6, starting transfers between devices: 8 us -> 9.18 us  [moved(): return lax.ppermute(value, axes, pairs)]
    dynamic_update_slice x1 -> x0, local copies, waits for them, and re-layouts: 0.72 us -> none  [split_columns(): image = lax.dynamic_update_slice(image, theirs[1], (0, 0, start))]
    unnamed x4, local copies, waits for them, and re-layouts: 0.01 us -> 0.43 us
    ppermute x4 -> x6, waiting for transfers between devices: 11.1 us -> 11.1 us  [moved(): return lax.ppermute(value, axes, pairs)]
  transfers between devices with their start and end apart: 4 -> 6, of which waited for: 3 -> 3; matrix products, arithmetic and copies ran while one was open for 0% -> 0% of each run, Pallas kernels for 5% -> 13%
where the time goes in v6:
time: 31.2 us; the launch traced here: 30.9 us
  waiting for transfers between devices  11.1 us (36%)
  Pallas kernels  9.48 us (30%)
  starting transfers between devices  9.18 us (29%)
  between operations  0.7 us (2%)
  local copies, waits for them, and re-layouts  0.43 us (1%)
    ppermute x6, waiting for transfers between devices, moved(): return lax.ppermute(value, axes, pairs)  11.1 us
    ppermute x6, starting transfers between devices, moved(): return lax.ppermute(value, axes, pairs)  9.18 us
    pallas_call x1, Pallas kernels, split_columns(): pl.pallas_call(forward_kernel, out_shape=(own, sent(SPARE), jax.ShapeDtyp...  3.4 us
    pallas_call x1, Pallas kernels, split_columns(): pl.pallas_call(backward_kernel, out_shape=(own, sent(0)), in_specs=[vmem]...  1.88 us
    pallas_call x1, Pallas kernels, split_columns(): pl.pallas_call(lambda *refs: band_kernel(count * ROWS, *refs), out_shape=...  1.45 us
    pallas_call x1, Pallas kernels, split_columns(): pl.pallas_call(lambda *refs: pack_kernel(width, step, *refs), out_shape=(...  1.39 us
    pallas_call x1, Pallas kernels, split_columns(): pl.pallas_call(update_kernel, out_shape=(own, own), in_specs=[vmem, vmem,...  0.73 us
  transfers between devices with their start and end apart: 6, of which 3 were waited for; matrix products, arithmetic and copies ran while one was open for 0% of the time, Pallas kernels for 13%

profile of v6, /device:TPU:20, one launch (start us, length us, event | category | flops | bytes accessed | tf_op | source)
XLA Modules:
  0.0 30.9 jit_solution(14054821173009093164)
XLA Ops:
  0.6 1.4 %pack.1 = (f32[81,8,128]{2,1,0:T(8,128)S(1)}, f32[65,8,128]{2,1,0:T(8,128)S(1)}, f32[25,8,128]{2,1,0:T(8,128)S(1)}, f32[16,8,1152]{2,1,0:T(8,128)S(1)}) custom-call(f32[2,2,16,2048]{3,2,1,0:T(8,128)} %refs_0_.3, f32[2,16,2048]{2,1,0:T(8,128)} %refs_1_.3, f32[2,16,2048]{2,1,0:T(8,128)} %refs_2_.1), custom_call_target="tpu_custom_call" | custom-call | tf_op jit(solution)/shard_map/pack/pallas_call | solution.py:606
  2.0 1.6 %collective-permute-start = (f32[65,8,128]{2,1,0:T(8,128)S(1)}, f32[65,8,128]{2,1,0:T(8,128)S(1)}, u32[]{:S(2)}, u32[]{:S(2)}) collective-permute-start(f32[65,8,128]{2,1,0:T(8,128)S(1)} %get-tuple-element.23), channel_id=1, source_target_pairs={{0,16},{1,17},{2,18},{3,19},{4,20},{5,21},{6,22},{7,23},{8,24},{9,... | collective-permute-start | bytes 798728 | tf_op jit(solution)/shard_map/ppermute | solution.py:599
  3.6 1.9 %collective-permute-start.2 = (f32[25,8,128]{2,1,0:T(8,128)S(1)}, f32[25,8,128]{2,1,0:T(8,128)S(1)}, u32[]{:S(2)}, u32[]{:S(2)}) collective-permute-start(f32[25,8,128]{2,1,0:T(8,128)S(1)} %get-tuple-element.27), channel_id=1, source_target_pairs={{1,18},{2,17},{3,20},{4,19},{5,22},{6,21},{7,24},{8,23},{9,26},{10... | collective-permute-start | bytes 307208 | tf_op jit(solution)/shard_map/ppermute | solution.py:599
  5.5 3.6 %collective-permute-start.1 = (f32[81,8,128]{2,1,0:T(8,128)S(1)}, f32[81,8,128]{2,1,0:T(8,128)S(1)}, u32[]{:S(2)}, u32[]{:S(2)}) collective-permute-start(f32[81,8,128]{2,1,0:T(8,128)S(1)} %get-tuple-element.26), channel_id=1, source_target_pairs={{1,2},{2,1},{3,4},{4,3},{5,6},{6,5},{7,8},{8,7},{9,10},{10,9},{11,... | collective-permute-start | bytes 995336 | tf_op jit(solution)/shard_map/ppermute | solution.py:599
  9.1 2.2 %collective-permute-done.bulk = f32[65,8,128]{2,1,0:T(8,128)S(1)} collective-permute-done((f32[65,8,128]{2,1,0:T(8,128)S(1)}, f32[65,8,128]{2,1,0:T(8,128)S(1)}, u32[]{:S(2)}, u32[]{:S(2)}) %collective-permute-start) | collective-permute-done | bytes 266272 | tf_op jit(solution)/shard_map/ppermute | solution.py:599
  11.3 0.0 copy-start
  11.3 0.0 copy-start.1
  11.3 0.2 relay.1
  11.5 0.1 collective-permute-start.3
  11.6 0.4 %copy-done = f32[2,2,15]{2,1,0:T(2,128)S(1)} copy-done((f32[2,2,15]{2,1,0:T(2,128)S(1)}, f32[2,2,15]{2,1,0:T(2,128)}, u32[]{:S(2)}) %copy-start) | copy-done | bytes 264
  12.0 0.0 copy-done.1
  12.0 1.5 %bands.1 = (bf16[2,240,288]{2,1,0:T(8,128)(2,1)S(1)}, bf16[2,144,192]{2,1,0:T(8,128)(2,1)S(1)}, f32[2,8,128]{2,1,0:T(8,128)S(1)}) custom-call(f32[2,2,15]{2,1,0:T(2,128)S(1)} %copy-done, f32[2]{0:T(128)S(1)} %copy-done.1), custom_call_target="tpu_custom_call" | custom-call | flops 10000000000 | bytes 1000000 | tf_op jit(solution)/shard_map/bands/pallas_call | solution.py:623
  13.5 0.5 %own_phases.1 = f32[2,4,2,16,1152]{4,3,2,1,0:T(8,128)S(1)} custom-call(f32[2,8,128]{2,1,0:T(8,128)S(1)} %get-tuple-element.20.freq_tiles, f32[16,8,1152]{2,1,0:T(8,128)S(1)} %get-tuple-element.22.window, f32[8,8,1152]{2,1,0:T(8,128)S(1)} %get-tuple-element.24.partner), custom_call_target="tpu_custom_call" | custom-call | tf_op jit(solution)/shard_map/own_phases/pallas_call | solution.py:647
  13.9 0.0 collective-permute-done.2.cross_far
  14.0 5.1 %collective-permute-done.1.cross = f32[81,8,128]{2,1,0:T(8,128)S(1)} collective-permute-done((f32[81,8,128]{2,1,0:T(8,128)S(1)}, f32[81,8,128]{2,1,0:T(8,128)S(1)}, u32[]{:S(2)}, u32[]{:S(2)}) %collective-permute-start.1) | collective-permute-done | bytes 331808 | tf_op jit(solution)/shard_map/ppermute | solution.py:599
  19.1 0.0 collective-permute-done.3.chip
  19.1 3.4 %forward.1 = (f32[2,16,2048]{2,1,0:T(8,128)}, f32[33,8,128]{2,1,0:T(8,128)S(1)}, f32[2,3,3,16,1152]{4,3,2,1,0:T(8,128)S(1)}, f32[2,2,16,1152]{3,2,1,0:T(8,128)S(...) custom-call(f32[2,8,128]{2,1,0:T(8,128)S(1)} %get-tuple-element.20.freq_tiles, ...), custom_call_target="tpu_custom_call" | custom-call | tf_op jit(solution)/shard_map/forward/pallas_call | solution.py:658
  22.5 0.9 %collective-permute-start.5 = (f32[33,8,128]{2,1,0:T(8,128)S(1)}, f32[33,8,128]{2,1,0:T(8,128)S(1)}, u32[]{:S(2)}, u32[]{:S(2)}) collective-permute-start(f32[33,8,128]{2,1,0:T(8,128)S(1)} %get-tuple-element.35), channel_id=1, source_target_pairs={{0,16},{1,17},{2,18},{3,19},{4,20},{5,21},{6,22},{7,23},{8,24},{9,... | collective-permute-start | bytes 405512 | tf_op jit(solution)/shard_map/ppermute | solution.py:599
  23.3 1.9 %backward.1 = (f32[2,16,2048]{2,1,0:T(8,128)}, f32[32,8,128]{2,1,0:T(8,128)S(1)}) custom-call(f32[2,8,128]{2,1,0:T(8,128)S(1)} %get-tuple-element.20.freq_tiles, bf16[2,144,192]{2,1,0:T(8,128)(2,1)S(1)} %get-tuple-element.21.back_bands, f32[2,4,2,16,1152]{4,3,2,1,0:T(8,128)S(1)} %own_phases.1, f32[2,2,16,1152]{3,2,1,0:T(8,128)S(1)} %get-tuple-element.29.halo_phases, ...), custom_call_target="tpu_custom_call" | custom-call | flops 10000000000 | bytes 1000000 | tf_op jit(solution)/shard_map/backward/pallas_call | solution.py:679
  25.2 1.2 %collective-permute-start.4 = (f32[32,8,128]{2,1,0:T(8,128)S(1)}, f32[32,8,128]{2,1,0:T(8,128)S(1)}, u32[]{:S(2)}, u32[]{:S(2)}) collective-permute-start(f32[32,8,128]{2,1,0:T(8,128)S(1)} %get-tuple-element.34), channel_id=1, source_target_pairs={{0,16},{1,17},{2,18},{3,19},{4,20},{5,21},{6,22},{7,23},{8,24},{9,... | collective-permute-start | bytes 393224 | tf_op jit(solution)/shard_map/ppermute | solution.py:599
  26.4 3.8 %collective-permute-done.4.gradient_tiles = f32[32,8,128]{2,1,0:T(8,128)S(1)} collective-permute-done((f32[32,8,128]{2,1,0:T(8,128)S(1)}, f32[32,8,128]{2,1,0:T(8,128)S(1)}, u32[]{:S(2)}, u32[]{:S(2)}) %collective-permute-start.4) | collective-permute-done | bytes 131104 | tf_op jit(solution)/shard_map/ppermute | solution.py:599
  30.2 0.0 collective-permute-done.5.image_tiles
  30.2 0.7 %update.1 = (f32[2,16,2048]{2,1,0:T(8,128)}, f32[2,16,2048]{2,1,0:T(8,128)}) custom-call(f32[32,8,128]{2,1,0:T(8,128)S(1)} %collective-permute-done.4.gradient_tiles, f32[33,8,128]{2,1,0:T(8,128)S(1)} %collective-permute-done.5.image_tiles, f32[2,16,2048]{2,1,0:T(8,128)} %get-tuple-element.36.gradient_in, ...), custom_call_target="tpu_custom_call", output_to_operand_aliasing={{0}: (2, {}), {1}: (3, {})} | custom-call | tf_op jit(solution)/shard_map/update/pallas_call | solution.py:696
Async XLA Ops:
  2.0 9.3 %collective-permute-start = (f32[65,8,128]{2,1,0:T(8,128)S(1)}, f32[65,8,128]{2,1,0:T(8,128)S(1)}, u32[]{:S(2)}, u32[]{:S(2)}) collective-permute-start(f32[65,8,128]{2,1,0:T(8,128)S(1)} %get-tuple-element.23), channel_id=1, source_target_pairs={{0,16},{1,17},{2,18},{3,19},{4,20},{5,21},{6,22},{7,23},{8,24},{9,... | collective-permute-start | bytes 798728 | tf_op jit(solution)/shard_map/ppermute | solution.py:599
  3.6 10.4 %collective-permute-start.2 = (f32[25,8,128]{2,1,0:T(8,128)S(1)}, f32[25,8,128]{2,1,0:T(8,128)S(1)}, u32[]{:S(2)}, u32[]{:S(2)}) collective-permute-start(f32[25,8,128]{2,1,0:T(8,128)S(1)} %get-tuple-element.27), channel_id=1, source_target_pairs={{1,18},{2,17},{3,20},{4,19},{5,22},{6,21},{7,24},{8,23},{9,26},{10... | collective-permute-start | bytes 307208 | tf_op jit(solution)/shard_map/ppermute | solution.py:599
  5.5 13.6 %collective-permute-start.1 = (f32[81,8,128]{2,1,0:T(8,128)S(1)}, f32[81,8,128]{2,1,0:T(8,128)S(1)}, u32[]{:S(2)}, u32[]{:S(2)}) collective-permute-start(f32[81,8,128]{2,1,0:T(8,128)S(1)} %get-tuple-element.26), channel_id=1, source_target_pairs={{1,2},{2,1},{3,4},{4,3},{5,6},{6,5},{7,8},{8,7},{9,10},{10,9},{11,... | collective-permute-start | bytes 995336 | tf_op jit(solution)/shard_map/ppermute | solution.py:599
  11.3 0.7 %copy-start = (f32[2,2,15]{2,1,0:T(2,128)S(1)}, f32[2,2,15]{2,1,0:T(2,128)}, u32[]{:S(2)}) copy-start(f32[2,2,15]{2,1,0:T(2,128)} %refs_0_.2) | copy-start | bytes 724
  11.3 0.7 %copy-start.1 = (f32[2]{0:T(128)S(1)}, f32[2]{0:T(128)}, u32[]{:S(2)}) copy-start(f32[2]{0:T(128)} %refs_1_.2) | copy-start | bytes 28
  11.5 7.5 %collective-permute-start.3 = (f32[105,8,128]{2,1,0:T(8,128)S(1)}, f32[105,8,128]{2,1,0:T(8,128)S(1)}, u32[]{:S(2)}, u32[]{:S(2)}) collective-permute-start(f32[105,8,128]{2,1,0:T(8,128)S(1)} %get-tuple-element.28), channel_id=1, source_target_pairs={{0,1},{1,0},{2,3},{3,2},{4,5},{5,4},{6,7},{7,6},{8,9},{9,8},{10,11... | collective-permute-start | bytes 1290248 | tf_op jit(solution)/shard_map/ppermute | solution.py:599
  22.5 7.7 %collective-permute-start.5 = (f32[33,8,128]{2,1,0:T(8,128)S(1)}, f32[33,8,128]{2,1,0:T(8,128)S(1)}, u32[]{:S(2)}, u32[]{:S(2)}) collective-permute-start(f32[33,8,128]{2,1,0:T(8,128)S(1)} %get-tuple-element.35), channel_id=1, source_target_pairs={{0,16},{1,17},{2,18},{3,19},{4,20},{5,21},{6,22},{7,23},{8,24},{9,... | collective-permute-start | bytes 405512 | tf_op jit(solution)/shard_map/ppermute | solution.py:599
  25.2 5.0 %collective-permute-start.4 = (f32[32,8,128]{2,1,0:T(8,128)S(1)}, f32[32,8,128]{2,1,0:T(8,128)S(1)}, u32[]{:S(2)}, u32[]{:S(2)}) collective-permute-start(f32[32,8,128]{2,1,0:T(8,128)S(1)} %get-tuple-element.34), channel_id=1, source_target_pairs={{0,16},{1,17},{2,18},{3,19},{4,20},{5,21},{6,22},{7,23},{8,24},{9,... | collective-permute-start | bytes 393224 | tf_op jit(solution)/shard_map/ppermute | solution.py:599

commit v7 on v5

--- a/solution.py
+++ b/solution.py
@@ -286,10 +286,10 @@
 
 
 def pack_kernel(width, step, surf_in, slow_in, pert_in, cross, bulk, cross_far, window, surf, slow, pert, sems):
-    copies = [
-        pltpu.make_async_copy(source, target, sems.at[n])
-        for n, (source, target) in enumerate(((slow_in, slow), (pert_in, pert), (surf_in, surf)))
-    ]
+    pairs = [(slow_in.at[level], slow.at[level]) for level in range(2)]
+    pairs += [(pert_in.at[level], pert.at[level]) for level in range(2)]
+    pairs += [(surf_in.at[f, part], surf.at[f, part]) for f in range(2) for part in range(2)]
+    copies = [pltpu.make_async_copy(source, target, sems.at[n]) for n, (source, target) in enumerate(pairs)]
     for copy in copies:
         copy.start()
     for copy in copies:
@@ -333,7 +333,7 @@
 
         @pl.when(depth == own)
         def _():
-            other = [unpack_rows(bulk.at[1 - own], 8, n, own) for n in range(8)]
+            other = [unpack_rows(bulk, 8, n, own) for n in range(8)]
             for n in range(8):
                 partner[n] = other[n]
             readers = {
@@ -576,13 +576,13 @@
             pltpu.VMEM(surface_data.shape, f32),
             pltpu.VMEM(slowness.shape, f32),
             pltpu.VMEM(perturbation.shape, f32),
-            pltpu.SemaphoreType.DMA((3,)),
+            pltpu.SemaphoreType.DMA((8,)),
         ],
         compiler_params=params(32),
         name="pack",
     )(*(pltpu.with_memory_space_constraint(x, pltpu.HBM) for x in (surface_data, slowness, perturbation)))
     cross = moved(cross, False, "cross")
-    bulk = lax.all_gather(bulk, "depth")
+    bulk = moved(bulk, True, "same")
     cross_far = moved(cross_far, True, "cross")
     bands, back_bands, freq_tiles = pl.pallas_call(
         lambda *refs: band_kernel(count * ROWS, *refs),

time: 37.5 us -> 29.6 us (0.79)
  blocking collectives: 8.82 us -> 0 us
  waiting for transfers between devices: 11.1 us -> 11.8 us
  local copies, waits for them, and re-layouts: 0.72 us -> 1.15 us
    all_gather x1 -> x0, blocking collectives: 8.82 us -> none  [split_columns(): bulk = lax.all_gather(bulk, 'depth')]
    ppermute x4 -> x5, waiting for transfers between devices: 11.1 us -> 11.8 us  [moved(): return lax.ppermute(value, axes, pairs)]
    unnamed x4, local copies, waits for them, and re-layouts: 0.01 us -> 0.43 us
    ppermute x4 -> x5, starting transfers between devices: 8 us -> 7.69 us  [moved(): return lax.ppermute(value, axes, pairs)]
  transfers between devices with their start and end apart: 4 -> 5, of which waited for: 3 -> 4; matrix products, arithmetic and copies ran while one was open for 0% -> 0% of each run, Pallas kernels for 5% -> 7%
where the time goes in v7:
time: 29.6 us; the launch traced here: 29.4 us
  waiting for transfers between devices  11.8 us (40%)
  Pallas kernels  8.01 us (27%)
  starting transfers between devices  7.69 us (26%)
  local copies, waits for them, and re-layouts  1.15 us (4%)
  between operations  0.69 us (2%)
    ppermute x5, waiting for transfers between devices, moved(): return lax.ppermute(value, axes, pairs)  11.8 us
    ppermute x5, starting transfers between devices, moved(): return lax.ppermute(value, axes, pairs)  7.69 us
    pallas_call x1, Pallas kernels, split_columns(): pl.pallas_call(lambda *refs: sweep_kernel(width, *refs), out_shape=(own,...  4.41 us
    pallas_call x1, Pallas kernels, split_columns(): pl.pallas_call(lambda *refs: pack_kernel(width, step, *refs), out_shape=(...  1.51 us
    pallas_call x1, Pallas kernels, split_columns(): pl.pallas_call(lambda *refs: band_kernel(count * ROWS, *refs), out_shape=...  1.45 us
    dynamic_update_slice x1, local copies, waits for them, and re-layouts, split_columns(): image = lax.dynamic_update_slice(image, theirs[1], (0, 0, start))  0.72 us
  transfers between devices with their start and end apart: 5, of which 4 were waited for; matrix products, arithmetic and copies ran while one was open for 0% of the time, Pallas kernels for 7%

profile of v7, /device:TPU:20, one launch (start us, length us, event | category | flops | bytes accessed | tf_op | source)
XLA Modules:
  0.0 29.4 jit_solution(7375682380489831309)
XLA Ops:
  0.6 1.5 %pack.1 = (f32[81,8,128]{2,1,0:T(8,128)S(1)}, f32[65,8,128]{2,1,0:T(8,128)S(1)}, f32[25,8,128]{2,1,0:T(8,128)S(1)}, f32[16,8,1152]{2,1,0:T(8,128)S(1)}) custom-call(f32[2,2,16,2048]{3,2,1,0:T(8,128)} %refs_0_.3, f32[2,16,2048]{2,1,0:T(8,128)} %refs_1_.3, f32[2,16,2048]{2,1,0:T(8,128)} %refs_2_.1), custom_call_target="tpu_custom_call" | custom-call | tf_op jit(solution)/shard_map/pack/pallas_call | solution.py:570
  2.1 1.6 %collective-permute-start = (f32[65,8,128]{2,1,0:T(8,128)S(1)}, f32[65,8,128]{2,1,0:T(8,128)S(1)}, u32[]{:S(2)}, u32[]{:S(2)}) collective-permute-start(f32[65,8,128]{2,1,0:T(8,128)S(1)} %get-tuple-element.18), channel_id=1, source_target_pairs={{0,16},{1,17},{2,18},{3,19},{4,20},{5,21},{6,22},{7,23},{8,24},{9,... | collective-permute-start | bytes 798728 | tf_op jit(solution)/shard_map/ppermute | solution.py:563
  3.7 1.9 %collective-permute-start.1 = (f32[81,8,128]{2,1,0:T(8,128)S(1)}, f32[81,8,128]{2,1,0:T(8,128)S(1)}, u32[]{:S(2)}, u32[]{:S(2)}) collective-permute-start(f32[81,8,128]{2,1,0:T(8,128)S(1)} %get-tuple-element.20), channel_id=1, source_target_pairs={{1,2},{2,1},{3,4},{4,3},{5,6},{6,5},{7,8},{8,7},{9,10},{10,9},{11,... | collective-permute-start | bytes 995336 | tf_op jit(solution)/shard_map/ppermute | solution.py:563
  5.6 3.6 %collective-permute-start.2 = (f32[25,8,128]{2,1,0:T(8,128)S(1)}, f32[25,8,128]{2,1,0:T(8,128)S(1)}, u32[]{:S(2)}, u32[]{:S(2)}) collective-permute-start(f32[25,8,128]{2,1,0:T(8,128)S(1)} %get-tuple-element.21), channel_id=1, source_target_pairs={{1,18},{2,17},{3,20},{4,19},{5,22},{6,21},{7,24},{8,23},{9,26},{10... | collective-permute-start | bytes 307208 | tf_op jit(solution)/shard_map/ppermute | solution.py:563
  9.2 1.1 %collective-permute-done.bulk = f32[65,8,128]{2,1,0:T(8,128)S(1)} collective-permute-done((f32[65,8,128]{2,1,0:T(8,128)S(1)}, f32[65,8,128]{2,1,0:T(8,128)S(1)}, u32[]{:S(2)}, u32[]{:S(2)}) %collective-permute-start) | collective-permute-done | bytes 266272 | tf_op jit(solution)/shard_map/ppermute | solution.py:563
  10.4 0.0 copy-start
  10.4 0.0 copy-start.1
  10.4 0.2 relay.1
  10.5 0.1 collective-permute-start.3
  10.6 0.4 %copy-done = f32[2,2,15]{2,1,0:T(2,128)S(1)} copy-done((f32[2,2,15]{2,1,0:T(2,128)S(1)}, f32[2,2,15]{2,1,0:T(2,128)}, u32[]{:S(2)}) %copy-start) | copy-done | bytes 264
  11.0 0.0 copy-done.1
  11.0 1.5 %bands.1 = (bf16[2,240,288]{2,1,0:T(8,128)(2,1)S(1)}, bf16[2,144,192]{2,1,0:T(8,128)(2,1)S(1)}, f32[2,8,128]{2,1,0:T(8,128)S(1)}) custom-call(f32[2,2,15]{2,1,0:T(2,128)S(1)} %copy-done, f32[2]{0:T(128)S(1)} %copy-done.1), custom_call_target="tpu_custom_call" | custom-call | flops 10000000000 | bytes 1000000 | tf_op jit(solution)/shard_map/bands/pallas_call | solution.py:587
  12.5 0.5 %own_phases.1.refs_3_ = f32[2,4,2,16,1152]{4,3,2,1,0:T(8,128)S(1)} custom-call(f32[2,8,128]{2,1,0:T(8,128)S(1)} %get-tuple-element.14.freq_tiles.refs_0_, f32[16,8,1152]{2,1,0:T(8,128)S(1)} %get-tuple-element.17.window.refs_4_, f32[8,8,1152]{2,1,0:T(8,128)S(1)} %get-tuple-element.19.partner.refs_5_), custom_call_target="tpu_custom_call" | custom-call | tf_op jit(solution)/shard_map/own_phases/pallas_call | solution.py:611
  13.0 0.7 %collective-permute-done.2.refs_7_ = f32[25,8,128]{2,1,0:T(8,128)S(1)} collective-permute-done((f32[25,8,128]{2,1,0:T(8,128)S(1)}, f32[25,8,128]{2,1,0:T(8,128)S(1)}, u32[]{:S(2)}, u32[]{:S(2)}) %collective-permute-start.2) | collective-permute-done | bytes 102432 | tf_op jit(solution)/shard_map/ppermute | solution.py:563
  13.6 4.2 %collective-permute-done.1.refs_6_ = f32[81,8,128]{2,1,0:T(8,128)S(1)} collective-permute-done((f32[81,8,128]{2,1,0:T(8,128)S(1)}, f32[81,8,128]{2,1,0:T(8,128)S(1)}, u32[]{:S(2)}, u32[]{:S(2)}) %collective-permute-start.1) | collective-permute-done | bytes 331808 | tf_op jit(solution)/shard_map/ppermute | solution.py:563
  17.9 0.0 collective-permute-done.3.refs_8_
  17.9 4.4 %sweep.1 = (f32[2,16,2048]{2,1,0:T(8,128)}, f32[2,16,2048]{2,1,0:T(8,128)}, f32[2,2,16,1024]{3,2,1,0:T(8,128)S(1)}) custom-call(f32[2,8,128]{2,1,0:T(8,128)S(1)} %get-tuple-element.14.freq_tiles.refs_0_, bf16[2,240,288]{2,1,0:T(8,128)(2,1)S(1)} %get-tuple-element.15.refs_1_, bf16[2,144,192]{2,1,0:T(8,128)(2,1)S(1)} %get-tuple-element.16.refs_2_, ...), custom_call_target="tpu_custom_call" | custom-call | tf_op jit(solution)/shard_map/sweep/pallas_call | solution.py:621
  22.3 0.5 %collective-permute-start.4 = (f32[2,2,16,1024]{3,2,1,0:T(8,128)S(1)}, f32[2,2,16,1024]{3,2,1,0:T(8,128)S(1)}, u32[]{:S(2)}, u32[]{:S(2)}) collective-permute-start(f32[2,2,16,1024]{3,2,1,0:T(8,128)S(1)} %get-tuple-element.24), channel_id=1, source_target_pairs={{0,16},{1,17},{2,18},{3,19},{4,20},{5,21},{6,22},{7,23},{8,24},{9,... | collective-permute-start | bytes 786440 | tf_op jit(solution)/shard_map/ppermute | solution.py:563
  22.8 5.8 %collective-permute-done.4 = f32[2,2,16,1024]{3,2,1,0:T(8,128)S(1)} collective-permute-done((f32[2,2,16,1024]{3,2,1,0:T(8,128)S(1)}, f32[2,2,16,1024]{3,2,1,0:T(8,128)S(1)}, u32[]{:S(2)}, u32[]{:S(2)}) %collective-permute-start.4) | collective-permute-done | bytes 262176 | tf_op jit(solution)/shard_map/ppermute | solution.py:563
  28.7 0.7 %fusion = (f32[2,16,2048]{2,1,0:T(8,128)}, f32[2,16,2048]{2,1,0:T(8,128)}) fusion(f32[2,16,2048]{2,1,0:T(8,128)} %get-tuple-element.25, s32[]{:T(128)S(6)} %select_n.4, f32[2,2,16,1024]{3,2,1,0:T(8,128)S(1)} %collective-permute-done.4, f32[2,16,2048]{2,1,0:T(8,128)} %get-tuple-element.23), kind=kLoop, calls=%fused_computation.1 | loop fusion | bytes 524292 | tf_op jit(solution)/shard_map/dynamic_update_slice | solution.py:643
Async XLA Ops:
  2.1 8.2 %collective-permute-start = (f32[65,8,128]{2,1,0:T(8,128)S(1)}, f32[65,8,128]{2,1,0:T(8,128)S(1)}, u32[]{:S(2)}, u32[]{:S(2)}) collective-permute-start(f32[65,8,128]{2,1,0:T(8,128)S(1)} %get-tuple-element.18), channel_id=1, source_target_pairs={{0,16},{1,17},{2,18},{3,19},{4,20},{5,21},{6,22},{7,23},{8,24},{9,... | collective-permute-start | bytes 798728 | tf_op jit(solution)/shard_map/ppermute | solution.py:563
  3.7 14.2 %collective-permute-start.1 = (f32[81,8,128]{2,1,0:T(8,128)S(1)}, f32[81,8,128]{2,1,0:T(8,128)S(1)}, u32[]{:S(2)}, u32[]{:S(2)}) collective-permute-start(f32[81,8,128]{2,1,0:T(8,128)S(1)} %get-tuple-element.20), channel_id=1, source_target_pairs={{1,2},{2,1},{3,4},{4,3},{5,6},{6,5},{7,8},{8,7},{9,10},{10,9},{11,... | collective-permute-start | bytes 995336 | tf_op jit(solution)/shard_map/ppermute | solution.py:563
  5.6 8.0 %collective-permute-start.2 = (f32[25,8,128]{2,1,0:T(8,128)S(1)}, f32[25,8,128]{2,1,0:T(8,128)S(1)}, u32[]{:S(2)}, u32[]{:S(2)}) collective-permute-start(f32[25,8,128]{2,1,0:T(8,128)S(1)} %get-tuple-element.21), channel_id=1, source_target_pairs={{1,18},{2,17},{3,20},{4,19},{5,22},{6,21},{7,24},{8,23},{9,26},{10... | collective-permute-start | bytes 307208 | tf_op jit(solution)/shard_map/ppermute | solution.py:563
  10.4 0.7 %copy-start = (f32[2,2,15]{2,1,0:T(2,128)S(1)}, f32[2,2,15]{2,1,0:T(2,128)}, u32[]{:S(2)}) copy-start(f32[2,2,15]{2,1,0:T(2,128)} %refs_0_.2) | copy-start | bytes 724
  10.4 0.7 %copy-start.1 = (f32[2]{0:T(128)S(1)}, f32[2]{0:T(128)}, u32[]{:S(2)}) copy-start(f32[2]{0:T(128)} %refs_1_.2) | copy-start | bytes 28
  10.5 7.3 %collective-permute-start.3 = (f32[105,8,128]{2,1,0:T(8,128)S(1)}, f32[105,8,128]{2,1,0:T(8,128)S(1)}, u32[]{:S(2)}, u32[]{:S(2)}) collective-permute-start(f32[105,8,128]{2,1,0:T(8,128)S(1)} %get-tuple-element.22), channel_id=1, source_target_pairs={{0,1},{1,0},{2,3},{3,2},{4,5},{5,4},{6,7},{7,6},{8,9},{9,8},{10,11... | collective-permute-start | bytes 1290248 | tf_op jit(solution)/shard_map/ppermute | solution.py:563
  22.3 6.4 %collective-permute-start.4 = (f32[2,2,16,1024]{3,2,1,0:T(8,128)S(1)}, f32[2,2,16,1024]{3,2,1,0:T(8,128)S(1)}, u32[]{:S(2)}, u32[]{:S(2)}) collective-permute-start(f32[2,2,16,1024]{3,2,1,0:T(8,128)S(1)} %get-tuple-element.24), channel_id=1, source_target_pairs={{0,16},{1,17},{2,18},{3,19},{4,20},{5,21},{6,22},{7,23},{8,24},{9,... | collective-permute-start | bytes 786440 | tf_op jit(solution)/shard_map/ppermute | solution.py:563

commit v8 on v5

--- a/solution.py
+++ b/solution.py
@@ -302,11 +302,13 @@
             lanes = slice(side * step, side * step + width)
             return lambda level, tile: ref[level, 8 * tile : 8 * tile + 8, lanes]
 
-        def surface(plane, tile):
-            return surf[plane // 2, plane % 2, 8 * tile : 8 * tile + 8, own * step : own * step + width]
+        def surface_reader(side):
+            lanes = slice(side * step, side * step + width)
+            return lambda plane, tile: surf[plane // 2, plane % 2, 8 * tile : 8 * tile + 8, lanes]
 
         @pl.when(depth == own)
         def _():
+            surface, surface_far = surface_reader(own), surface_reader(1 - own)
             slow_near, pert_near = reader(slow, own), reader(pert, own)
             slow_far, pert_far = reader(slow, 1 - own), reader(pert, 1 - own)
             both = [(level, tile) for level in range(2) for tile in range(2)]
@@ -321,9 +323,10 @@
 
                 @pl.when((lax.rem(place, 2) == 1) == down)
                 def _():
-                    edges = edge_surface(surface, down) + edge_levels(own, slow_near, pert_near, down)
+                    edges = edge_surface(surface, down)[:4] + edge_levels(own, slow_near, pert_near, down)
                     pack_rows(cross, edges, own)
-                    pack_rows(cross_far, edge_levels(own, slow_far, pert_far, down), 1 - own)
+                    edges = edge_surface(surface_far, down)[4:] + edge_levels(own, slow_far, pert_far, down)
+                    pack_rows(cross_far, edges, 1 - own)
 
 
 def relay_kernel(window, bulk, chip, partner):
@@ -333,7 +336,7 @@
 
         @pl.when(depth == own)
         def _():
-            other = [unpack_rows(bulk.at[1 - own], 8, n, own) for n in range(8)]
+            other = [unpack_rows(bulk, 8, n, own) for n in range(8)]
             for n in range(8):
                 partner[n] = other[n]
             readers = {
@@ -418,8 +421,9 @@
 
     def fill(own, below_is_chip):
         chip_edges = [unpack_rows(chip, 13, n, own) for n in range(13)]
-        cross_edges = [unpack_rows(cross, 10, n, own) for n in range(10)]
-        cross_edges += [unpack_rows(cross_far, 3, n, own) for n in range(3)]
+        same = [unpack_rows(cross, 7, n, own) for n in range(7)]
+        other = [unpack_rows(cross_far, 6, n, own) for n in range(6)]
+        cross_edges = same[:4] + other[:3] + same[4:] + other[3:]
         above, below = (cross_edges, chip_edges) if below_is_chip else (chip_edges, cross_edges)
         for level in range(2):
             for tile in range(2):
@@ -569,7 +573,7 @@
     params = lambda mib: pltpu.CompilerParams(vmem_limit_bytes=mib * 2**20)
     cross, bulk, cross_far, window = pl.pallas_call(
         lambda *refs: pack_kernel(width, step, *refs),
-        out_shape=(packed(10), packed(8), packed(3), tile(16)),
+        out_shape=(packed(7), packed(8), packed(6), tile(16)),
         in_specs=[pl.BlockSpec(memory_space=pltpu.HBM)] * 3,
         out_specs=(vmem,) * 4,
         scratch_shapes=[
@@ -582,7 +586,7 @@
         name="pack",
     )(*(pltpu.with_memory_space_constraint(x, pltpu.HBM) for x in (surface_data, slowness, perturbation)))
     cross = moved(cross, False, "cross")
-    bulk = lax.all_gather(bulk, "depth")
+    bulk = moved(bulk, True, "same")
     cross_far = moved(cross_far, True, "cross")
     bands, back_bands, freq_tiles = pl.pallas_call(
         lambda *refs: band_kernel(count * ROWS, *refs),

time: 37.5 us -> 29.6 us (0.79)
  blocking collectives: 8.82 us -> 0 us
  waiting for transfers between devices: 11.1 us -> 11.9 us
  local copies, waits for them, and re-layouts: 0.72 us -> 1.15 us
    all_gather x1 -> x0, blocking collectives: 8.82 us -> none  [split_columns(): bulk = lax.all_gather(bulk, 'depth')]
    ppermute x4 -> x5, waiting for transfers between devices: 11.1 us -> 11.9 us  [moved(): return lax.ppermute(value, axes, pairs)]
    unnamed x4, local copies, waits for them, and re-layouts: 0.01 us -> 0.43 us
    ppermute x4 -> x5, starting transfers between devices: 8 us -> 7.69 us  [moved(): return lax.ppermute(value, axes, pairs)]
  transfers between devices with their start and end apart: 4 -> 5, of which waited for: 3 -> 4; matrix products, arithmetic and copies ran while one was open for 0% -> 0% of each run, Pallas kernels for 5% -> 7%
where the time goes in v8:
time: 29.6 us; the launch traced here: 29.4 us
  waiting for transfers between devices  11.9 us (40%)
  Pallas kernels  7.88 us (27%)
  starting transfers between devices  7.69 us (26%)
  local copies, waits for them, and re-layouts  1.15 us (4%)
  between operations  0.69 us (2%)
    ppermute x5, waiting for transfers between devices, moved(): return lax.ppermute(value, axes, pairs)  11.9 us
    ppermute x5, starting transfers between devices, moved(): return lax.ppermute(value, axes, pairs)  7.69 us
    pallas_call x1, Pallas kernels, split_columns(): pl.pallas_call(lambda *refs: sweep_kernel(width, *refs), out_shape=(own,...  4.4 us
    pallas_call x1, Pallas kernels, split_columns(): pl.pallas_call(lambda *refs: band_kernel(count * ROWS, *refs), out_shape=...  1.45 us
    pallas_call x1, Pallas kernels, split_columns(): pl.pallas_call(lambda *refs: pack_kernel(width, step, *refs), out_shape=(...  1.38 us
    dynamic_update_slice x1, local copies, waits for them, and re-layouts, split_columns(): image = lax.dynamic_update_slice(image, theirs[1], (0, 0, start))  0.72 us
  transfers between devices with their start and end apart: 5, of which 4 were waited for; matrix products, arithmetic and copies ran while one was open for 0% of the time, Pallas kernels for 7%

profile of v8, /device:TPU:20, one launch (start us, length us, event | category | flops | bytes accessed | tf_op | source)
XLA Modules:
  0.0 29.4 jit_solution(5121329156942399712)
XLA Ops:
  0.6 1.4 %pack.1 = (f32[57,8,128]{2,1,0:T(8,128)S(1)}, f32[65,8,128]{2,1,0:T(8,128)S(1)}, f32[49,8,128]{2,1,0:T(8,128)S(1)}, f32[16,8,1152]{2,1,0:T(8,128)S(1)}) custom-call(f32[2,2,16,2048]{3,2,1,0:T(8,128)} %refs_0_.3, f32[2,16,2048]{2,1,0:T(8,128)} %refs_1_.3, f32[2,16,2048]{2,1,0:T(8,128)} %refs_2_.1), custom_call_target="tpu_custom_call" | custom-call | tf_op jit(solution)/shard_map/pack/pallas_call | solution.py:574
  2.0 1.6 %collective-permute-start = (f32[65,8,128]{2,1,0:T(8,128)S(1)}, f32[65,8,128]{2,1,0:T(8,128)S(1)}, u32[]{:S(2)}, u32[]{:S(2)}) collective-permute-start(f32[65,8,128]{2,1,0:T(8,128)S(1)} %get-tuple-element.18), channel_id=1, source_target_pairs={{0,16},{1,17},{2,18},{3,19},{4,20},{5,21},{6,22},{7,23},{8,24},{9,... | collective-permute-start | bytes 798728 | tf_op jit(solution)/shard_map/ppermute | solution.py:567
  3.6 1.9 %collective-permute-start.1 = (f32[57,8,128]{2,1,0:T(8,128)S(1)}, f32[57,8,128]{2,1,0:T(8,128)S(1)}, u32[]{:S(2)}, u32[]{:S(2)}) collective-permute-start(f32[57,8,128]{2,1,0:T(8,128)S(1)} %get-tuple-element.20), channel_id=1, source_target_pairs={{1,2},{2,1},{3,4},{4,3},{5,6},{6,5},{7,8},{8,7},{9,10},{10,9},{11,... | collective-permute-start | bytes 700424 | tf_op jit(solution)/shard_map/ppermute | solution.py:567
  5.5 3.6 %collective-permute-start.2 = (f32[49,8,128]{2,1,0:T(8,128)S(1)}, f32[49,8,128]{2,1,0:T(8,128)S(1)}, u32[]{:S(2)}, u32[]{:S(2)}) collective-permute-start(f32[49,8,128]{2,1,0:T(8,128)S(1)} %get-tuple-element.21), channel_id=1, source_target_pairs={{1,18},{2,17},{3,20},{4,19},{5,22},{6,21},{7,24},{8,23},{9,26},{10... | collective-permute-start | bytes 602120 | tf_op jit(solution)/shard_map/ppermute | solution.py:567
  9.1 1.1 %collective-permute-done.bulk = f32[65,8,128]{2,1,0:T(8,128)S(1)} collective-permute-done((f32[65,8,128]{2,1,0:T(8,128)S(1)}, f32[65,8,128]{2,1,0:T(8,128)S(1)}, u32[]{:S(2)}, u32[]{:S(2)}) %collective-permute-start) | collective-permute-done | bytes 266272 | tf_op jit(solution)/shard_map/ppermute | solution.py:567
  10.2 0.0 copy-start
  10.2 0.0 copy-start.1
  10.2 0.2 relay.1
  10.4 0.1 collective-permute-start.3
  10.5 0.4 %copy-done = f32[2,2,15]{2,1,0:T(2,128)S(1)} copy-done((f32[2,2,15]{2,1,0:T(2,128)S(1)}, f32[2,2,15]{2,1,0:T(2,128)}, u32[]{:S(2)}) %copy-start) | copy-done | bytes 264
  10.9 0.0 copy-done.1
  10.9 1.5 %bands.1 = (bf16[2,240,288]{2,1,0:T(8,128)(2,1)S(1)}, bf16[2,144,192]{2,1,0:T(8,128)(2,1)S(1)}, f32[2,8,128]{2,1,0:T(8,128)S(1)}) custom-call(f32[2,2,15]{2,1,0:T(2,128)S(1)} %copy-done, f32[2]{0:T(128)S(1)} %copy-done.1), custom_call_target="tpu_custom_call" | custom-call | flops 10000000000 | bytes 1000000 | tf_op jit(solution)/shard_map/bands/pallas_call | solution.py:591
  12.4 0.5 %own_phases.1.refs_3_ = f32[2,4,2,16,1152]{4,3,2,1,0:T(8,128)S(1)} custom-call(f32[2,8,128]{2,1,0:T(8,128)S(1)} %get-tuple-element.14.freq_tiles.refs_0_, f32[16,8,1152]{2,1,0:T(8,128)S(1)} %get-tuple-element.17.window.refs_4_, f32[8,8,1152]{2,1,0:T(8,128)S(1)} %get-tuple-element.19.partner.refs_5_), custom_call_target="tpu_custom_call" | custom-call | tf_op jit(solution)/shard_map/own_phases/pallas_call | solution.py:615
  12.9 1.4 %collective-permute-done.2.refs_7_ = f32[49,8,128]{2,1,0:T(8,128)S(1)} collective-permute-done((f32[49,8,128]{2,1,0:T(8,128)S(1)}, f32[49,8,128]{2,1,0:T(8,128)S(1)}, u32[]{:S(2)}, u32[]{:S(2)}) %collective-permute-start.2) | collective-permute-done | bytes 200736 | tf_op jit(solution)/shard_map/ppermute | solution.py:567
  14.3 3.5 %collective-permute-done.1.refs_6_ = f32[57,8,128]{2,1,0:T(8,128)S(1)} collective-permute-done((f32[57,8,128]{2,1,0:T(8,128)S(1)}, f32[57,8,128]{2,1,0:T(8,128)S(1)}, u32[]{:S(2)}, u32[]{:S(2)}) %collective-permute-start.1) | collective-permute-done | bytes 233504 | tf_op jit(solution)/shard_map/ppermute | solution.py:567
  17.8 0.0 collective-permute-done.3.refs_8_
  17.8 4.4 %sweep.1 = (f32[2,16,2048]{2,1,0:T(8,128)}, f32[2,16,2048]{2,1,0:T(8,128)}, f32[2,2,16,1024]{3,2,1,0:T(8,128)S(1)}) custom-call(f32[2,8,128]{2,1,0:T(8,128)S(1)} %get-tuple-element.14.freq_tiles.refs_0_, bf16[2,240,288]{2,1,0:T(8,128)(2,1)S(1)} %get-tuple-element.15.refs_1_, bf16[2,144,192]{2,1,0:T(8,128)(2,1)S(1)} %get-tuple-element.16.refs_2_, ...), custom_call_target="tpu_custom_call" | custom-call | tf_op jit(solution)/shard_map/sweep/pallas_call | solution.py:625
  22.2 0.5 %collective-permute-start.4 = (f32[2,2,16,1024]{3,2,1,0:T(8,128)S(1)}, f32[2,2,16,1024]{3,2,1,0:T(8,128)S(1)}, u32[]{:S(2)}, u32[]{:S(2)}) collective-permute-start(f32[2,2,16,1024]{3,2,1,0:T(8,128)S(1)} %get-tuple-element.24), channel_id=1, source_target_pairs={{0,16},{1,17},{2,18},{3,19},{4,20},{5,21},{6,22},{7,23},{8,24},{9,... | collective-permute-start | bytes 786440 | tf_op jit(solution)/shard_map/ppermute | solution.py:567
  22.7 5.9 %collective-permute-done.4 = f32[2,2,16,1024]{3,2,1,0:T(8,128)S(1)} collective-permute-done((f32[2,2,16,1024]{3,2,1,0:T(8,128)S(1)}, f32[2,2,16,1024]{3,2,1,0:T(8,128)S(1)}, u32[]{:S(2)}, u32[]{:S(2)}) %collective-permute-start.4) | collective-permute-done | bytes 262176 | tf_op jit(solution)/shard_map/ppermute | solution.py:567
  28.6 0.7 %fusion = (f32[2,16,2048]{2,1,0:T(8,128)}, f32[2,16,2048]{2,1,0:T(8,128)}) fusion(f32[2,16,2048]{2,1,0:T(8,128)} %get-tuple-element.25, s32[]{:T(128)S(6)} %select_n.4, f32[2,2,16,1024]{3,2,1,0:T(8,128)S(1)} %collective-permute-done.4, f32[2,16,2048]{2,1,0:T(8,128)} %get-tuple-element.23), kind=kLoop, calls=%fused_computation.1 | loop fusion | bytes 524292 | tf_op jit(solution)/shard_map/dynamic_update_slice | solution.py:647
Async XLA Ops:
  2.0 8.2 %collective-permute-start = (f32[65,8,128]{2,1,0:T(8,128)S(1)}, f32[65,8,128]{2,1,0:T(8,128)S(1)}, u32[]{:S(2)}, u32[]{:S(2)}) collective-permute-start(f32[65,8,128]{2,1,0:T(8,128)S(1)} %get-tuple-element.18), channel_id=1, source_target_pairs={{0,16},{1,17},{2,18},{3,19},{4,20},{5,21},{6,22},{7,23},{8,24},{9,... | collective-permute-start | bytes 798728 | tf_op jit(solution)/shard_map/ppermute | solution.py:567
  3.6 14.2 %collective-permute-start.1 = (f32[57,8,128]{2,1,0:T(8,128)S(1)}, f32[57,8,128]{2,1,0:T(8,128)S(1)}, u32[]{:S(2)}, u32[]{:S(2)}) collective-permute-start(f32[57,8,128]{2,1,0:T(8,128)S(1)} %get-tuple-element.20), channel_id=1, source_target_pairs={{1,2},{2,1},{3,4},{4,3},{5,6},{6,5},{7,8},{8,7},{9,10},{10,9},{11,... | collective-permute-start | bytes 700424 | tf_op jit(solution)/shard_map/ppermute | solution.py:567
  5.5 8.8 %collective-permute-start.2 = (f32[49,8,128]{2,1,0:T(8,128)S(1)}, f32[49,8,128]{2,1,0:T(8,128)S(1)}, u32[]{:S(2)}, u32[]{:S(2)}) collective-permute-start(f32[49,8,128]{2,1,0:T(8,128)S(1)} %get-tuple-element.21), channel_id=1, source_target_pairs={{1,18},{2,17},{3,20},{4,19},{5,22},{6,21},{7,24},{8,23},{9,26},{10... | collective-permute-start | bytes 602120 | tf_op jit(solution)/shard_map/ppermute | solution.py:567
  10.2 0.7 %copy-start = (f32[2,2,15]{2,1,0:T(2,128)S(1)}, f32[2,2,15]{2,1,0:T(2,128)}, u32[]{:S(2)}) copy-start(f32[2,2,15]{2,1,0:T(2,128)} %refs_0_.2) | copy-start | bytes 724
  10.2 0.7 %copy-start.1 = (f32[2]{0:T(128)S(1)}, f32[2]{0:T(128)}, u32[]{:S(2)}) copy-start(f32[2]{0:T(128)} %refs_1_.2) | copy-start | bytes 28
  10.4 7.3 %collective-permute-start.3 = (f32[105,8,128]{2,1,0:T(8,128)S(1)}, f32[105,8,128]{2,1,0:T(8,128)S(1)}, u32[]{:S(2)}, u32[]{:S(2)}) collective-permute-start(f32[105,8,128]{2,1,0:T(8,128)S(1)} %get-tuple-element.22), channel_id=1, source_target_pairs={{0,1},{1,0},{2,3},{3,2},{4,5},{5,4},{6,7},{7,6},{8,9},{9,8},{10,11... | collective-permute-start | bytes 1290248 | tf_op jit(solution)/shard_map/ppermute | solution.py:567
  22.2 6.5 %collective-permute-start.4 = (f32[2,2,16,1024]{3,2,1,0:T(8,128)S(1)}, f32[2,2,16,1024]{3,2,1,0:T(8,128)S(1)}, u32[]{:S(2)}, u32[]{:S(2)}) collective-permute-start(f32[2,2,16,1024]{3,2,1,0:T(8,128)S(1)} %get-tuple-element.24), channel_id=1, source_target_pairs={{0,16},{1,17},{2,18},{3,19},{4,20},{5,21},{6,22},{7,23},{8,24},{9,... | collective-permute-start | bytes 786440 | tf_op jit(solution)/shard_map/ppermute | solution.py:567

commit v9 on v5

--- a/solution.py
+++ b/solution.py
@@ -333,7 +333,7 @@
 
         @pl.when(depth == own)
         def _():
-            other = [unpack_rows(bulk.at[1 - own], 8, n, own) for n in range(8)]
+            other = [unpack_rows(bulk, 8, n, own) for n in range(8)]
             for n in range(8):
                 partner[n] = other[n]
             readers = {
@@ -401,19 +401,29 @@
         operand[f, base + 32 : base + 48] = low
 
     def stencil(f, matrix, out_tiles, in_tiles):
+        inner_tiles = min(in_tiles, 5)
         product = jnp.dot(
-            matrix[f, : 48 * out_tiles, : 48 * in_tiles],
-            operand[f, : 48 * in_tiles],
+            matrix[f, : 48 * out_tiles, : 48 * inner_tiles],
+            operand[f, : 48 * inner_tiles],
             preferred_element_type=jnp.float32,
         )
+        slabs = [product[16 * n : 16 * n + 16] for n in range(3 * out_tiles)]
+        if in_tiles > inner_tiles:
+            outer = jnp.dot(
+                matrix[f, 48 * (out_tiles - 1) : 48 * out_tiles, 48 * inner_tiles : 48 * in_tiles],
+                operand[f, 48 * inner_tiles : 48 * in_tiles],
+                preferred_element_type=jnp.float32,
+            )
+            for n in range(3):
+                slabs[3 * out_tiles - 3 + n] += outer[16 * n : 16 * n + 16]
         result = []
         for tile in range(out_tiles):
-            base = 48 * tile
-            left = pltpu.roll(product[base : base + 16], 1, 1)
-            right = pltpu.roll(product[base + 32 : base + 48], width - 1, 1)
+            before, same, after = slabs[3 * tile : 3 * tile + 3]
+            left = pltpu.roll(before, 1, 1)
+            right = pltpu.roll(after, width - 1, 1)
             left = jnp.concatenate([jnp.where(lane == 0, 0.0, left[:, :LANES]), left[:, LANES:]], axis=1)
             right = jnp.concatenate([right[:, :half], jnp.where(lane == LANES - 1, 0.0, right[:, half:])], axis=1)
-            result.append(product[base + 16 : base + 32] + left + right)
+            result.append(same + left + right)
         return result
 
     def fill(own, below_is_chip):
@@ -582,7 +592,7 @@
         name="pack",
     )(*(pltpu.with_memory_space_constraint(x, pltpu.HBM) for x in (surface_data, slowness, perturbation)))
     cross = moved(cross, False, "cross")
-    bulk = lax.all_gather(bulk, "depth")
+    bulk = moved(bulk, True, "same")
     cross_far = moved(cross_far, True, "cross")
     bands, back_bands, freq_tiles = pl.pallas_call(
         lambda *refs: band_kernel(count * ROWS, *refs),

time: 37.5 us -> 29.2 us (0.78)
  blocking collectives: 8.82 us -> 0 us
  waiting for transfers between devices: 11.1 us -> 11.9 us
  local copies, waits for them, and re-layouts: 0.72 us -> 1.15 us
    all_gather x1 -> x0, blocking collectives: 8.82 us -> none  [split_columns(): bulk = lax.all_gather(bulk, 'depth')]
    ppermute x4 -> x5, waiting for transfers between devices: 11.1 us -> 11.9 us  [moved(): return lax.ppermute(value, axes, pairs)]
    unnamed x4, local copies, waits for them, and re-layouts: 0.01 us -> 0.43 us
    ppermute x4 -> x5, starting transfers between devices: 8 us -> 7.68 us  [moved(): return lax.ppermute(value, axes, pairs)]
  transfers between devices with their start and end apart: 4 -> 5, of which waited for: 3 -> 4; matrix products, arithmetic and copies ran while one was open for 0% -> 0% of each run, Pallas kernels for 5% -> 7%
where the time goes in v9:
time: 29.2 us; the launch traced here: 29 us
  waiting for transfers between devices  11.9 us (41%)
  Pallas kernels  7.68 us (26%)
  starting transfers between devices  7.68 us (26%)
  local copies, waits for them, and re-layouts  1.15 us (4%)
  between operations  0.69 us (2%)
    ppermute x5, waiting for transfers between devices, moved(): return lax.ppermute(value, axes, pairs)  11.9 us
    ppermute x5, starting transfers between devices, moved(): return lax.ppermute(value, axes, pairs)  7.68 us
    pallas_call x1, Pallas kernels, split_columns(): pl.pallas_call(lambda *refs: sweep_kernel(width, *refs), out_shape=(own,...  4.2 us
    pallas_call x1, Pallas kernels, split_columns(): pl.pallas_call(lambda *refs: band_kernel(count * ROWS, *refs), out_shape=...  1.45 us
    pallas_call x1, Pallas kernels, split_columns(): pl.pallas_call(lambda *refs: pack_kernel(width, step, *refs), out_shape=(...  1.39 us
    dynamic_update_slice x1, local copies, waits for them, and re-layouts, split_columns(): image = lax.dynamic_update_slice(image, theirs[1], (0, 0, start))  0.72 us
  transfers between devices with their start and end apart: 5, of which 4 were waited for; matrix products, arithmetic and copies ran while one was open for 0% of the time, Pallas kernels for 7%

profile of v9, /device:TPU:20, one launch (start us, length us, event | category | flops | bytes accessed | tf_op | source)
XLA Modules:
  0.0 29.0 jit_solution(2590441160471818546)
XLA Ops:
  0.6 1.4 %pack.1 = (f32[81,8,128]{2,1,0:T(8,128)S(1)}, f32[65,8,128]{2,1,0:T(8,128)S(1)}, f32[25,8,128]{2,1,0:T(8,128)S(1)}, f32[16,8,1152]{2,1,0:T(8,128)S(1)}) custom-call(f32[2,2,16,2048]{3,2,1,0:T(8,128)} %refs_0_.3, f32[2,16,2048]{2,1,0:T(8,128)} %refs_1_.3, f32[2,16,2048]{2,1,0:T(8,128)} %refs_2_.1), custom_call_target="tpu_custom_call" | custom-call | tf_op jit(solution)/shard_map/pack/pallas_call | solution.py:580
  2.0 1.6 %collective-permute-start = (f32[65,8,128]{2,1,0:T(8,128)S(1)}, f32[65,8,128]{2,1,0:T(8,128)S(1)}, u32[]{:S(2)}, u32[]{:S(2)}) collective-permute-start(f32[65,8,128]{2,1,0:T(8,128)S(1)} %get-tuple-element.18), channel_id=1, source_target_pairs={{0,16},{1,17},{2,18},{3,19},{4,20},{5,21},{6,22},{7,23},{8,24},{9,... | collective-permute-start | bytes 798728 | tf_op jit(solution)/shard_map/ppermute | solution.py:573
  3.6 1.9 %collective-permute-start.1 = (f32[81,8,128]{2,1,0:T(8,128)S(1)}, f32[81,8,128]{2,1,0:T(8,128)S(1)}, u32[]{:S(2)}, u32[]{:S(2)}) collective-permute-start(f32[81,8,128]{2,1,0:T(8,128)S(1)} %get-tuple-element.20), channel_id=1, source_target_pairs={{1,2},{2,1},{3,4},{4,3},{5,6},{6,5},{7,8},{8,7},{9,10},{10,9},{11,... | collective-permute-start | bytes 995336 | tf_op jit(solution)/shard_map/ppermute | solution.py:573
  5.5 3.6 %collective-permute-start.2 = (f32[25,8,128]{2,1,0:T(8,128)S(1)}, f32[25,8,128]{2,1,0:T(8,128)S(1)}, u32[]{:S(2)}, u32[]{:S(2)}) collective-permute-start(f32[25,8,128]{2,1,0:T(8,128)S(1)} %get-tuple-element.21), channel_id=1, source_target_pairs={{1,18},{2,17},{3,20},{4,19},{5,22},{6,21},{7,24},{8,23},{9,26},{10... | collective-permute-start | bytes 307208 | tf_op jit(solution)/shard_map/ppermute | solution.py:573
  9.1 1.1 %collective-permute-done.bulk = f32[65,8,128]{2,1,0:T(8,128)S(1)} collective-permute-done((f32[65,8,128]{2,1,0:T(8,128)S(1)}, f32[65,8,128]{2,1,0:T(8,128)S(1)}, u32[]{:S(2)}, u32[]{:S(2)}) %collective-permute-start) | collective-permute-done | bytes 266272 | tf_op jit(solution)/shard_map/ppermute | solution.py:573
  10.2 0.0 copy-start
  10.2 0.0 copy-start.1
  10.2 0.2 relay.1
  10.4 0.1 collective-permute-start.3
  10.5 0.4 %copy-done = f32[2,2,15]{2,1,0:T(2,128)S(1)} copy-done((f32[2,2,15]{2,1,0:T(2,128)S(1)}, f32[2,2,15]{2,1,0:T(2,128)}, u32[]{:S(2)}) %copy-start) | copy-done | bytes 264
  10.9 0.0 copy-done.1
  10.9 1.5 %bands.1 = (bf16[2,240,288]{2,1,0:T(8,128)(2,1)S(1)}, bf16[2,144,192]{2,1,0:T(8,128)(2,1)S(1)}, f32[2,8,128]{2,1,0:T(8,128)S(1)}) custom-call(f32[2,2,15]{2,1,0:T(2,128)S(1)} %copy-done, f32[2]{0:T(128)S(1)} %copy-done.1), custom_call_target="tpu_custom_call" | custom-call | flops 10000000000 | bytes 1000000 | tf_op jit(solution)/shard_map/bands/pallas_call | solution.py:597
  12.4 0.5 %own_phases.1.refs_3_ = f32[2,4,2,16,1152]{4,3,2,1,0:T(8,128)S(1)} custom-call(f32[2,8,128]{2,1,0:T(8,128)S(1)} %get-tuple-element.14.freq_tiles.refs_0_, f32[16,8,1152]{2,1,0:T(8,128)S(1)} %get-tuple-element.17.window.refs_4_, f32[8,8,1152]{2,1,0:T(8,128)S(1)} %get-tuple-element.19.partner.refs_5_), custom_call_target="tpu_custom_call" | custom-call | tf_op jit(solution)/shard_map/own_phases/pallas_call | solution.py:621
  12.9 0.7 %collective-permute-done.2.refs_7_ = f32[25,8,128]{2,1,0:T(8,128)S(1)} collective-permute-done((f32[25,8,128]{2,1,0:T(8,128)S(1)}, f32[25,8,128]{2,1,0:T(8,128)S(1)}, u32[]{:S(2)}, u32[]{:S(2)}) %collective-permute-start.2) | collective-permute-done | bytes 102432 | tf_op jit(solution)/shard_map/ppermute | solution.py:573
  13.5 4.2 %collective-permute-done.1.refs_6_ = f32[81,8,128]{2,1,0:T(8,128)S(1)} collective-permute-done((f32[81,8,128]{2,1,0:T(8,128)S(1)}, f32[81,8,128]{2,1,0:T(8,128)S(1)}, u32[]{:S(2)}, u32[]{:S(2)}) %collective-permute-start.1) | collective-permute-done | bytes 331808 | tf_op jit(solution)/shard_map/ppermute | solution.py:573
  17.8 0.0 collective-permute-done.3.refs_8_
  17.8 4.2 %sweep.1 = (f32[2,16,2048]{2,1,0:T(8,128)}, f32[2,16,2048]{2,1,0:T(8,128)}, f32[2,2,16,1024]{3,2,1,0:T(8,128)S(1)}) custom-call(f32[2,8,128]{2,1,0:T(8,128)S(1)} %get-tuple-element.14.freq_tiles.refs_0_, bf16[2,240,288]{2,1,0:T(8,128)(2,1)S(1)} %get-tuple-element.15.refs_1_, bf16[2,144,192]{2,1,0:T(8,128)(2,1)S(1)} %get-tuple-element.16.refs_2_, ...), custom_call_target="tpu_custom_call" | custom-call | tf_op jit(solution)/shard_map/sweep/pallas_call | solution.py:631
  22.0 0.5 %collective-permute-start.4 = (f32[2,2,16,1024]{3,2,1,0:T(8,128)S(1)}, f32[2,2,16,1024]{3,2,1,0:T(8,128)S(1)}, u32[]{:S(2)}, u32[]{:S(2)}) collective-permute-start(f32[2,2,16,1024]{3,2,1,0:T(8,128)S(1)} %get-tuple-element.24), channel_id=1, source_target_pairs={{0,16},{1,17},{2,18},{3,19},{4,20},{5,21},{6,22},{7,23},{8,24},{9,... | collective-permute-start | bytes 786440 | tf_op jit(solution)/shard_map/ppermute | solution.py:573
  22.5 5.8 %collective-permute-done.4 = f32[2,2,16,1024]{3,2,1,0:T(8,128)S(1)} collective-permute-done((f32[2,2,16,1024]{3,2,1,0:T(8,128)S(1)}, f32[2,2,16,1024]{3,2,1,0:T(8,128)S(1)}, u32[]{:S(2)}, u32[]{:S(2)}) %collective-permute-start.4) | collective-permute-done | bytes 262176 | tf_op jit(solution)/shard_map/ppermute | solution.py:573
  28.3 0.7 %fusion = (f32[2,16,2048]{2,1,0:T(8,128)}, f32[2,16,2048]{2,1,0:T(8,128)}) fusion(f32[2,16,2048]{2,1,0:T(8,128)} %get-tuple-element.25, s32[]{:T(128)S(6)} %select_n.4, f32[2,2,16,1024]{3,2,1,0:T(8,128)S(1)} %collective-permute-done.4, f32[2,16,2048]{2,1,0:T(8,128)} %get-tuple-element.23), kind=kLoop, calls=%fused_computation.1 | loop fusion | bytes 524292 | tf_op jit(solution)/shard_map/dynamic_update_slice | solution.py:653
Async XLA Ops:
  2.0 8.2 %collective-permute-start = (f32[65,8,128]{2,1,0:T(8,128)S(1)}, f32[65,8,128]{2,1,0:T(8,128)S(1)}, u32[]{:S(2)}, u32[]{:S(2)}) collective-permute-start(f32[65,8,128]{2,1,0:T(8,128)S(1)} %get-tuple-element.18), channel_id=1, source_target_pairs={{0,16},{1,17},{2,18},{3,19},{4,20},{5,21},{6,22},{7,23},{8,24},{9,... | collective-permute-start | bytes 798728 | tf_op jit(solution)/shard_map/ppermute | solution.py:573
  3.6 14.2 %collective-permute-start.1 = (f32[81,8,128]{2,1,0:T(8,128)S(1)}, f32[81,8,128]{2,1,0:T(8,128)S(1)}, u32[]{:S(2)}, u32[]{:S(2)}) collective-permute-start(f32[81,8,128]{2,1,0:T(8,128)S(1)} %get-tuple-element.20), channel_id=1, source_target_pairs={{1,2},{2,1},{3,4},{4,3},{5,6},{6,5},{7,8},{8,7},{9,10},{10,9},{11,... | collective-permute-start | bytes 995336 | tf_op jit(solution)/shard_map/ppermute | solution.py:573
  5.5 8.0 %collective-permute-start.2 = (f32[25,8,128]{2,1,0:T(8,128)S(1)}, f32[25,8,128]{2,1,0:T(8,128)S(1)}, u32[]{:S(2)}, u32[]{:S(2)}) collective-permute-start(f32[25,8,128]{2,1,0:T(8,128)S(1)} %get-tuple-element.21), channel_id=1, source_target_pairs={{1,18},{2,17},{3,20},{4,19},{5,22},{6,21},{7,24},{8,23},{9,26},{10... | collective-permute-start | bytes 307208 | tf_op jit(solution)/shard_map/ppermute | solution.py:573
  10.2 0.7 %copy-start = (f32[2,2,15]{2,1,0:T(2,128)S(1)}, f32[2,2,15]{2,1,0:T(2,128)}, u32[]{:S(2)}) copy-start(f32[2,2,15]{2,1,0:T(2,128)} %refs_0_.2) | copy-start | bytes 724
  10.2 0.7 %copy-start.1 = (f32[2]{0:T(128)S(1)}, f32[2]{0:T(128)}, u32[]{:S(2)}) copy-start(f32[2]{0:T(128)} %refs_1_.2) | copy-start | bytes 28
  10.4 7.3 %collective-permute-start.3 = (f32[105,8,128]{2,1,0:T(8,128)S(1)}, f32[105,8,128]{2,1,0:T(8,128)S(1)}, u32[]{:S(2)}, u32[]{:S(2)}) collective-permute-start(f32[105,8,128]{2,1,0:T(8,128)S(1)} %get-tuple-element.22), channel_id=1, source_target_pairs={{0,1},{1,0},{2,3},{3,2},{4,5},{5,4},{6,7},{7,6},{8,9},{9,8},{10,11... | collective-permute-start | bytes 1290248 | tf_op jit(solution)/shard_map/ppermute | solution.py:573
  22.0 6.4 %collective-permute-start.4 = (f32[2,2,16,1024]{3,2,1,0:T(8,128)S(1)}, f32[2,2,16,1024]{3,2,1,0:T(8,128)S(1)}, u32[]{:S(2)}, u32[]{:S(2)}) collective-permute-start(f32[2,2,16,1024]{3,2,1,0:T(8,128)S(1)} %get-tuple-element.24), channel_id=1, source_target_pairs={{0,16},{1,17},{2,18},{3,19},{4,20},{5,21},{6,22},{7,23},{8,24},{9,... | collective-permute-start | bytes 786440 | tf_op jit(solution)/shard_map/ppermute | solution.py:573

commit v10 on v9

--- a/solution.py
+++ b/solution.py
@@ -285,7 +285,7 @@
     return [(tiles[plane], outer[plane]) for plane in range(4)]
 
 
-def pack_kernel(width, step, surf_in, slow_in, pert_in, cross, bulk, cross_far, window, surf, slow, pert, sems):
+def pack_kernel(width, step, surf_in, slow_in, pert_in, cross, chip, bulk, rest, cross_far, window, surf, slow, pert, sems):
     copies = [
         pltpu.make_async_copy(source, target, sems.at[n])
         for n, (source, target) in enumerate(((slow_in, slow), (pert_in, pert), (surf_in, surf)))
@@ -316,7 +316,14 @@
             for plane in range(4):
                 for tile in range(2):
                     window[2 * plane + tile] = surface(plane, tile)
-            pack_rows(bulk, [slow_far(*at) for at in both] + [pert_far(*at) for at in both], 1 - own)
+            slow_tiles = [slow_far(*at) for at in both]
+            pert_tiles = [pert_far(*at) for at in both]
+            if own == 0:
+                pack_rows(bulk, slow_tiles + pert_tiles[2:], 1)
+                pack_rows(rest, pert_tiles[:2], 1)
+            else:
+                pack_rows(bulk, slow_tiles[:2] + pert_tiles, 0)
+                pack_rows(rest, slow_tiles[2:], 0)
             for down in (False, True):
 
                 @pl.when((lax.rem(place, 2) == 1) == down)
@@ -324,30 +331,32 @@
                     edges = edge_surface(surface, down) + edge_levels(own, slow_near, pert_near, down)
                     pack_rows(cross, edges, own)
                     pack_rows(cross_far, edge_levels(own, slow_far, pert_far, down), 1 - own)
-
-
-def relay_kernel(window, bulk, chip, partner):
+                    edges = edge_surface(surface, not down) + edge_levels(own, slow_near, pert_near, not down)
+                    pack_rows(chip, edges, own)
+
+
+def relay_kernel(bulk, chip_far, partner):
     depth = lax.axis_index("depth")
     place = lax.axis_index("xy")
     for own in range(2):
 
         @pl.when(depth == own)
         def _():
-            other = [unpack_rows(bulk, 8, n, own) for n in range(8)]
-            for n in range(8):
+            other = [unpack_rows(bulk, 6, n, own) for n in range(6)]
+            for n in range(6):
                 partner[n] = other[n]
-            readers = {
-                own: (lambda level, tile: window[8 + 2 * level + tile], lambda level, tile: window[12 + 2 * level + tile]),
-                1 - own: (lambda level, tile: other[2 * level + tile], lambda level, tile: other[4 + 2 * level + tile]),
-            }
+
+            def slow(level, tile):
+                return other[2 * level + tile]
+
+            def pert(level, tile):
+                return other[2 + 2 * level + tile]
+
             for down in (False, True):
 
                 @pl.when((lax.rem(place, 2) == 0) == down)
                 def _():
-                    edges = edge_surface(lambda plane, tile: window[2 * plane + tile], down)
-                    for levels in (own, 1 - own):
-                        edges = edges + edge_levels(levels, *readers[levels], down)
-                    pack_rows(chip, edges, own)
+                    pack_rows(chip_far, edge_levels(1 - own, slow, pert, down), own)
 
 
 def phase(half):
@@ -363,16 +372,25 @@
     return 1.0 - twice * sine, twice * cosine
 
 
-def own_phases_kernel(freq_tiles, window, partner, phases):
-    depth = lax.axis_index("depth")
-    for level in range(4):
-        for tile in range(2):
-            own, other = window[8 + 2 * (level % 2) + tile], partner[2 * (level % 2) + tile]
-            slow = jnp.where(depth == level // 2, own, other)
-            for f in range(2):
-                cosine, sine = phase(over_columns(freq_tiles[f], slow) * 0.25 * slow)
-                phases[f, level, tile, :8] = cosine
-                phases[f, level, tile, 8:] = sine
+def own_phases_kernel(freq_tiles, window, partner, rest, phases, pert):
+    for own in range(2):
+
+        @pl.when(lax.axis_index("depth") == own)
+        def _():
+            last = [unpack_rows(rest, 2, tile, own) for tile in range(2)]
+            first = [partner[n] for n in range(6)]
+            slow = first[:2] + last if own == 0 else first[:4]
+            others = first[2:] if own == 0 else last + first[4:]
+            for n in range(4):
+                pert[n] = others[n]
+            for level in range(4):
+                for tile in range(2):
+                    at = 2 * (level % 2) + tile
+                    plane = window[8 + at] if level // 2 == own else slow[at]
+                    for f in range(2):
+                        cosine, sine = phase(over_columns(freq_tiles[f], plane) * 0.25 * plane)
+                        phases[f, level, tile, :8] = cosine
+                        phases[f, level, tile, 8:] = sine
 
 
 def over_columns(tile, like):
@@ -380,7 +398,7 @@
 
 
 def sweep_kernel(
-    width, freq_tiles, bands, back_bands, own_phases, window, partner, cross, cross_far, chip,
+    width, freq_tiles, bands, back_bands, own_phases, window, partner, cross, cross_far, chip, chip_far,
     gradient, image, theirs, slow_win, pert_win, operand, halo_phases, fields, image_win, grad_win,
 ):
     depth = lax.axis_index("depth")
@@ -427,14 +445,15 @@
         return result
 
     def fill(own, below_is_chip):
-        chip_edges = [unpack_rows(chip, 13, n, own) for n in range(13)]
+        chip_edges = [unpack_rows(chip, 10, n, own) for n in range(10)]
+        chip_edges += [unpack_rows(chip_far, 3, n, own) for n in range(3)]
         cross_edges = [unpack_rows(cross, 10, n, own) for n in range(10)]
         cross_edges += [unpack_rows(cross_far, 3, n, own) for n in range(3)]
         above, below = (cross_edges, chip_edges) if below_is_chip else (chip_edges, cross_edges)
         for level in range(2):
             for tile in range(2):
                 pert_win[2 * own + level, tile] = window[12 + 2 * level + tile]
-                pert_win[2 * (1 - own) + level, tile] = partner[4 + 2 * level + tile]
+                pert_win[2 * (1 - own) + level, tile] = partner[2 * level + tile]
         at = (7, 10) if own == 0 else (10, 7)
         up, down = above[at[0] : at[0] + 3], below[at[0] : at[0] + 3]
         for level in range(2):
@@ -577,11 +596,11 @@
     tile = lambda n: jax.ShapeDtypeStruct((n, 8, width), f32)
     packed = lambda n: jax.ShapeDtypeStruct((n * half // LANES + 1, 8, LANES), f32)
     params = lambda mib: pltpu.CompilerParams(vmem_limit_bytes=mib * 2**20)
-    cross, bulk, cross_far, window = pl.pallas_call(
+    cross, chip, bulk, rest, cross_far, window = pl.pallas_call(
         lambda *refs: pack_kernel(width, step, *refs),
-        out_shape=(packed(10), packed(8), packed(3), tile(16)),
+        out_shape=(packed(10), packed(10), packed(6), packed(2), packed(3), tile(16)),
         in_specs=[pl.BlockSpec(memory_space=pltpu.HBM)] * 3,
-        out_specs=(vmem,) * 4,
+        out_specs=(vmem,) * 6,
         scratch_shapes=[
             pltpu.VMEM(surface_data.shape, f32),
             pltpu.VMEM(slowness.shape, f32),
@@ -593,6 +612,7 @@
     )(*(pltpu.with_memory_space_constraint(x, pltpu.HBM) for x in (surface_data, slowness, perturbation)))
     cross = moved(cross, False, "cross")
     bulk = moved(bulk, True, "same")
+    rest = moved(rest, True, "same")
     cross_far = moved(cross_far, True, "cross")
     bands, back_bands, freq_tiles = pl.pallas_call(
         lambda *refs: band_kernel(count * ROWS, *refs),
@@ -604,34 +624,35 @@
         in_specs=[smem] * 2,
         out_specs=(vmem,) * 3,
         compiler_params=params(16),
-        cost_estimate=pl.CostEstimate(flops=10**10, bytes_accessed=10**6, transcendentals=0),
+        cost_estimate=pl.CostEstimate(flops=10**6, bytes_accessed=10**6, transcendentals=0),
         name="bands",
     )(coefficients, frequencies)
-    chip, partner = pl.pallas_call(
+    chip_far, partner = pl.pallas_call(
         relay_kernel,
-        out_shape=(packed(13), tile(8)),
-        in_specs=[vmem] * 2,
+        out_shape=(packed(3), tile(6)),
+        in_specs=[vmem],
         out_specs=(vmem,) * 2,
         compiler_params=params(32),
-        cost_estimate=pl.CostEstimate(flops=10**10, bytes_accessed=10**6, transcendentals=0),
+        cost_estimate=pl.CostEstimate(flops=10**6, bytes_accessed=10**6, transcendentals=0),
         name="relay",
-    )(window, bulk)
+    )(bulk)
     chip = moved(chip, False, "chip")
-
-    own_phases = pl.pallas_call(
+    chip_far = moved(chip_far, False, "chip")
+
+    own_phases, partner = pl.pallas_call(
         own_phases_kernel,
-        out_shape=jax.ShapeDtypeStruct((2, 4, 2, 16, width), f32),
-        in_specs=[vmem] * 3,
-        out_specs=vmem,
+        out_shape=(jax.ShapeDtypeStruct((2, 4, 2, 16, width), f32), tile(4)),
+        in_specs=[vmem] * 4,
+        out_specs=(vmem,) * 2,
         compiler_params=params(16),
         name="own_phases",
-    )(freq_tiles, window, partner)
+    )(freq_tiles, window, partner, rest)
 
     own = jax.ShapeDtypeStruct((2, ROWS, columns), f32)
     gradient, image, theirs = pl.pallas_call(
         lambda *refs: sweep_kernel(width, *refs),
         out_shape=(own, own, jax.ShapeDtypeStruct((2, 2, ROWS, half), f32)),
-        in_specs=[vmem] * 9,
+        in_specs=[vmem] * 10,
         out_specs=(vmem,) * 3,
         scratch_shapes=[
             pltpu.VMEM((3, 3, 8, width), f32),
@@ -645,7 +666,7 @@
         compiler_params=params(40),
         name="sweep",
     )(
-        freq_tiles, bands, back_bands, own_phases, window, partner, cross, cross_far, chip,
+        freq_tiles, bands, back_bands, own_phases, window, partner, cross, cross_far, chip, chip_far,
     )
     theirs = moved(theirs, True, "same")
     start = (1 - lax.axis_index("depth")) * half

time: 29.2 us -> 33.9 us (1.16)
  the two profiles are of different devices: /device:TPU:20 before, /device:TPU:0 now
where the time goes in v10:
time: 33.9 us; the launch traced here: 33.8 us
  waiting for transfers between devices  12.5 us (37%)
  starting transfers between devices  12.1 us (36%)
  Pallas kernels  7.7 us (23%)
  local copies, waits for them, and re-layouts  0.73 us (2%)
  between operations  0.73 us (2%)
    ppermute x7, waiting for transfers between devices, moved(): return lax.ppermute(value, axes, pairs)  12.5 us
    ppermute x7, starting transfers between devices, moved(): return lax.ppermute(value, axes, pairs)  12.1 us
    pallas_call x1, Pallas kernels, split_columns(): pl.pallas_call(lambda *refs: sweep_kernel(width, *refs), out_shape=(own,...  4.21 us
    pallas_call x1, Pallas kernels, split_columns(): pl.pallas_call(lambda *refs: band_kernel(count * ROWS, *refs), out_shape=...  1.45 us
    pallas_call x1, Pallas kernels, split_columns(): pl.pallas_call(lambda *refs: pack_kernel(width, step, *refs), out_shape=(...  1.41 us
    dynamic_update_slice x1, local copies, waits for them, and re-layouts, split_columns(): image = lax.dynamic_update_slice(image, theirs[1], (0, 0, start))  0.72 us
  transfers between devices with their start and end apart: 7, of which 3 were waited for; matrix products, arithmetic and copies ran while one was open for 0% of the time, Pallas kernels for 6%

profile of v10, /device:TPU:0, one launch (start us, length us, event | category | flops | bytes accessed | tf_op | source)
XLA Modules:
  0.0 33.8 jit_solution(9216882919630423794)
XLA Ops:
  0.6 0.0 copy-start.1
  0.6 0.0 copy-start
  0.7 1.4 %pack.1 = (f32[81,8,128]{2,1,0:T(8,128)S(1)}, f32[81,8,128]{2,1,0:T(8,128)S(1)}, f32[49,8,128]{2,1,0:T(8,128)S(1)}, f32[17,8,128]{2,1,0:T(8,128)S(1)}, f32[25,8,...) custom-call(f32[2,2,16,2048]{3,2,1,0:T(8,128)} %refs_0_.3, f32[2,16,2048]{2,1,0:T(8,128)} %refs_1_.3, f32[2,16,2048]{2,1,0:T(8,128)} %refs_2_.1), custom_call_target="tpu_custom_call" | custom-call | tf_op jit(solution)/shard_map/pack/pallas_call | solution.py:599
  2.1 0.7 %collective-permute-start.2 = (f32[81,8,128]{2,1,0:T(8,128)S(1)}, f32[81,8,128]{2,1,0:T(8,128)S(1)}, u32[]{:S(2)}, u32[]{:S(2)}) collective-permute-start(f32[81,8,128]{2,1,0:T(8,128)S(1)} %get-tuple-element.27), channel_id=1, source_target_pairs={{1,2},{2,1},{3,4},{4,3},{5,6},{6,5},{7,8},{8,7},{9,10},{10,9},{11,... | collective-permute-start | bytes 995336 | tf_op jit(solution)/shard_map/ppermute | solution.py:592
  2.8 4.4 %collective-permute-start.4 = (f32[81,8,128]{2,1,0:T(8,128)S(1)}, f32[81,8,128]{2,1,0:T(8,128)S(1)}, u32[]{:S(2)}, u32[]{:S(2)}) collective-permute-start(f32[81,8,128]{2,1,0:T(8,128)S(1)} %get-tuple-element.29), channel_id=1, source_target_pairs={{0,1},{1,0},{2,3},{3,2},{4,5},{5,4},{6,7},{7,6},{8,9},{9,8},{10,11... | collective-permute-start | bytes 995336 | tf_op jit(solution)/shard_map/ppermute | solution.py:592
  7.1 1.5 %collective-permute-start = (f32[49,8,128]{2,1,0:T(8,128)S(1)}, f32[49,8,128]{2,1,0:T(8,128)S(1)}, u32[]{:S(2)}, u32[]{:S(2)}) collective-permute-start(f32[49,8,128]{2,1,0:T(8,128)S(1)} %get-tuple-element.22), channel_id=1, source_target_pairs={{0,16},{1,17},{2,18},{3,19},{4,20},{5,21},{6,22},{7,23},{8,24},{9,... | collective-permute-start | bytes 602120 | tf_op jit(solution)/shard_map/ppermute | solution.py:592
  8.6 0.7 %collective-permute-start.3 = (f32[25,8,128]{2,1,0:T(8,128)S(1)}, f32[25,8,128]{2,1,0:T(8,128)S(1)}, u32[]{:S(2)}, u32[]{:S(2)}) collective-permute-start(f32[25,8,128]{2,1,0:T(8,128)S(1)} %get-tuple-element.28), channel_id=1, source_target_pairs={{1,18},{2,17},{3,20},{4,19},{5,22},{6,21},{7,24},{8,23},{9,26},{10... | collective-permute-start | bytes 307208 | tf_op jit(solution)/shard_map/ppermute | solution.py:592
  9.3 4.8 %collective-permute-done.bulk = f32[49,8,128]{2,1,0:T(8,128)S(1)} collective-permute-done((f32[49,8,128]{2,1,0:T(8,128)S(1)}, f32[49,8,128]{2,1,0:T(8,128)S(1)}, u32[]{:S(2)}, u32[]{:S(2)}) %collective-permute-start) | collective-permute-done | bytes 200736 | tf_op jit(solution)/shard_map/ppermute | solution.py:592
  14.1 0.1 relay.1
  14.3 0.0 collective-permute-start.5
  14.3 3.2 %collective-permute-start.1 = (f32[17,8,128]{2,1,0:T(8,128)S(1)}, f32[17,8,128]{2,1,0:T(8,128)S(1)}, u32[]{:S(2)}, u32[]{:S(2)}) collective-permute-start(f32[17,8,128]{2,1,0:T(8,128)S(1)} %get-tuple-element.24), channel_id=1, source_target_pairs={{0,16},{1,17},{2,18},{3,19},{4,20},{5,21},{6,22},{7,23},{8,24},{9,... | collective-permute-start | bytes 208904 | tf_op jit(solution)/shard_map/ppermute | solution.py:592
  17.5 0.0 copy-done.1
  17.5 0.0 copy-done
  17.5 1.5 %bands.1 = (bf16[2,240,288]{2,1,0:T(8,128)(2,1)S(1)}, bf16[2,144,192]{2,1,0:T(8,128)(2,1)S(1)}, f32[2,8,128]{2,1,0:T(8,128)S(1)}) custom-call(f32[2,2,15]{2,1,0:T(2,128)S(1)} %copy-done, f32[2]{0:T(128)S(1)} %copy-done.1), custom_call_target="tpu_custom_call" | custom-call | flops 1000000 | bytes 1000000 | tf_op jit(solution)/shard_map/bands/pallas_call | solution.py:617
  18.9 1.3 %collective-permute-done.1.rest = f32[17,8,128]{2,1,0:T(8,128)S(1)} collective-permute-done((f32[17,8,128]{2,1,0:T(8,128)S(1)}, f32[17,8,128]{2,1,0:T(8,128)S(1)}, u32[]{:S(2)}, u32[]{:S(2)}) %collective-permute-start.1) | collective-permute-done | bytes 69664 | tf_op jit(solution)/shard_map/ppermute | solution.py:592
  20.2 0.5 %own_phases.1 = (f32[2,4,2,16,1152]{4,3,2,1,0:T(8,128)S(1)}, f32[4,8,1152]{2,1,0:T(8,128)S(1)}) custom-call(f32[2,8,128]{2,1,0:T(8,128)S(1)} %get-tuple-element.18.freq_tiles.refs_0_, f32[16,8,1152]{2,1,0:T(8,128)S(1)} %get-tuple-element.21.window.refs_4_, f32[6,8,1152]{2,1,0:T(8,128)S(1)} %get-tuple-element.23.partner, ...), custom_call_target="tpu_custom_call" | custom-call | tf_op jit(solution)/shard_map/own_phases/pallas_call | solution.py:642
  20.7 0.0 collective-permute-done.3.refs_7_
  20.7 0.0 collective-permute-done.5.refs_9_
  20.7 0.0 collective-permute-done.2.refs_6_
  20.8 0.0 collective-permute-done.4.refs_8_
  20.8 4.2 %sweep.1 = (f32[2,16,2048]{2,1,0:T(8,128)}, f32[2,16,2048]{2,1,0:T(8,128)}, f32[2,2,16,1024]{3,2,1,0:T(8,128)S(1)}) custom-call(f32[2,8,128]{2,1,0:T(8,128)S(1)} %get-tuple-element.18.freq_tiles.refs_0_, bf16[2,240,288]{2,1,0:T(8,128)(2,1)S(1)} %get-tuple-element.19.refs_1_, bf16[2,144,192]{2,1,0:T(8,128)(2,1)S(1)} %get-tuple-element.20.refs_2_, ...), custom_call_target="tpu_custom_call" | custom-call | tf_op jit(solution)/shard_map/sweep/pallas_call | solution.py:652
  25.0 1.8 %collective-permute-start.6 = (f32[2,2,16,1024]{3,2,1,0:T(8,128)S(1)}, f32[2,2,16,1024]{3,2,1,0:T(8,128)S(1)}, u32[]{:S(2)}, u32[]{:S(2)}) collective-permute-start(f32[2,2,16,1024]{3,2,1,0:T(8,128)S(1)} %get-tuple-element.32), channel_id=1, source_target_pairs={{0,16},{1,17},{2,18},{3,19},{4,20},{5,21},{6,22},{7,23},{8,24},{9,... | collective-permute-start | bytes 786440 | tf_op jit(solution)/shard_map/ppermute | solution.py:592
  26.7 6.3 %collective-permute-done.6 = f32[2,2,16,1024]{3,2,1,0:T(8,128)S(1)} collective-permute-done((f32[2,2,16,1024]{3,2,1,0:T(8,128)S(1)}, f32[2,2,16,1024]{3,2,1,0:T(8,128)S(1)}, u32[]{:S(2)}, u32[]{:S(2)}) %collective-permute-start.6) | collective-permute-done | bytes 262176 | tf_op jit(solution)/shard_map/ppermute | solution.py:592
  33.0 0.7 %fusion = (f32[2,16,2048]{2,1,0:T(8,128)}, f32[2,16,2048]{2,1,0:T(8,128)}) fusion(f32[2,16,2048]{2,1,0:T(8,128)} %get-tuple-element.33, s32[]{:T(128)S(6)} %select_n.4, f32[2,2,16,1024]{3,2,1,0:T(8,128)S(1)} %collective-permute-done.6, f32[2,16,2048]{2,1,0:T(8,128)} %get-tuple-element.31), kind=kLoop, calls=%fused_computation.1 | loop fusion | bytes 524292 | tf_op jit(solution)/shard_map/dynamic_update_slice | solution.py:674
Async XLA Ops:
  0.6 16.8 %copy-start.1 = (f32[2]{0:T(128)S(1)}, f32[2]{0:T(128)}, u32[]{:S(2)}) copy-start(f32[2]{0:T(128)} %refs_1_.2) | copy-start | bytes 28
  0.6 16.8 %copy-start = (f32[2,2,15]{2,1,0:T(2,128)S(1)}, f32[2,2,15]{2,1,0:T(2,128)}, u32[]{:S(2)}) copy-start(f32[2,2,15]{2,1,0:T(2,128)} %refs_0_.2) | copy-start | bytes 724
  2.1 18.7 %collective-permute-start.2 = (f32[81,8,128]{2,1,0:T(8,128)S(1)}, f32[81,8,128]{2,1,0:T(8,128)S(1)}, u32[]{:S(2)}, u32[]{:S(2)}) collective-permute-start(f32[81,8,128]{2,1,0:T(8,128)S(1)} %get-tuple-element.27), channel_id=1, source_target_pairs={{1,2},{2,1},{3,4},{4,3},{5,6},{6,5},{7,8},{8,7},{9,10},{10,9},{11,... | collective-permute-start | bytes 995336 | tf_op jit(solution)/shard_map/ppermute | solution.py:592
  2.8 18.0 %collective-permute-start.4 = (f32[81,8,128]{2,1,0:T(8,128)S(1)}, f32[81,8,128]{2,1,0:T(8,128)S(1)}, u32[]{:S(2)}, u32[]{:S(2)}) collective-permute-start(f32[81,8,128]{2,1,0:T(8,128)S(1)} %get-tuple-element.29), channel_id=1, source_target_pairs={{0,1},{1,0},{2,3},{3,2},{4,5},{5,4},{6,7},{7,6},{8,9},{9,8},{10,11... | collective-permute-start | bytes 995336 | tf_op jit(solution)/shard_map/ppermute | solution.py:592
  7.1 7.0 %collective-permute-start = (f32[49,8,128]{2,1,0:T(8,128)S(1)}, f32[49,8,128]{2,1,0:T(8,128)S(1)}, u32[]{:S(2)}, u32[]{:S(2)}) collective-permute-start(f32[49,8,128]{2,1,0:T(8,128)S(1)} %get-tuple-element.22), channel_id=1, source_target_pairs={{0,16},{1,17},{2,18},{3,19},{4,20},{5,21},{6,22},{7,23},{8,24},{9,... | collective-permute-start | bytes 602120 | tf_op jit(solution)/shard_map/ppermute | solution.py:592
  8.6 12.1 %collective-permute-start.3 = (f32[25,8,128]{2,1,0:T(8,128)S(1)}, f32[25,8,128]{2,1,0:T(8,128)S(1)}, u32[]{:S(2)}, u32[]{:S(2)}) collective-permute-start(f32[25,8,128]{2,1,0:T(8,128)S(1)} %get-tuple-element.28), channel_id=1, source_target_pairs={{1,18},{2,17},{3,20},{4,19},{5,22},{6,21},{7,24},{8,23},{9,26},{10... | collective-permute-start | bytes 307208 | tf_op jit(solution)/shard_map/ppermute | solution.py:592
  14.3 6.5 %collective-permute-start.5 = (f32[25,8,128]{2,1,0:T(8,128)S(1)}, f32[25,8,128]{2,1,0:T(8,128)S(1)}, u32[]{:S(2)}, u32[]{:S(2)}) collective-permute-start(f32[25,8,128]{2,1,0:T(8,128)S(1)} %get-tuple-element.30), channel_id=1, source_target_pairs={{0,1},{1,0},{2,3},{3,2},{4,5},{5,4},{6,7},{7,6},{8,9},{9,8},{10,11... | collective-permute-start | bytes 307208 | tf_op jit(solution)/shard_map/ppermute | solution.py:592
  14.3 6.0 %collective-permute-start.1 = (f32[17,8,128]{2,1,0:T(8,128)S(1)}, f32[17,8,128]{2,1,0:T(8,128)S(1)}, u32[]{:S(2)}, u32[]{:S(2)}) collective-permute-start(f32[17,8,128]{2,1,0:T(8,128)S(1)} %get-tuple-element.24), channel_id=1, source_target_pairs={{0,16},{1,17},{2,18},{3,19},{4,20},{5,21},{6,22},{7,23},{8,24},{9,... | collective-permute-start | bytes 208904 | tf_op jit(solution)/shard_map/ppermute | solution.py:592
  25.0 8.1 %collective-permute-start.6 = (f32[2,2,16,1024]{3,2,1,0:T(8,128)S(1)}, f32[2,2,16,1024]{3,2,1,0:T(8,128)S(1)}, u32[]{:S(2)}, u32[]{:S(2)}) collective-permute-start(f32[2,2,16,1024]{3,2,1,0:T(8,128)S(1)} %get-tuple-element.32), channel_id=1, source_target_pairs={{0,16},{1,17},{2,18},{3,19},{4,20},{5,21},{6,22},{7,23},{8,24},{9,... | collective-permute-start | bytes 786440 | tf_op jit(solution)/shard_map/ppermute | solution.py:592

commit v11 on v9

--- a/solution.py
+++ b/solution.py
@@ -285,7 +285,7 @@
     return [(tiles[plane], outer[plane]) for plane in range(4)]
 
 
-def pack_kernel(width, step, surf_in, slow_in, pert_in, cross, bulk, cross_far, window, surf, slow, pert, sems):
+def pack_kernel(width, step, surf_in, slow_in, pert_in, cross, chip, bulk, rest, cross_far, window, surf, slow, pert, sems):
     copies = [
         pltpu.make_async_copy(source, target, sems.at[n])
         for n, (source, target) in enumerate(((slow_in, slow), (pert_in, pert), (surf_in, surf)))
@@ -316,7 +316,14 @@
             for plane in range(4):
                 for tile in range(2):
                     window[2 * plane + tile] = surface(plane, tile)
-            pack_rows(bulk, [slow_far(*at) for at in both] + [pert_far(*at) for at in both], 1 - own)
+            slow_tiles = [slow_far(*at) for at in both]
+            pert_tiles = [pert_far(*at) for at in both]
+            if own == 0:
+                pack_rows(bulk, slow_tiles + pert_tiles[2:], 1)
+                pack_rows(rest, pert_tiles[:2], 1)
+            else:
+                pack_rows(bulk, slow_tiles[:2] + pert_tiles, 0)
+                pack_rows(rest, slow_tiles[2:], 0)
             for down in (False, True):
 
                 @pl.when((lax.rem(place, 2) == 1) == down)
@@ -324,30 +331,33 @@
                     edges = edge_surface(surface, down) + edge_levels(own, slow_near, pert_near, down)
                     pack_rows(cross, edges, own)
                     pack_rows(cross_far, edge_levels(own, slow_far, pert_far, down), 1 - own)
-
-
-def relay_kernel(window, bulk, chip, partner):
+                    edges = edge_surface(surface, not down) + edge_levels(own, slow_near, pert_near, not down)
+                    pack_rows(chip, edges, own)
+
+
+def relay_kernel(bulk, rest, order, chip_far, partner):
     depth = lax.axis_index("depth")
     place = lax.axis_index("xy")
     for own in range(2):
 
         @pl.when(depth == own)
         def _():
-            other = [unpack_rows(bulk, 8, n, own) for n in range(8)]
+            other = [unpack_rows(bulk, 6, n, own) for n in range(6)]
+            last = [unpack_rows(rest, 2, n, own) for n in range(2)]
+            other = other[:2] + last + other[2:] if own == 0 else other[:4] + last + other[4:]
             for n in range(8):
                 partner[n] = other[n]
-            readers = {
-                own: (lambda level, tile: window[8 + 2 * level + tile], lambda level, tile: window[12 + 2 * level + tile]),
-                1 - own: (lambda level, tile: other[2 * level + tile], lambda level, tile: other[4 + 2 * level + tile]),
-            }
             for down in (False, True):
 
                 @pl.when((lax.rem(place, 2) == 0) == down)
                 def _():
-                    edges = edge_surface(lambda plane, tile: window[2 * plane + tile], down)
-                    for levels in (own, 1 - own):
-                        edges = edges + edge_levels(levels, *readers[levels], down)
-                    pack_rows(chip, edges, own)
+                    edges = edge_levels(
+                        1 - own,
+                        lambda level, tile: other[2 * level + tile],
+                        lambda level, tile: other[4 + 2 * level + tile],
+                        down,
+                    )
+                    pack_rows(chip_far, edges, own)
 
 
 def phase(half):
@@ -380,7 +390,7 @@
 
 
 def sweep_kernel(
-    width, freq_tiles, bands, back_bands, own_phases, window, partner, cross, cross_far, chip,
+    width, freq_tiles, bands, back_bands, own_phases, window, partner, cross, cross_far, chip, chip_far,
     gradient, image, theirs, slow_win, pert_win, operand, halo_phases, fields, image_win, grad_win,
 ):
     depth = lax.axis_index("depth")
@@ -427,7 +437,8 @@
         return result
 
     def fill(own, below_is_chip):
-        chip_edges = [unpack_rows(chip, 13, n, own) for n in range(13)]
+        chip_edges = [unpack_rows(chip, 10, n, own) for n in range(10)]
+        chip_edges += [unpack_rows(chip_far, 3, n, own) for n in range(3)]
         cross_edges = [unpack_rows(cross, 10, n, own) for n in range(10)]
         cross_edges += [unpack_rows(cross_far, 3, n, own) for n in range(3)]
         above, below = (cross_edges, chip_edges) if below_is_chip else (chip_edges, cross_edges)
@@ -577,11 +588,11 @@
     tile = lambda n: jax.ShapeDtypeStruct((n, 8, width), f32)
     packed = lambda n: jax.ShapeDtypeStruct((n * half // LANES + 1, 8, LANES), f32)
     params = lambda mib: pltpu.CompilerParams(vmem_limit_bytes=mib * 2**20)
-    cross, bulk, cross_far, window = pl.pallas_call(
+    cross, chip, bulk, rest, cross_far, window = pl.pallas_call(
         lambda *refs: pack_kernel(width, step, *refs),
-        out_shape=(packed(10), packed(8), packed(3), tile(16)),
+        out_shape=(packed(10), packed(10), packed(6), packed(2), packed(3), tile(16)),
         in_specs=[pl.BlockSpec(memory_space=pltpu.HBM)] * 3,
-        out_specs=(vmem,) * 4,
+        out_specs=(vmem,) * 6,
         scratch_shapes=[
             pltpu.VMEM(surface_data.shape, f32),
             pltpu.VMEM(slowness.shape, f32),
@@ -593,6 +604,7 @@
     )(*(pltpu.with_memory_space_constraint(x, pltpu.HBM) for x in (surface_data, slowness, perturbation)))
     cross = moved(cross, False, "cross")
     bulk = moved(bulk, True, "same")
+    rest = moved(rest, True, "same")
     cross_far = moved(cross_far, True, "cross")
     bands, back_bands, freq_tiles = pl.pallas_call(
         lambda *refs: band_kernel(count * ROWS, *refs),
@@ -604,19 +616,20 @@
         in_specs=[smem] * 2,
         out_specs=(vmem,) * 3,
         compiler_params=params(16),
-        cost_estimate=pl.CostEstimate(flops=10**10, bytes_accessed=10**6, transcendentals=0),
+        cost_estimate=pl.CostEstimate(flops=10**6, bytes_accessed=10**6, transcendentals=0),
         name="bands",
     )(coefficients, frequencies)
-    chip, partner = pl.pallas_call(
+    chip_far, partner = pl.pallas_call(
         relay_kernel,
-        out_shape=(packed(13), tile(8)),
-        in_specs=[vmem] * 2,
+        out_shape=(packed(3), tile(8)),
+        in_specs=[vmem] * 3,
         out_specs=(vmem,) * 2,
         compiler_params=params(32),
-        cost_estimate=pl.CostEstimate(flops=10**10, bytes_accessed=10**6, transcendentals=0),
+        cost_estimate=pl.CostEstimate(flops=10**6, bytes_accessed=10**6, transcendentals=0),
         name="relay",
-    )(window, bulk)
+    )(bulk, rest, freq_tiles)
     chip = moved(chip, False, "chip")
+    chip_far = moved(chip_far, False, "chip")
 
     own_phases = pl.pallas_call(
         own_phases_kernel,
@@ -631,7 +644,7 @@
     gradient, image, theirs = pl.pallas_call(
         lambda *refs: sweep_kernel(width, *refs),
         out_shape=(own, own, jax.ShapeDtypeStruct((2, 2, ROWS, half), f32)),
-        in_specs=[vmem] * 9,
+        in_specs=[vmem] * 10,
         out_specs=(vmem,) * 3,
         scratch_shapes=[
             pltpu.VMEM((3, 3, 8, width), f32),
@@ -645,7 +658,7 @@
         compiler_params=params(40),
         name="sweep",
     )(
-        freq_tiles, bands, back_bands, own_phases, window, partner, cross, cross_far, chip,
+        freq_tiles, bands, back_bands, own_phases, window, partner, cross, cross_far, chip, chip_far,
     )
     theirs = moved(theirs, True, "same")
     start = (1 - lax.axis_index("depth")) * half

time: 29.2 us -> 32.2 us (1.10)
  the two profiles are of different devices: /device:TPU:20 before, /device:TPU:0 now
where the time goes in v11:
time: 32.2 us; the launch traced here: 32 us
  waiting for transfers between devices  12.3 us (38%)
  starting transfers between devices  9.24 us (29%)
  Pallas kernels  7.67 us (24%)
  local copies, waits for them, and re-layouts  2.05 us (6%)
  between operations  0.7 us (2%)
    ppermute x7, waiting for transfers between devices, moved(): return lax.ppermute(value, axes, pairs)  12.3 us
    ppermute x7, starting transfers between devices, moved(): return lax.ppermute(value, axes, pairs)  9.24 us
    pallas_call x1, Pallas kernels, split_columns(): pl.pallas_call(lambda *refs: sweep_kernel(width, *refs), out_shape=(own,...  4.2 us
    pallas_call x1, Pallas kernels, split_columns(): pl.pallas_call(lambda *refs: band_kernel(count * ROWS, *refs), out_shape=...  1.45 us
    pallas_call x1, Pallas kernels, split_columns(): pl.pallas_call(lambda *refs: pack_kernel(width, step, *refs), out_shape=(...  1.4 us
    unnamed x4, local copies, waits for them, and re-layouts  1.33 us
    dynamic_update_slice x1, local copies, waits for them, and re-layouts, split_columns(): image = lax.dynamic_update_slice(image, theirs[1], (0, 0, start))  0.72 us
  transfers between devices with their start and end apart: 7, of which 3 were waited for; matrix products, arithmetic and copies ran while one was open for 0% of the time, Pallas kernels for 6%

profile of v11, /device:TPU:0, one launch (start us, length us, event | category | flops | bytes accessed | tf_op | source)
XLA Modules:
  0.0 32.0 jit_solution(11445495604380994636)
XLA Ops:
  0.6 1.4 %pack.1 = (f32[81,8,128]{2,1,0:T(8,128)S(1)}, f32[81,8,128]{2,1,0:T(8,128)S(1)}, f32[49,8,128]{2,1,0:T(8,128)S(1)}, f32[17,8,128]{2,1,0:T(8,128)S(1)}, f32[25,8,...) custom-call(f32[2,2,16,2048]{3,2,1,0:T(8,128)} %refs_0_.3, f32[2,16,2048]{2,1,0:T(8,128)} %refs_1_.3, f32[2,16,2048]{2,1,0:T(8,128)} %refs_2_.1), custom_call_target="tpu_custom_call" | custom-call | tf_op jit(solution)/shard_map/pack/pallas_call | solution.py:591
  2.0 0.7 %collective-permute-start.2 = (f32[81,8,128]{2,1,0:T(8,128)S(1)}, f32[81,8,128]{2,1,0:T(8,128)S(1)}, u32[]{:S(2)}, u32[]{:S(2)}) collective-permute-start(f32[81,8,128]{2,1,0:T(8,128)S(1)} %get-tuple-element.23), channel_id=1, source_target_pairs={{1,2},{2,1},{3,4},{4,3},{5,6},{6,5},{7,8},{8,7},{9,10},{10,9},{11,... | collective-permute-start | bytes 995336 | tf_op jit(solution)/shard_map/ppermute | solution.py:584
  2.7 4.4 %collective-permute-start.4 = (f32[81,8,128]{2,1,0:T(8,128)S(1)}, f32[81,8,128]{2,1,0:T(8,128)S(1)}, u32[]{:S(2)}, u32[]{:S(2)}) collective-permute-start(f32[81,8,128]{2,1,0:T(8,128)S(1)} %get-tuple-element.25), channel_id=1, source_target_pairs={{0,1},{1,0},{2,3},{3,2},{4,5},{5,4},{6,7},{7,6},{8,9},{9,8},{10,11... | collective-permute-start | bytes 995336 | tf_op jit(solution)/shard_map/ppermute | solution.py:584
  7.1 1.5 %collective-permute-start = (f32[49,8,128]{2,1,0:T(8,128)S(1)}, f32[49,8,128]{2,1,0:T(8,128)S(1)}, u32[]{:S(2)}, u32[]{:S(2)}) collective-permute-start(f32[49,8,128]{2,1,0:T(8,128)S(1)} %get-tuple-element.20), channel_id=1, source_target_pairs={{0,16},{1,17},{2,18},{3,19},{4,20},{5,21},{6,22},{7,23},{8,24},{9,... | collective-permute-start | bytes 602120 | tf_op jit(solution)/shard_map/ppermute | solution.py:584
  8.6 0.5 %collective-permute-start.1 = (f32[17,8,128]{2,1,0:T(8,128)S(1)}, f32[17,8,128]{2,1,0:T(8,128)S(1)}, u32[]{:S(2)}, u32[]{:S(2)}) collective-permute-start(f32[17,8,128]{2,1,0:T(8,128)S(1)} %get-tuple-element.21), channel_id=1, source_target_pairs={{0,16},{1,17},{2,18},{3,19},{4,20},{5,21},{6,22},{7,23},{8,24},{9,... | collective-permute-start | bytes 208904 | tf_op jit(solution)/shard_map/ppermute | solution.py:584
  9.1 0.7 %collective-permute-start.3 = (f32[25,8,128]{2,1,0:T(8,128)S(1)}, f32[25,8,128]{2,1,0:T(8,128)S(1)}, u32[]{:S(2)}, u32[]{:S(2)}) collective-permute-start(f32[25,8,128]{2,1,0:T(8,128)S(1)} %get-tuple-element.24), channel_id=1, source_target_pairs={{1,18},{2,17},{3,20},{4,19},{5,22},{6,21},{7,24},{8,23},{9,26},{10... | collective-permute-start | bytes 307208 | tf_op jit(solution)/shard_map/ppermute | solution.py:584
  9.8 0.0 copy-start
  9.8 0.7 %copy-done = f32[2,2,15]{2,1,0:T(2,128)S(1)} copy-done((f32[2,2,15]{2,1,0:T(2,128)S(1)}, f32[2,2,15]{2,1,0:T(2,128)}, u32[]{:S(2)}) %copy-start) | copy-done | bytes 264
  10.5 0.0 copy-start.1
  10.5 0.7 %copy-done.1 = f32[2]{0:T(128)S(1)} copy-done((f32[2]{0:T(128)S(1)}, f32[2]{0:T(128)}, u32[]{:S(2)}) %copy-start.1) | copy-done | bytes 32
  11.1 1.5 %bands.1 = (bf16[2,240,288]{2,1,0:T(8,128)(2,1)S(1)}, bf16[2,144,192]{2,1,0:T(8,128)(2,1)S(1)}, f32[2,8,128]{2,1,0:T(8,128)S(1)}) custom-call(f32[2,2,15]{2,1,0:T(2,128)S(1)} %copy-done, f32[2]{0:T(128)S(1)} %copy-done.1), custom_call_target="tpu_custom_call" | custom-call | flops 1000000 | bytes 1000000 | tf_op jit(solution)/shard_map/bands/pallas_call | solution.py:609
  12.6 4.6 %collective-permute-done.1.rest = f32[17,8,128]{2,1,0:T(8,128)S(1)} collective-permute-done((f32[17,8,128]{2,1,0:T(8,128)S(1)}, f32[17,8,128]{2,1,0:T(8,128)S(1)}, u32[]{:S(2)}, u32[]{:S(2)}) %collective-permute-start.1) | collective-permute-done | bytes 69664 | tf_op jit(solution)/shard_map/ppermute | solution.py:584
  17.2 0.0 collective-permute-done.bulk
  17.2 0.1 relay.1
  17.4 0.0 collective-permute-start.5
  17.4 0.5 %own_phases.1.refs_3_ = f32[2,4,2,16,1152]{4,3,2,1,0:T(8,128)S(1)} custom-call(f32[2,8,128]{2,1,0:T(8,128)S(1)} %get-tuple-element.16.order.freq_tiles.refs_0_, f32[16,8,1152]{2,1,0:T(8,128)S(1)} %get-tuple-element.19.window.refs_4_, f32[8,8,1152]{2,1,0:T(8,128)S(1)} %get-tuple-element.22.partner.refs_5_), custom_call_target="tpu_custom_call" | custom-call | tf_op jit(solution)/shard_map/own_phases/pallas_call | solution.py:634
  17.9 0.0 collective-permute-done.3.refs_7_
  17.9 0.8 %collective-permute-done.5.refs_9_ = f32[25,8,128]{2,1,0:T(8,128)S(1)} collective-permute-done((f32[25,8,128]{2,1,0:T(8,128)S(1)}, f32[25,8,128]{2,1,0:T(8,128)S(1)}, u32[]{:S(2)}, u32[]{:S(2)}) %collective-permute-start.5) | collective-permute-done | bytes 102432 | tf_op jit(solution)/shard_map/ppermute | solution.py:584
  18.7 0.0 collective-permute-done.2.refs_6_
  18.7 0.0 collective-permute-done.4.refs_8_
  18.7 4.2 %sweep.1 = (f32[2,16,2048]{2,1,0:T(8,128)}, f32[2,16,2048]{2,1,0:T(8,128)}, f32[2,2,16,1024]{3,2,1,0:T(8,128)S(1)}) custom-call(f32[2,8,128]{2,1,0:T(8,128)S(1)} %get-tuple-element.16.order.freq_tiles.refs_0_, bf16[2,240,288]{2,1,0:T(8,128)(2,1)S(1)} %get-tuple-element.17.refs_1_, bf16[2,144,192]{2,1,0:T(8,128)(2,1)S(1)} %get-tuple-element.18.refs_2_, ...), custom_call_target="tpu_custom_call" | custom-call | tf_op jit(solution)/shard_map/sweep/pallas_call | solution.py:644
  22.9 1.5 %collective-permute-start.6 = (f32[2,2,16,1024]{3,2,1,0:T(8,128)S(1)}, f32[2,2,16,1024]{3,2,1,0:T(8,128)S(1)}, u32[]{:S(2)}, u32[]{:S(2)}) collective-permute-start(f32[2,2,16,1024]{3,2,1,0:T(8,128)S(1)} %get-tuple-element.28), channel_id=1, source_target_pairs={{0,16},{1,17},{2,18},{3,19},{4,20},{5,21},{6,22},{7,23},{8,24},{9,... | collective-permute-start | bytes 786440 | tf_op jit(solution)/shard_map/ppermute | solution.py:584
  24.4 6.9 %collective-permute-done.6 = f32[2,2,16,1024]{3,2,1,0:T(8,128)S(1)} collective-permute-done((f32[2,2,16,1024]{3,2,1,0:T(8,128)S(1)}, f32[2,2,16,1024]{3,2,1,0:T(8,128)S(1)}, u32[]{:S(2)}, u32[]{:S(2)}) %collective-permute-start.6) | collective-permute-done | bytes 262176 | tf_op jit(solution)/shard_map/ppermute | solution.py:584
  31.2 0.7 %fusion = (f32[2,16,2048]{2,1,0:T(8,128)}, f32[2,16,2048]{2,1,0:T(8,128)}) fusion(f32[2,16,2048]{2,1,0:T(8,128)} %get-tuple-element.29, s32[]{:T(128)S(6)} %select_n.4, f32[2,2,16,1024]{3,2,1,0:T(8,128)S(1)} %collective-permute-done.6, f32[2,16,2048]{2,1,0:T(8,128)} %get-tuple-element.27), kind=kLoop, calls=%fused_computation.1 | loop fusion | bytes 524292 | tf_op jit(solution)/shard_map/dynamic_update_slice | solution.py:666
Async XLA Ops:
  2.0 16.6 %collective-permute-start.2 = (f32[81,8,128]{2,1,0:T(8,128)S(1)}, f32[81,8,128]{2,1,0:T(8,128)S(1)}, u32[]{:S(2)}, u32[]{:S(2)}) collective-permute-start(f32[81,8,128]{2,1,0:T(8,128)S(1)} %get-tuple-element.23), channel_id=1, source_target_pairs={{1,2},{2,1},{3,4},{4,3},{5,6},{6,5},{7,8},{8,7},{9,10},{10,9},{11,... | collective-permute-start | bytes 995336 | tf_op jit(solution)/shard_map/ppermute | solution.py:584
  2.7 16.0 %collective-permute-start.4 = (f32[81,8,128]{2,1,0:T(8,128)S(1)}, f32[81,8,128]{2,1,0:T(8,128)S(1)}, u32[]{:S(2)}, u32[]{:S(2)}) collective-permute-start(f32[81,8,128]{2,1,0:T(8,128)S(1)} %get-tuple-element.25), channel_id=1, source_target_pairs={{0,1},{1,0},{2,3},{3,2},{4,5},{5,4},{6,7},{7,6},{8,9},{9,8},{10,11... | collective-permute-start | bytes 995336 | tf_op jit(solution)/shard_map/ppermute | solution.py:584
  7.1 10.1 %collective-permute-start = (f32[49,8,128]{2,1,0:T(8,128)S(1)}, f32[49,8,128]{2,1,0:T(8,128)S(1)}, u32[]{:S(2)}, u32[]{:S(2)}) collective-permute-start(f32[49,8,128]{2,1,0:T(8,128)S(1)} %get-tuple-element.20), channel_id=1, source_target_pairs={{0,16},{1,17},{2,18},{3,19},{4,20},{5,21},{6,22},{7,23},{8,24},{9,... | collective-permute-start | bytes 602120 | tf_op jit(solution)/shard_map/ppermute | solution.py:584
  8.6 8.6 %collective-permute-start.1 = (f32[17,8,128]{2,1,0:T(8,128)S(1)}, f32[17,8,128]{2,1,0:T(8,128)S(1)}, u32[]{:S(2)}, u32[]{:S(2)}) collective-permute-start(f32[17,8,128]{2,1,0:T(8,128)S(1)} %get-tuple-element.21), channel_id=1, source_target_pairs={{0,16},{1,17},{2,18},{3,19},{4,20},{5,21},{6,22},{7,23},{8,24},{9,... | collective-permute-start | bytes 208904 | tf_op jit(solution)/shard_map/ppermute | solution.py:584
  9.1 8.7 %collective-permute-start.3 = (f32[25,8,128]{2,1,0:T(8,128)S(1)}, f32[25,8,128]{2,1,0:T(8,128)S(1)}, u32[]{:S(2)}, u32[]{:S(2)}) collective-permute-start(f32[25,8,128]{2,1,0:T(8,128)S(1)} %get-tuple-element.24), channel_id=1, source_target_pairs={{1,18},{2,17},{3,20},{4,19},{5,22},{6,21},{7,24},{8,23},{9,26},{10... | collective-permute-start | bytes 307208 | tf_op jit(solution)/shard_map/ppermute | solution.py:584
  9.8 0.7 %copy-start = (f32[2,2,15]{2,1,0:T(2,128)S(1)}, f32[2,2,15]{2,1,0:T(2,128)}, u32[]{:S(2)}) copy-start(f32[2,2,15]{2,1,0:T(2,128)} %refs_0_.2) | copy-start | bytes 724
  10.5 0.7 %copy-start.1 = (f32[2]{0:T(128)S(1)}, f32[2]{0:T(128)}, u32[]{:S(2)}) copy-start(f32[2]{0:T(128)} %refs_1_.2) | copy-start | bytes 28
  17.4 1.3 %collective-permute-start.5 = (f32[25,8,128]{2,1,0:T(8,128)S(1)}, f32[25,8,128]{2,1,0:T(8,128)S(1)}, u32[]{:S(2)}, u32[]{:S(2)}) collective-permute-start(f32[25,8,128]{2,1,0:T(8,128)S(1)} %get-tuple-element.26), channel_id=1, source_target_pairs={{0,1},{1,0},{2,3},{3,2},{4,5},{5,4},{6,7},{7,6},{8,9},{9,8},{10,11... | collective-permute-start | bytes 307208 | tf_op jit(solution)/shard_map/ppermute | solution.py:584
  22.9 8.4 %collective-permute-start.6 = (f32[2,2,16,1024]{3,2,1,0:T(8,128)S(1)}, f32[2,2,16,1024]{3,2,1,0:T(8,128)S(1)}, u32[]{:S(2)}, u32[]{:S(2)}) collective-permute-start(f32[2,2,16,1024]{3,2,1,0:T(8,128)S(1)} %get-tuple-element.28), channel_id=1, source_target_pairs={{0,16},{1,17},{2,18},{3,19},{4,20},{5,21},{6,22},{7,23},{8,24},{9,... | collective-permute-start | bytes 786440 | tf_op jit(solution)/shard_map/ppermute | solution.py:584

commit v12 on v9

--- a/solution.py
+++ b/solution.py
@@ -400,7 +400,7 @@
         operand[f, base + 16 : base + 32] = high
         operand[f, base + 32 : base + 48] = low
 
-    def stencil(f, matrix, out_tiles, in_tiles):
+    def multiply(f, matrix, out_tiles, in_tiles):
         inner_tiles = min(in_tiles, 5)
         product = jnp.dot(
             matrix[f, : 48 * out_tiles, : 48 * inner_tiles],
@@ -416,8 +416,11 @@
             )
             for n in range(3):
                 slabs[3 * out_tiles - 3 + n] += outer[16 * n : 16 * n + 16]
+        return slabs
+
+    def combine(slabs):
         result = []
-        for tile in range(out_tiles):
+        for tile in range(len(slabs) // 3):
             before, same, after = slabs[3 * tile : 3 * tile + 3]
             left = pltpu.roll(before, 1, 1)
             right = pltpu.roll(after, width - 1, 1)
@@ -494,11 +497,9 @@
             halo_phases[f, level - 1, 8:] = sine
         return cosine, sine
 
-    tiles = (6, 5, 5, 4)
-    for level in range(3):
-        for f in range(2):
-            fields_now = stencil(f, bands, tiles[level + 1], tiles[level])
-            for tile, value in enumerate(fields_now):
+    def step_forward(level):
+        def finish(f, values):
+            for tile, value in enumerate(values):
                 cosine, sine = phases_of(f, level, tile)
                 v_re, v_im = value[:8], value[8:]
                 re = cosine * v_re - sine * v_im
@@ -509,8 +510,11 @@
                     fields[f, level, tile] = both
                 if tile < 2:
                     add_image(f, level, tile, re, im)
-    for f in range(2):
-        for tile, value in enumerate(stencil(f, bands, 4, 4)):
+
+        return finish
+
+    def turn(f, values):
+        for tile, value in enumerate(values):
             twice = 2.0 * pert_win[3, tile]
             v_re, v_im = value[:8], value[8:]
             if tile < 2:
@@ -520,10 +524,10 @@
                 add_image(f, 3, tile, re, im)
                 add_gradient(f, 3, tile, twice * re, twice * im, re, im)
             store_operand(f, tile, jnp.concatenate([twice * v_re, twice * v_im], axis=0))
-    tiles = (2, 3, 3, 4)
-    for level in (2, 1, 0):
-        for f in range(2):
-            for tile, value in enumerate(stencil(f, back_bands, tiles[level], tiles[level + 1])):
+
+    def step_back(level):
+        def finish(f, values):
+            for tile, value in enumerate(values):
                 twice = 2.0 * pert_win[level, tile]
                 u_re, u_im = fields[f, level, tile, :8], fields[f, level, tile, 8:]
                 w_re = value[:8] + twice * u_re
@@ -537,6 +541,24 @@
                         cosine, sine = halo_phases[f, level - 1, :8], halo_phases[f, level - 1, 8:]
                     back = [cosine * w_re + sine * w_im, cosine * w_im - sine * w_re]
                     store_operand(f, tile, jnp.concatenate(back, axis=0))
+
+        return finish
+
+    steps = [
+        (bands, 5, 6, step_forward(0)),
+        (bands, 5, 5, step_forward(1)),
+        (bands, 4, 5, step_forward(2)),
+        (bands, 4, 4, turn),
+        (back_bands, 3, 4, step_back(2)),
+        (back_bands, 3, 3, step_back(1)),
+        (back_bands, 2, 3, step_back(0)),
+    ]
+    work = [(f,) + step for step in steps for f in range(2)]
+    slabs = multiply(*work[0][:4])
+    for n, (f, matrix, out_tiles, in_tiles, finish) in enumerate(work):
+        following = multiply(*work[n + 1][:4]) if n + 1 < len(work) else None
+        finish(f, combine(slabs))
+        slabs = following
 
     for own in range(2):
 

time: 29.2 us -> 29.2 us (level)
  no operation moved by 1% of the time
where the time goes in v12:
time: 29.2 us; the launch traced here: 29 us
  waiting for transfers between devices  11.9 us (41%)
  Pallas kernels  7.68 us (26%)
  starting transfers between devices  7.68 us (26%)
  local copies, waits for them, and re-layouts  1.15 us (4%)
  between operations  0.69 us (2%)
    ppermute x5, waiting for transfers between devices, moved(): return lax.ppermute(value, axes, pairs)  11.9 us
    ppermute x5, starting transfers between devices, moved(): return lax.ppermute(value, axes, pairs)  7.68 us
    pallas_call x1, Pallas kernels, split_columns(): pl.pallas_call(lambda *refs: sweep_kernel(width, *refs), out_shape=(own,...  4.2 us
    pallas_call x1, Pallas kernels, split_columns(): pl.pallas_call(lambda *refs: band_kernel(count * ROWS, *refs), out_shape=...  1.45 us
    pallas_call x1, Pallas kernels, split_columns(): pl.pallas_call(lambda *refs: pack_kernel(width, step, *refs), out_shape=(...  1.39 us
    dynamic_update_slice x1, local copies, waits for them, and re-layouts, split_columns(): image = lax.dynamic_update_slice(image, theirs[1], (0, 0, start))  0.72 us
  transfers between devices with their start and end apart: 5, of which 4 were waited for; matrix products, arithmetic and copies ran while one was open for 0% of the time, Pallas kernels for 7%

profile of v12, /device:TPU:20, one launch (start us, length us, event | category | flops | bytes accessed | tf_op | source)
XLA Modules:
  0.0 29.0 jit_solution(2590441160471818546)
XLA Ops:
  0.6 1.4 %pack.1 = (f32[81,8,128]{2,1,0:T(8,128)S(1)}, f32[65,8,128]{2,1,0:T(8,128)S(1)}, f32[25,8,128]{2,1,0:T(8,128)S(1)}, f32[16,8,1152]{2,1,0:T(8,128)S(1)}) custom-call(f32[2,2,16,2048]{3,2,1,0:T(8,128)} %refs_0_.3, f32[2,16,2048]{2,1,0:T(8,128)} %refs_1_.3, f32[2,16,2048]{2,1,0:T(8,128)} %refs_2_.1), custom_call_target="tpu_custom_call" | custom-call | tf_op jit(solution)/shard_map/pack/pallas_call | solution.py:602
  2.0 1.6 %collective-permute-start = (f32[65,8,128]{2,1,0:T(8,128)S(1)}, f32[65,8,128]{2,1,0:T(8,128)S(1)}, u32[]{:S(2)}, u32[]{:S(2)}) collective-permute-start(f32[65,8,128]{2,1,0:T(8,128)S(1)} %get-tuple-element.18), channel_id=1, source_target_pairs={{0,16},{1,17},{2,18},{3,19},{4,20},{5,21},{6,22},{7,23},{8,24},{9,... | collective-permute-start | bytes 798728 | tf_op jit(solution)/shard_map/ppermute | solution.py:595
  3.6 1.9 %collective-permute-start.1 = (f32[81,8,128]{2,1,0:T(8,128)S(1)}, f32[81,8,128]{2,1,0:T(8,128)S(1)}, u32[]{:S(2)}, u32[]{:S(2)}) collective-permute-start(f32[81,8,128]{2,1,0:T(8,128)S(1)} %get-tuple-element.20), channel_id=1, source_target_pairs={{1,2},{2,1},{3,4},{4,3},{5,6},{6,5},{7,8},{8,7},{9,10},{10,9},{11,... | collective-permute-start | bytes 995336 | tf_op jit(solution)/shard_map/ppermute | solution.py:595
  5.5 3.6 %collective-permute-start.2 = (f32[25,8,128]{2,1,0:T(8,128)S(1)}, f32[25,8,128]{2,1,0:T(8,128)S(1)}, u32[]{:S(2)}, u32[]{:S(2)}) collective-permute-start(f32[25,8,128]{2,1,0:T(8,128)S(1)} %get-tuple-element.21), channel_id=1, source_target_pairs={{1,18},{2,17},{3,20},{4,19},{5,22},{6,21},{7,24},{8,23},{9,26},{10... | collective-permute-start | bytes 307208 | tf_op jit(solution)/shard_map/ppermute | solution.py:595
  9.1 1.1 %collective-permute-done.bulk = f32[65,8,128]{2,1,0:T(8,128)S(1)} collective-permute-done((f32[65,8,128]{2,1,0:T(8,128)S(1)}, f32[65,8,128]{2,1,0:T(8,128)S(1)}, u32[]{:S(2)}, u32[]{:S(2)}) %collective-permute-start) | collective-permute-done | bytes 266272 | tf_op jit(solution)/shard_map/ppermute | solution.py:595
  10.2 0.0 copy-start
  10.2 0.0 copy-start.1
  10.2 0.2 relay.1
  10.4 0.1 collective-permute-start.3
  10.5 0.4 %copy-done = f32[2,2,15]{2,1,0:T(2,128)S(1)} copy-done((f32[2,2,15]{2,1,0:T(2,128)S(1)}, f32[2,2,15]{2,1,0:T(2,128)}, u32[]{:S(2)}) %copy-start) | copy-done | bytes 264
  10.9 0.0 copy-done.1
  10.9 1.5 %bands.1 = (bf16[2,240,288]{2,1,0:T(8,128)(2,1)S(1)}, bf16[2,144,192]{2,1,0:T(8,128)(2,1)S(1)}, f32[2,8,128]{2,1,0:T(8,128)S(1)}) custom-call(f32[2,2,15]{2,1,0:T(2,128)S(1)} %copy-done, f32[2]{0:T(128)S(1)} %copy-done.1), custom_call_target="tpu_custom_call" | custom-call | flops 10000000000 | bytes 1000000 | tf_op jit(solution)/shard_map/bands/pallas_call | solution.py:619
  12.4 0.5 %own_phases.1.refs_3_ = f32[2,4,2,16,1152]{4,3,2,1,0:T(8,128)S(1)} custom-call(f32[2,8,128]{2,1,0:T(8,128)S(1)} %get-tuple-element.14.freq_tiles.refs_0_, f32[16,8,1152]{2,1,0:T(8,128)S(1)} %get-tuple-element.17.window.refs_4_, f32[8,8,1152]{2,1,0:T(8,128)S(1)} %get-tuple-element.19.partner.refs_5_), custom_call_target="tpu_custom_call" | custom-call | tf_op jit(solution)/shard_map/own_phases/pallas_call | solution.py:643
  12.9 0.7 %collective-permute-done.2.refs_7_ = f32[25,8,128]{2,1,0:T(8,128)S(1)} collective-permute-done((f32[25,8,128]{2,1,0:T(8,128)S(1)}, f32[25,8,128]{2,1,0:T(8,128)S(1)}, u32[]{:S(2)}, u32[]{:S(2)}) %collective-permute-start.2) | collective-permute-done | bytes 102432 | tf_op jit(solution)/shard_map/ppermute | solution.py:595
  13.5 4.2 %collective-permute-done.1.refs_6_ = f32[81,8,128]{2,1,0:T(8,128)S(1)} collective-permute-done((f32[81,8,128]{2,1,0:T(8,128)S(1)}, f32[81,8,128]{2,1,0:T(8,128)S(1)}, u32[]{:S(2)}, u32[]{:S(2)}) %collective-permute-start.1) | collective-permute-done | bytes 331808 | tf_op jit(solution)/shard_map/ppermute | solution.py:595
  17.8 0.0 collective-permute-done.3.refs_8_
  17.8 4.2 %sweep.1 = (f32[2,16,2048]{2,1,0:T(8,128)}, f32[2,16,2048]{2,1,0:T(8,128)}, f32[2,2,16,1024]{3,2,1,0:T(8,128)S(1)}) custom-call(f32[2,8,128]{2,1,0:T(8,128)S(1)} %get-tuple-element.14.freq_tiles.refs_0_, bf16[2,240,288]{2,1,0:T(8,128)(2,1)S(1)} %get-tuple-element.15.refs_1_, bf16[2,144,192]{2,1,0:T(8,128)(2,1)S(1)} %get-tuple-element.16.refs_2_, ...), custom_call_target="tpu_custom_call" | custom-call | tf_op jit(solution)/shard_map/sweep/pallas_call | solution.py:653
  22.0 0.5 %collective-permute-start.4 = (f32[2,2,16,1024]{3,2,1,0:T(8,128)S(1)}, f32[2,2,16,1024]{3,2,1,0:T(8,128)S(1)}, u32[]{:S(2)}, u32[]{:S(2)}) collective-permute-start(f32[2,2,16,1024]{3,2,1,0:T(8,128)S(1)} %get-tuple-element.24), channel_id=1, source_target_pairs={{0,16},{1,17},{2,18},{3,19},{4,20},{5,21},{6,22},{7,23},{8,24},{9,... | collective-permute-start | bytes 786440 | tf_op jit(solution)/shard_map/ppermute | solution.py:595
  22.5 5.8 %collective-permute-done.4 = f32[2,2,16,1024]{3,2,1,0:T(8,128)S(1)} collective-permute-done((f32[2,2,16,1024]{3,2,1,0:T(8,128)S(1)}, f32[2,2,16,1024]{3,2,1,0:T(8,128)S(1)}, u32[]{:S(2)}, u32[]{:S(2)}) %collective-permute-start.4) | collective-permute-done | bytes 262176 | tf_op jit(solution)/shard_map/ppermute | solution.py:595
  28.3 0.7 %fusion = (f32[2,16,2048]{2,1,0:T(8,128)}, f32[2,16,2048]{2,1,0:T(8,128)}) fusion(f32[2,16,2048]{2,1,0:T(8,128)} %get-tuple-element.25, s32[]{:T(128)S(6)} %select_n.4, f32[2,2,16,1024]{3,2,1,0:T(8,128)S(1)} %collective-permute-done.4, f32[2,16,2048]{2,1,0:T(8,128)} %get-tuple-element.23), kind=kLoop, calls=%fused_computation.1 | loop fusion | bytes 524292 | tf_op jit(solution)/shard_map/dynamic_update_slice | solution.py:675
Async XLA Ops:
  2.0 8.2 %collective-permute-start = (f32[65,8,128]{2,1,0:T(8,128)S(1)}, f32[65,8,128]{2,1,0:T(8,128)S(1)}, u32[]{:S(2)}, u32[]{:S(2)}) collective-permute-start(f32[65,8,128]{2,1,0:T(8,128)S(1)} %get-tuple-element.18), channel_id=1, source_target_pairs={{0,16},{1,17},{2,18},{3,19},{4,20},{5,21},{6,22},{7,23},{8,24},{9,... | collective-permute-start | bytes 798728 | tf_op jit(solution)/shard_map/ppermute | solution.py:595
  3.6 14.2 %collective-permute-start.1 = (f32[81,8,128]{2,1,0:T(8,128)S(1)}, f32[81,8,128]{2,1,0:T(8,128)S(1)}, u32[]{:S(2)}, u32[]{:S(2)}) collective-permute-start(f32[81,8,128]{2,1,0:T(8,128)S(1)} %get-tuple-element.20), channel_id=1, source_target_pairs={{1,2},{2,1},{3,4},{4,3},{5,6},{6,5},{7,8},{8,7},{9,10},{10,9},{11,... | collective-permute-start | bytes 995336 | tf_op jit(solution)/shard_map/ppermute | solution.py:595
  5.5 8.0 %collective-permute-start.2 = (f32[25,8,128]{2,1,0:T(8,128)S(1)}, f32[25,8,128]{2,1,0:T(8,128)S(1)}, u32[]{:S(2)}, u32[]{:S(2)}) collective-permute-start(f32[25,8,128]{2,1,0:T(8,128)S(1)} %get-tuple-element.21), channel_id=1, source_target_pairs={{1,18},{2,17},{3,20},{4,19},{5,22},{6,21},{7,24},{8,23},{9,26},{10... | collective-permute-start | bytes 307208 | tf_op jit(solution)/shard_map/ppermute | solution.py:595
  10.2 0.7 %copy-start = (f32[2,2,15]{2,1,0:T(2,128)S(1)}, f32[2,2,15]{2,1,0:T(2,128)}, u32[]{:S(2)}) copy-start(f32[2,2,15]{2,1,0:T(2,128)} %refs_0_.2) | copy-start | bytes 724
  10.2 0.7 %copy-start.1 = (f32[2]{0:T(128)S(1)}, f32[2]{0:T(128)}, u32[]{:S(2)}) copy-start(f32[2]{0:T(128)} %refs_1_.2) | copy-start | bytes 28
  10.4 7.3 %collective-permute-start.3 = (f32[105,8,128]{2,1,0:T(8,128)S(1)}, f32[105,8,128]{2,1,0:T(8,128)S(1)}, u32[]{:S(2)}, u32[]{:S(2)}) collective-permute-start(f32[105,8,128]{2,1,0:T(8,128)S(1)} %get-tuple-element.22), channel_id=1, source_target_pairs={{0,1},{1,0},{2,3},{3,2},{4,5},{5,4},{6,7},{7,6},{8,9},{9,8},{10,11... | collective-permute-start | bytes 1290248 | tf_op jit(solution)/shard_map/ppermute | solution.py:595
  22.0 6.4 %collective-permute-start.4 = (f32[2,2,16,1024]{3,2,1,0:T(8,128)S(1)}, f32[2,2,16,1024]{3,2,1,0:T(8,128)S(1)}, u32[]{:S(2)}, u32[]{:S(2)}) collective-permute-start(f32[2,2,16,1024]{3,2,1,0:T(8,128)S(1)} %get-tuple-element.24), channel_id=1, source_target_pairs={{0,16},{1,17},{2,18},{3,19},{4,20},{5,21},{6,22},{7,23},{8,24},{9,... | collective-permute-start | bytes 786440 | tf_op jit(solution)/shard_map/ppermute | solution.py:595

commit v13 on v12

--- a/solution.py
+++ b/solution.py
@@ -302,11 +302,13 @@
             lanes = slice(side * step, side * step + width)
             return lambda level, tile: ref[level, 8 * tile : 8 * tile + 8, lanes]
 
-        def surface(plane, tile):
-            return surf[plane // 2, plane % 2, 8 * tile : 8 * tile + 8, own * step : own * step + width]
+        def surface_reader(side):
+            lanes = slice(side * step, side * step + width)
+            return lambda plane, tile: surf[plane // 2, plane % 2, 8 * tile : 8 * tile + 8, lanes]
 
         @pl.when(depth == own)
         def _():
+            surface, surface_far = surface_reader(own), surface_reader(1 - own)
             slow_near, pert_near = reader(slow, own), reader(pert, own)
             slow_far, pert_far = reader(slow, 1 - own), reader(pert, 1 - own)
             both = [(level, tile) for level in range(2) for tile in range(2)]
@@ -321,9 +323,10 @@
 
                 @pl.when((lax.rem(place, 2) == 1) == down)
                 def _():
-                    edges = edge_surface(surface, down) + edge_levels(own, slow_near, pert_near, down)
+                    edges = edge_surface(surface, down)[:4] + edge_levels(own, slow_near, pert_near, down)
                     pack_rows(cross, edges, own)
-                    pack_rows(cross_far, edge_levels(own, slow_far, pert_far, down), 1 - own)
+                    edges = edge_surface(surface_far, down)[4:] + edge_levels(own, slow_far, pert_far, down)
+                    pack_rows(cross_far, edges, 1 - own)
 
 
 def relay_kernel(window, bulk, chip, partner):
@@ -381,7 +384,7 @@
 
 def sweep_kernel(
     width, freq_tiles, bands, back_bands, own_phases, window, partner, cross, cross_far, chip,
-    gradient, image, theirs, slow_win, pert_win, operand, halo_phases, fields, image_win, grad_win,
+    mine, theirs, slow_win, pert_win, operand, halo_phases, fields, image_win, grad_win,
 ):
     depth = lax.axis_index("depth")
     place = lax.axis_index("xy")
@@ -431,8 +434,9 @@
 
     def fill(own, below_is_chip):
         chip_edges = [unpack_rows(chip, 13, n, own) for n in range(13)]
-        cross_edges = [unpack_rows(cross, 10, n, own) for n in range(10)]
-        cross_edges += [unpack_rows(cross_far, 3, n, own) for n in range(3)]
+        same = [unpack_rows(cross, 7, n, own) for n in range(7)]
+        other = [unpack_rows(cross_far, 6, n, own) for n in range(6)]
+        cross_edges = same[:4] + other[:3] + same[4:] + other[3:]
         above, below = (cross_edges, chip_edges) if below_is_chip else (chip_edges, cross_edges)
         for level in range(2):
             for tile in range(2):
@@ -565,14 +569,27 @@
         @pl.when(depth == own)
         def _():
             inner = slice(own * LANES, own * LANES + half)
-            outer = slice(own * half, own * half + half)
             for level in range(2):
                 for tile in range(2):
                     rows = slice(8 * tile, 8 * tile + 8)
-                    gradient[level, rows, outer] = grad_win[2 * own + level, tile, :, inner]
-                    image[level, rows, outer] = image_win[2 * own + level, tile, :, inner]
+                    mine[0, level, rows] = grad_win[2 * own + level, tile, :, inner]
+                    mine[1, level, rows] = image_win[2 * own + level, tile, :, inner]
                     theirs[0, level, rows] = grad_win[2 * (1 - own) + level, tile, :, inner]
                     theirs[1, level, rows] = image_win[2 * (1 - own) + level, tile, :, inner]
+
+
+def place_kernel(mine, received, gradient, image, sems):
+    half = mine.shape[3]
+    depth = lax.axis_index("depth")
+    copies = []
+    for n, whole in enumerate((gradient, image)):
+        for m, (part, side) in enumerate(((mine, depth), (received, 1 - depth))):
+            lanes = pl.ds(pl.multiple_of(side * half, LANES), half)
+            copies.append(pltpu.make_async_copy(part.at[n], whole.at[:, :, lanes], sems.at[2 * n + m]))
+    for copy in copies:
+        copy.start()
+    for copy in copies:
+        copy.wait()
 
 
 def split_columns(surface_data, frequencies, coefficients, slowness, perturbation):
@@ -601,7 +618,7 @@
     params = lambda mib: pltpu.CompilerParams(vmem_limit_bytes=mib * 2**20)
     cross, bulk, cross_far, window = pl.pallas_call(
         lambda *refs: pack_kernel(width, step, *refs),
-        out_shape=(packed(10), packed(8), packed(3), tile(16)),
+        out_shape=(packed(7), packed(8), packed(6), tile(16)),
         in_specs=[pl.BlockSpec(memory_space=pltpu.HBM)] * 3,
         out_specs=(vmem,) * 4,
         scratch_shapes=[
@@ -650,11 +667,11 @@
     )(freq_tiles, window, partner)
 
     own = jax.ShapeDtypeStruct((2, ROWS, columns), f32)
-    gradient, image, theirs = pl.pallas_call(
+    mine, theirs = pl.pallas_call(
         lambda *refs: sweep_kernel(width, *refs),
-        out_shape=(own, own, jax.ShapeDtypeStruct((2, 2, ROWS, half), f32)),
+        out_shape=(jax.ShapeDtypeStruct((2, 2, ROWS, half), f32),) * 2,
         in_specs=[vmem] * 9,
-        out_specs=(vmem,) * 3,
+        out_specs=(vmem,) * 2,
         scratch_shapes=[
             pltpu.VMEM((3, 3, 8, width), f32),
             pltpu.VMEM((4, 4, 8, width), f32),
@@ -669,11 +686,17 @@
     )(
         freq_tiles, bands, back_bands, own_phases, window, partner, cross, cross_far, chip,
     )
-    theirs = moved(theirs, True, "same")
-    start = (1 - lax.axis_index("depth")) * half
-    gradient = lax.dynamic_update_slice(gradient, theirs[0], (0, 0, start))
-    image = lax.dynamic_update_slice(image, theirs[1], (0, 0, start))
-    return gradient, image
+    received = moved(theirs, True, "same")
+    hbm = pl.BlockSpec(memory_space=pltpu.HBM)
+    return pl.pallas_call(
+        place_kernel,
+        out_shape=(own, own),
+        in_specs=[vmem] * 2,
+        out_specs=(hbm,) * 2,
+        scratch_shapes=[pltpu.SemaphoreType.DMA((4,))],
+        compiler_params=params(8),
+        name="place",
+    )(mine, received)
 
 
 def on_slice(surface_data, frequencies, coefficients, slowness, perturbation):

time: 29.2 us -> 30.4 us (1.041)
  the two profiles are of different devices: /device:TPU:20 before, /device:TPU:25 now
where the time goes in v13:
time: 30.4 us; the launch traced here: 30.2 us
  waiting for transfers between devices  11.7 us (38%)
  starting transfers between devices  10.1 us (33%)
  Pallas kernels  7.7 us (25%)
  between operations  0.69 us (2%)
    ppermute x5, waiting for transfers between devices, moved(): return lax.ppermute(value, axes, pairs)  11.7 us
    ppermute x5, starting transfers between devices, moved(): return lax.ppermute(value, axes, pairs)  10.1 us
    pallas_call x1, Pallas kernels, split_columns(): pl.pallas_call(lambda *refs: sweep_kernel(width, *refs), out_shape=(jax.S...  3.41 us
    pallas_call x1, Pallas kernels, split_columns(): pl.pallas_call(lambda *refs: band_kernel(count * ROWS, *refs), out_shape=...  1.45 us
    pallas_call x1, Pallas kernels, split_columns(): pl.pallas_call(lambda *refs: pack_kernel(width, step, *refs), out_shape=(...  1.39 us
    pallas_call x1, Pallas kernels, split_columns(): pl.pallas_call(place_kernel, out_shape=(own, own), in_specs=[vmem] * 2, o...  0.82 us
  transfers between devices with their start and end apart: 5, of which 4 were waited for; matrix products, arithmetic and copies ran while one was open for 0% of the time, Pallas kernels for 7%

profile of v13, /device:TPU:25, one launch (start us, length us, event | category | flops | bytes accessed | tf_op | source)
XLA Modules:
  0.0 30.2 jit_solution(6668310496272620858)
XLA Ops:
  0.6 1.4 %pack.1 = (f32[57,8,128]{2,1,0:T(8,128)S(1)}, f32[65,8,128]{2,1,0:T(8,128)S(1)}, f32[49,8,128]{2,1,0:T(8,128)S(1)}, f32[16,8,1152]{2,1,0:T(8,128)S(1)}) custom-call(f32[2,2,16,2048]{3,2,1,0:T(8,128)} %refs_0_.3, f32[2,16,2048]{2,1,0:T(8,128)} %refs_1_.3, f32[2,16,2048]{2,1,0:T(8,128)} %refs_2_.1), custom_call_target="tpu_custom_call" | custom-call | tf_op jit(solution)/shard_map/pack/pallas_call | solution.py:619
  2.0 1.3 %collective-permute-start = (f32[65,8,128]{2,1,0:T(8,128)S(1)}, f32[65,8,128]{2,1,0:T(8,128)S(1)}, u32[]{:S(2)}, u32[]{:S(2)}) collective-permute-start(f32[65,8,128]{2,1,0:T(8,128)S(1)} %get-tuple-element.17), channel_id=1, source_target_pairs={{0,16},{1,17},{2,18},{3,19},{4,20},{5,21},{6,22},{7,23},{8,24},{9,... | collective-permute-start | bytes 798728 | tf_op jit(solution)/shard_map/ppermute | solution.py:612
  3.3 3.9 %collective-permute-start.2 = (f32[49,8,128]{2,1,0:T(8,128)S(1)}, f32[49,8,128]{2,1,0:T(8,128)S(1)}, u32[]{:S(2)}, u32[]{:S(2)}) collective-permute-start(f32[49,8,128]{2,1,0:T(8,128)S(1)} %get-tuple-element.20), channel_id=1, source_target_pairs={{1,18},{2,17},{3,20},{4,19},{5,22},{6,21},{7,24},{8,23},{9,26},{10... | collective-permute-start | bytes 602120 | tf_op jit(solution)/shard_map/ppermute | solution.py:612
  7.3 1.9 %collective-permute-start.1 = (f32[57,8,128]{2,1,0:T(8,128)S(1)}, f32[57,8,128]{2,1,0:T(8,128)S(1)}, u32[]{:S(2)}, u32[]{:S(2)}) collective-permute-start(f32[57,8,128]{2,1,0:T(8,128)S(1)} %get-tuple-element.19), channel_id=1, source_target_pairs={{1,2},{2,1},{3,4},{4,3},{5,6},{6,5},{7,8},{8,7},{9,10},{10,9},{11,... | collective-permute-start | bytes 700424 | tf_op jit(solution)/shard_map/ppermute | solution.py:612
  9.2 0.2 collective-permute-done.bulk
  9.4 0.0 copy-start
  9.4 0.0 copy-start.1
  9.4 0.2 relay.1
  9.5 2.4 %collective-permute-start.3 = (f32[105,8,128]{2,1,0:T(8,128)S(1)}, f32[105,8,128]{2,1,0:T(8,128)S(1)}, u32[]{:S(2)}, u32[]{:S(2)}) collective-permute-start(f32[105,8,128]{2,1,0:T(8,128)S(1)} %get-tuple-element.21), channel_id=1, source_target_pairs={{0,1},{1,0},{2,3},{3,2},{4,5},{5,4},{6,7},{7,6},{8,9},{9,8},{10,11... | collective-permute-start | bytes 1290248 | tf_op jit(solution)/shard_map/ppermute | solution.py:612
  11.9 0.0 copy-done
  11.9 0.0 copy-done.1
  11.9 1.5 %bands.1 = (bf16[2,240,288]{2,1,0:T(8,128)(2,1)S(1)}, bf16[2,144,192]{2,1,0:T(8,128)(2,1)S(1)}, f32[2,8,128]{2,1,0:T(8,128)S(1)}) custom-call(f32[2,2,15]{2,1,0:T(2,128)S(1)} %copy-done, f32[2]{0:T(128)S(1)} %copy-done.1), custom_call_target="tpu_custom_call" | custom-call | flops 10000000000 | bytes 1000000 | tf_op jit(solution)/shard_map/bands/pallas_call | solution.py:636
  13.4 0.5 %own_phases.1.refs_3_ = f32[2,4,2,16,1152]{4,3,2,1,0:T(8,128)S(1)} custom-call(f32[2,8,128]{2,1,0:T(8,128)S(1)} %get-tuple-element.13.freq_tiles.refs_0_, f32[16,8,1152]{2,1,0:T(8,128)S(1)} %get-tuple-element.16.window.refs_4_, f32[8,8,1152]{2,1,0:T(8,128)S(1)} %get-tuple-element.18.partner.refs_5_), custom_call_target="tpu_custom_call" | custom-call | tf_op jit(solution)/shard_map/own_phases/pallas_call | solution.py:660
  13.9 3.4 %collective-permute-done.2.refs_7_ = f32[49,8,128]{2,1,0:T(8,128)S(1)} collective-permute-done((f32[49,8,128]{2,1,0:T(8,128)S(1)}, f32[49,8,128]{2,1,0:T(8,128)S(1)}, u32[]{:S(2)}, u32[]{:S(2)}) %collective-permute-start.2) | collective-permute-done | bytes 200736 | tf_op jit(solution)/shard_map/ppermute | solution.py:612
  17.2 2.4 %collective-permute-done.1.refs_6_ = f32[57,8,128]{2,1,0:T(8,128)S(1)} collective-permute-done((f32[57,8,128]{2,1,0:T(8,128)S(1)}, f32[57,8,128]{2,1,0:T(8,128)S(1)}, u32[]{:S(2)}, u32[]{:S(2)}) %collective-permute-start.1) | collective-permute-done | bytes 233504 | tf_op jit(solution)/shard_map/ppermute | solution.py:612
  19.6 0.0 collective-permute-done.3.refs_8_
  19.6 3.4 %sweep.1 = (f32[2,2,16,1024]{3,2,1,0:T(8,128)S(1)}, f32[2,2,16,1024]{3,2,1,0:T(8,128)S(1)}) custom-call(f32[2,8,128]{2,1,0:T(8,128)S(1)} %get-tuple-element.13.freq_tiles.refs_0_, bf16[2,240,288]{2,1,0:T(8,128)(2,1)S(1)} %get-tuple-element.14.refs_1_, bf16[2,144,192]{2,1,0:T(8,128)(2,1)S(1)} %get-tuple-element.15.refs_2_, ...), custom_call_target="tpu_custom_call" | custom-call | tf_op jit(solution)/shard_map/sweep/pallas_call | solution.py:670
  23.1 0.6 %collective-permute-start.4 = (f32[2,2,16,1024]{3,2,1,0:T(8,128)S(1)}, f32[2,2,16,1024]{3,2,1,0:T(8,128)S(1)}, u32[]{:S(2)}, u32[]{:S(2)}) collective-permute-start(f32[2,2,16,1024]{3,2,1,0:T(8,128)S(1)} %get-tuple-element.23), channel_id=1, source_target_pairs={{0,16},{1,17},{2,18},{3,19},{4,20},{5,21},{6,22},{7,23},{8,24},{9,... | collective-permute-start | bytes 786440 | tf_op jit(solution)/shard_map/ppermute | solution.py:612
  23.6 5.7 %collective-permute-done.4.received = f32[2,2,16,1024]{3,2,1,0:T(8,128)S(1)} collective-permute-done((f32[2,2,16,1024]{3,2,1,0:T(8,128)S(1)}, f32[2,2,16,1024]{3,2,1,0:T(8,128)S(1)}, u32[]{:S(2)}, u32[]{:S(2)}) %collective-permute-start.4) | collective-permute-done | bytes 262176 | tf_op jit(solution)/shard_map/ppermute | solution.py:612
  29.4 0.8 %place.1 = (f32[2,16,2048]{2,1,0:T(8,128)}, f32[2,16,2048]{2,1,0:T(8,128)}) custom-call(f32[2,2,16,1024]{3,2,1,0:T(8,128)S(1)} %get-tuple-element.22.mine, f32[2,2,16,1024]{3,2,1,0:T(8,128)S(1)} %collective-permute-done.4.received), custom_call_target="tpu_custom_call" | custom-call | tf_op jit(solution)/shard_map/place/pallas_call | solution.py:691
Async XLA Ops:
  2.0 7.3 %collective-permute-start = (f32[65,8,128]{2,1,0:T(8,128)S(1)}, f32[65,8,128]{2,1,0:T(8,128)S(1)}, u32[]{:S(2)}, u32[]{:S(2)}) collective-permute-start(f32[65,8,128]{2,1,0:T(8,128)S(1)} %get-tuple-element.17), channel_id=1, source_target_pairs={{0,16},{1,17},{2,18},{3,19},{4,20},{5,21},{6,22},{7,23},{8,24},{9,... | collective-permute-start | bytes 798728 | tf_op jit(solution)/shard_map/ppermute | solution.py:612
  3.3 13.9 %collective-permute-start.2 = (f32[49,8,128]{2,1,0:T(8,128)S(1)}, f32[49,8,128]{2,1,0:T(8,128)S(1)}, u32[]{:S(2)}, u32[]{:S(2)}) collective-permute-start(f32[49,8,128]{2,1,0:T(8,128)S(1)} %get-tuple-element.20), channel_id=1, source_target_pairs={{1,18},{2,17},{3,20},{4,19},{5,22},{6,21},{7,24},{8,23},{9,26},{10... | collective-permute-start | bytes 602120 | tf_op jit(solution)/shard_map/ppermute | solution.py:612
  7.3 12.4 %collective-permute-start.1 = (f32[57,8,128]{2,1,0:T(8,128)S(1)}, f32[57,8,128]{2,1,0:T(8,128)S(1)}, u32[]{:S(2)}, u32[]{:S(2)}) collective-permute-start(f32[57,8,128]{2,1,0:T(8,128)S(1)} %get-tuple-element.19), channel_id=1, source_target_pairs={{1,2},{2,1},{3,4},{4,3},{5,6},{6,5},{7,8},{8,7},{9,10},{10,9},{11,... | collective-permute-start | bytes 700424 | tf_op jit(solution)/shard_map/ppermute | solution.py:612
  9.4 2.5 %copy-start = (f32[2,2,15]{2,1,0:T(2,128)S(1)}, f32[2,2,15]{2,1,0:T(2,128)}, u32[]{:S(2)}) copy-start(f32[2,2,15]{2,1,0:T(2,128)} %refs_0_.2) | copy-start | bytes 724
  9.4 2.5 %copy-start.1 = (f32[2]{0:T(128)S(1)}, f32[2]{0:T(128)}, u32[]{:S(2)}) copy-start(f32[2]{0:T(128)} %refs_1_.2) | copy-start | bytes 28
  9.5 10.1 %collective-permute-start.3 = (f32[105,8,128]{2,1,0:T(8,128)S(1)}, f32[105,8,128]{2,1,0:T(8,128)S(1)}, u32[]{:S(2)}, u32[]{:S(2)}) collective-permute-start(f32[105,8,128]{2,1,0:T(8,128)S(1)} %get-tuple-element.21), channel_id=1, source_target_pairs={{0,1},{1,0},{2,3},{3,2},{4,5},{5,4},{6,7},{7,6},{8,9},{9,8},{10,11... | collective-permute-start | bytes 1290248 | tf_op jit(solution)/shard_map/ppermute | solution.py:612
  23.1 6.3 %collective-permute-start.4 = (f32[2,2,16,1024]{3,2,1,0:T(8,128)S(1)}, f32[2,2,16,1024]{3,2,1,0:T(8,128)S(1)}, u32[]{:S(2)}, u32[]{:S(2)}) collective-permute-start(f32[2,2,16,1024]{3,2,1,0:T(8,128)S(1)} %get-tuple-element.23), channel_id=1, source_target_pairs={{0,16},{1,17},{2,18},{3,19},{4,20},{5,21},{6,22},{7,23},{8,24},{9,... | collective-permute-start | bytes 786440 | tf_op jit(solution)/shard_map/ppermute | solution.py:612

commit v14 on v13

--- a/solution.py
+++ b/solution.py
@@ -302,13 +302,11 @@
             lanes = slice(side * step, side * step + width)
             return lambda level, tile: ref[level, 8 * tile : 8 * tile + 8, lanes]
 
-        def surface_reader(side):
-            lanes = slice(side * step, side * step + width)
-            return lambda plane, tile: surf[plane // 2, plane % 2, 8 * tile : 8 * tile + 8, lanes]
+        def surface(plane, tile):
+            return surf[plane // 2, plane % 2, 8 * tile : 8 * tile + 8, own * step : own * step + width]
 
         @pl.when(depth == own)
         def _():
-            surface, surface_far = surface_reader(own), surface_reader(1 - own)
             slow_near, pert_near = reader(slow, own), reader(pert, own)
             slow_far, pert_far = reader(slow, 1 - own), reader(pert, 1 - own)
             both = [(level, tile) for level in range(2) for tile in range(2)]
@@ -323,10 +321,9 @@
 
                 @pl.when((lax.rem(place, 2) == 1) == down)
                 def _():
-                    edges = edge_surface(surface, down)[:4] + edge_levels(own, slow_near, pert_near, down)
+                    edges = edge_surface(surface, down) + edge_levels(own, slow_near, pert_near, down)
                     pack_rows(cross, edges, own)
-                    edges = edge_surface(surface_far, down)[4:] + edge_levels(own, slow_far, pert_far, down)
-                    pack_rows(cross_far, edges, 1 - own)
+                    pack_rows(cross_far, edge_levels(own, slow_far, pert_far, down), 1 - own)
 
 
 def relay_kernel(window, bulk, chip, partner):
@@ -434,9 +431,8 @@
 
     def fill(own, below_is_chip):
         chip_edges = [unpack_rows(chip, 13, n, own) for n in range(13)]
-        same = [unpack_rows(cross, 7, n, own) for n in range(7)]
-        other = [unpack_rows(cross_far, 6, n, own) for n in range(6)]
-        cross_edges = same[:4] + other[:3] + same[4:] + other[3:]
+        cross_edges = [unpack_rows(cross, 10, n, own) for n in range(10)]
+        cross_edges += [unpack_rows(cross_far, 3, n, own) for n in range(3)]
         above, below = (cross_edges, chip_edges) if below_is_chip else (chip_edges, cross_edges)
         for level in range(2):
             for tile in range(2):
@@ -618,7 +614,7 @@
     params = lambda mib: pltpu.CompilerParams(vmem_limit_bytes=mib * 2**20)
     cross, bulk, cross_far, window = pl.pallas_call(
         lambda *refs: pack_kernel(width, step, *refs),
-        out_shape=(packed(7), packed(8), packed(6), tile(16)),
+        out_shape=(packed(10), packed(8), packed(3), tile(16)),
         in_specs=[pl.BlockSpec(memory_space=pltpu.HBM)] * 3,
         out_specs=(vmem,) * 4,
         scratch_shapes=[
@@ -687,16 +683,10 @@
         freq_tiles, bands, back_bands, own_phases, window, partner, cross, cross_far, chip,
     )
     received = moved(theirs, True, "same")
-    hbm = pl.BlockSpec(memory_space=pltpu.HBM)
-    return pl.pallas_call(
-        place_kernel,
-        out_shape=(own, own),
-        in_specs=[vmem] * 2,
-        out_specs=(hbm,) * 2,
-        scratch_shapes=[pltpu.SemaphoreType.DMA((4,))],
-        compiler_params=params(8),
-        name="place",
-    )(mine, received)
+    start = lax.axis_index("depth") * half
+    whole = jnp.zeros((2, ROWS, columns), f32)
+    at = [lax.dynamic_update_slice(whole, mine[n], (0, 0, start)) for n in range(2)]
+    return tuple(lax.dynamic_update_slice(at[n], received[n], (0, 0, half - start)) for n in range(2))
 
 
 def on_slice(surface_data, frequencies, coefficients, slowness, perturbation):

time: 30.4 us -> 28.7 us (0.944)
  the two profiles are of different devices: /device:TPU:25 before, /device:TPU:20 now
where the time goes in v14:
time: 28.7 us; the launch traced here: 28.5 us
  waiting for transfers between devices  11.8 us (41%)
  starting transfers between devices  7.74 us (27%)
  Pallas kernels  6.93 us (24%)
  local copies, waits for them, and re-layouts  1.3 us (5%)
  between operations  0.75 us (3%)
    ppermute x5, waiting for transfers between devices, moved(): return lax.ppermute(value, axes, pairs)  11.8 us
    ppermute x5, starting transfers between devices, moved(): return lax.ppermute(value, axes, pairs)  7.74 us
    pallas_call x1, Pallas kernels, split_columns(): pl.pallas_call(lambda *refs: sweep_kernel(width, *refs), out_shape=(jax.S...  3.46 us
    pallas_call x1, Pallas kernels, split_columns(): pl.pallas_call(lambda *refs: band_kernel(count * ROWS, *refs), out_shape=...  1.45 us
    pallas_call x1, Pallas kernels, split_columns(): pl.pallas_call(lambda *refs: pack_kernel(width, step, *refs), out_shape=(...  1.39 us
    unnamed x8, local copies, waits for them, and re-layouts  1.2 us
  transfers between devices with their start and end apart: 5, of which 4 were waited for; matrix products, arithmetic and copies ran while one was open for 0% of the time, Pallas kernels for 7%

profile of v14, /device:TPU:20, one launch (start us, length us, event | category | flops | bytes accessed | tf_op | source)
XLA Modules:
  0.0 28.5 jit_solution(636245009829710974)
XLA Ops:
  0.6 1.4 %pack.1 = (f32[81,8,128]{2,1,0:T(8,128)S(1)}, f32[65,8,128]{2,1,0:T(8,128)S(1)}, f32[25,8,128]{2,1,0:T(8,128)S(1)}, f32[16,8,1152]{2,1,0:T(8,128)S(1)}) custom-call(f32[2,2,16,2048]{3,2,1,0:T(8,128)} %refs_0_.3, f32[2,16,2048]{2,1,0:T(8,128)} %refs_1_.3, f32[2,16,2048]{2,1,0:T(8,128)} %refs_2_.1), custom_call_target="tpu_custom_call" | custom-call | tf_op jit(solution)/shard_map/pack/pallas_call | solution.py:615
  2.0 1.6 %collective-permute-start = (f32[65,8,128]{2,1,0:T(8,128)S(1)}, f32[65,8,128]{2,1,0:T(8,128)S(1)}, u32[]{:S(2)}, u32[]{:S(2)}) collective-permute-start(f32[65,8,128]{2,1,0:T(8,128)S(1)} %get-tuple-element.17), channel_id=1, source_target_pairs={{0,16},{1,17},{2,18},{3,19},{4,20},{5,21},{6,22},{7,23},{8,24},{9,... | collective-permute-start | bytes 798728 | tf_op jit(solution)/shard_map/ppermute | solution.py:608
  3.6 1.9 %collective-permute-start.1 = (f32[81,8,128]{2,1,0:T(8,128)S(1)}, f32[81,8,128]{2,1,0:T(8,128)S(1)}, u32[]{:S(2)}, u32[]{:S(2)}) collective-permute-start(f32[81,8,128]{2,1,0:T(8,128)S(1)} %get-tuple-element.19), channel_id=1, source_target_pairs={{1,2},{2,1},{3,4},{4,3},{5,6},{6,5},{7,8},{8,7},{9,10},{10,9},{11,... | collective-permute-start | bytes 995336 | tf_op jit(solution)/shard_map/ppermute | solution.py:608
  5.5 3.6 %collective-permute-start.2 = (f32[25,8,128]{2,1,0:T(8,128)S(1)}, f32[25,8,128]{2,1,0:T(8,128)S(1)}, u32[]{:S(2)}, u32[]{:S(2)}) collective-permute-start(f32[25,8,128]{2,1,0:T(8,128)S(1)} %get-tuple-element.20), channel_id=1, source_target_pairs={{1,18},{2,17},{3,20},{4,19},{5,22},{6,21},{7,24},{8,23},{9,26},{10... | collective-permute-start | bytes 307208 | tf_op jit(solution)/shard_map/ppermute | solution.py:608
  9.1 1.1 %collective-permute-done.bulk = f32[65,8,128]{2,1,0:T(8,128)S(1)} collective-permute-done((f32[65,8,128]{2,1,0:T(8,128)S(1)}, f32[65,8,128]{2,1,0:T(8,128)S(1)}, u32[]{:S(2)}, u32[]{:S(2)}) %collective-permute-start) | collective-permute-done | bytes 266272 | tf_op jit(solution)/shard_map/ppermute | solution.py:608
  10.2 0.0 copy-start
  10.2 0.0 copy-start.1
  10.2 0.2 relay.1
  10.4 0.1 collective-permute-start.3
  10.5 0.4 %copy-done = f32[2,2,15]{2,1,0:T(2,128)S(1)} copy-done((f32[2,2,15]{2,1,0:T(2,128)S(1)}, f32[2,2,15]{2,1,0:T(2,128)}, u32[]{:S(2)}) %copy-start) | copy-done | bytes 264
  10.9 0.0 copy-done.1
  10.9 1.5 %bands.1 = (bf16[2,240,288]{2,1,0:T(8,128)(2,1)S(1)}, bf16[2,144,192]{2,1,0:T(8,128)(2,1)S(1)}, f32[2,8,128]{2,1,0:T(8,128)S(1)}) custom-call(f32[2,2,15]{2,1,0:T(2,128)S(1)} %copy-done, f32[2]{0:T(128)S(1)} %copy-done.1), custom_call_target="tpu_custom_call" | custom-call | flops 10000000000 | bytes 1000000 | tf_op jit(solution)/shard_map/bands/pallas_call | solution.py:632
  12.4 0.5 %own_phases.1.refs_3_ = f32[2,4,2,16,1152]{4,3,2,1,0:T(8,128)S(1)} custom-call(f32[2,8,128]{2,1,0:T(8,128)S(1)} %get-tuple-element.13.freq_tiles.refs_0_, f32[16,8,1152]{2,1,0:T(8,128)S(1)} %get-tuple-element.16.window.refs_4_, f32[8,8,1152]{2,1,0:T(8,128)S(1)} %get-tuple-element.18.partner.refs_5_), custom_call_target="tpu_custom_call" | custom-call | tf_op jit(solution)/shard_map/own_phases/pallas_call | solution.py:656
  12.9 0.7 %collective-permute-done.2.refs_7_ = f32[25,8,128]{2,1,0:T(8,128)S(1)} collective-permute-done((f32[25,8,128]{2,1,0:T(8,128)S(1)}, f32[25,8,128]{2,1,0:T(8,128)S(1)}, u32[]{:S(2)}, u32[]{:S(2)}) %collective-permute-start.2) | collective-permute-done | bytes 102432 | tf_op jit(solution)/shard_map/ppermute | solution.py:608
  13.5 4.2 %collective-permute-done.1.refs_6_ = f32[81,8,128]{2,1,0:T(8,128)S(1)} collective-permute-done((f32[81,8,128]{2,1,0:T(8,128)S(1)}, f32[81,8,128]{2,1,0:T(8,128)S(1)}, u32[]{:S(2)}, u32[]{:S(2)}) %collective-permute-start.1) | collective-permute-done | bytes 331808 | tf_op jit(solution)/shard_map/ppermute | solution.py:608
  17.8 0.0 collective-permute-done.3.refs_8_
  17.8 3.5 %sweep.1 = (f32[2,2,16,1024]{3,2,1,0:T(8,128)S(1)}, f32[2,2,16,1024]{3,2,1,0:T(8,128)S(1)}) custom-call(f32[2,8,128]{2,1,0:T(8,128)S(1)} %get-tuple-element.13.freq_tiles.refs_0_, bf16[2,240,288]{2,1,0:T(8,128)(2,1)S(1)} %get-tuple-element.14.refs_1_, bf16[2,144,192]{2,1,0:T(8,128)(2,1)S(1)} %get-tuple-element.15.refs_2_, ...), custom_call_target="tpu_custom_call" | custom-call | tf_op jit(solution)/shard_map/sweep/pallas_call | solution.py:666
  21.2 0.6 %collective-permute-start.4 = (f32[2,2,16,1024]{3,2,1,0:T(8,128)S(1)}, f32[2,2,16,1024]{3,2,1,0:T(8,128)S(1)}, u32[]{:S(2)}, u32[]{:S(2)}) collective-permute-start(f32[2,2,16,1024]{3,2,1,0:T(8,128)S(1)} %get-tuple-element.23), channel_id=1, source_target_pairs={{0,16},{1,17},{2,18},{3,19},{4,20},{5,21},{6,22},{7,23},{8,24},{9,... | collective-permute-start | bytes 786440 | tf_op jit(solution)/shard_map/ppermute | solution.py:608
  21.9 5.7 %collective-permute-done.4 = f32[2,2,16,1024]{3,2,1,0:T(8,128)S(1)} collective-permute-done((f32[2,2,16,1024]{3,2,1,0:T(8,128)S(1)}, f32[2,2,16,1024]{3,2,1,0:T(8,128)S(1)}, u32[]{:S(2)}, u32[]{:S(2)}) %collective-permute-start.4) | collective-permute-done | bytes 262176 | tf_op jit(solution)/shard_map/ppermute | solution.py:608
  27.7 0.0 copy-start.2
  27.7 0.0 copy-start.3
  27.7 0.7 %copy-done.2 = f32[2,16,2048]{2,1,0:T(8,128)} copy-done((f32[2,16,2048]{2,1,0:T(8,128)}, f32[2,16,2048]{2,1,0:T(8,128)S(1)}, u32[]{:S(2)}) %copy-start.2) | copy-done | bytes 262168
  28.4 0.1 copy-done.3
  (5 shorter events, 0.1 us)
Async XLA Ops:
  2.0 8.2 %collective-permute-start = (f32[65,8,128]{2,1,0:T(8,128)S(1)}, f32[65,8,128]{2,1,0:T(8,128)S(1)}, u32[]{:S(2)}, u32[]{:S(2)}) collective-permute-start(f32[65,8,128]{2,1,0:T(8,128)S(1)} %get-tuple-element.17), channel_id=1, source_target_pairs={{0,16},{1,17},{2,18},{3,19},{4,20},{5,21},{6,22},{7,23},{8,24},{9,... | collective-permute-start | bytes 798728 | tf_op jit(solution)/shard_map/ppermute | solution.py:608
  3.6 14.2 %collective-permute-start.1 = (f32[81,8,128]{2,1,0:T(8,128)S(1)}, f32[81,8,128]{2,1,0:T(8,128)S(1)}, u32[]{:S(2)}, u32[]{:S(2)}) collective-permute-start(f32[81,8,128]{2,1,0:T(8,128)S(1)} %get-tuple-element.19), channel_id=1, source_target_pairs={{1,2},{2,1},{3,4},{4,3},{5,6},{6,5},{7,8},{8,7},{9,10},{10,9},{11,... | collective-permute-start | bytes 995336 | tf_op jit(solution)/shard_map/ppermute | solution.py:608
  5.5 8.0 %collective-permute-start.2 = (f32[25,8,128]{2,1,0:T(8,128)S(1)}, f32[25,8,128]{2,1,0:T(8,128)S(1)}, u32[]{:S(2)}, u32[]{:S(2)}) collective-permute-start(f32[25,8,128]{2,1,0:T(8,128)S(1)} %get-tuple-element.20), channel_id=1, source_target_pairs={{1,18},{2,17},{3,20},{4,19},{5,22},{6,21},{7,24},{8,23},{9,26},{10... | collective-permute-start | bytes 307208 | tf_op jit(solution)/shard_map/ppermute | solution.py:608
  10.2 0.7 %copy-start = (f32[2,2,15]{2,1,0:T(2,128)S(1)}, f32[2,2,15]{2,1,0:T(2,128)}, u32[]{:S(2)}) copy-start(f32[2,2,15]{2,1,0:T(2,128)} %refs_0_.2) | copy-start | bytes 724
  10.2 0.7 %copy-start.1 = (f32[2]{0:T(128)S(1)}, f32[2]{0:T(128)}, u32[]{:S(2)}) copy-start(f32[2]{0:T(128)} %refs_1_.2) | copy-start | bytes 28
  10.4 7.3 %collective-permute-start.3 = (f32[105,8,128]{2,1,0:T(8,128)S(1)}, f32[105,8,128]{2,1,0:T(8,128)S(1)}, u32[]{:S(2)}, u32[]{:S(2)}) collective-permute-start(f32[105,8,128]{2,1,0:T(8,128)S(1)} %get-tuple-element.21), channel_id=1, source_target_pairs={{0,1},{1,0},{2,3},{3,2},{4,5},{5,4},{6,7},{7,6},{8,9},{9,8},{10,11... | collective-permute-start | bytes 1290248 | tf_op jit(solution)/shard_map/ppermute | solution.py:608
  21.2 6.4 %collective-permute-start.4 = (f32[2,2,16,1024]{3,2,1,0:T(8,128)S(1)}, f32[2,2,16,1024]{3,2,1,0:T(8,128)S(1)}, u32[]{:S(2)}, u32[]{:S(2)}) collective-permute-start(f32[2,2,16,1024]{3,2,1,0:T(8,128)S(1)} %get-tuple-element.23), channel_id=1, source_target_pairs={{0,16},{1,17},{2,18},{3,19},{4,20},{5,21},{6,22},{7,23},{8,24},{9,... | collective-permute-start | bytes 786440 | tf_op jit(solution)/shard_map/ppermute | solution.py:608
  27.7 0.7 %copy-start.2 = (f32[2,16,2048]{2,1,0:T(8,128)}, f32[2,16,2048]{2,1,0:T(8,128)S(1)}, u32[]{:S(2)}) copy-start(f32[2,16,2048]{2,1,0:T(8,128)S(1)} %get-tuple-element.24) | copy-start | bytes 786436
  27.7 0.8 %copy-start.3 = (f32[2,16,2048]{2,1,0:T(8,128)}, f32[2,16,2048]{2,1,0:T(8,128)S(1)}, u32[]{:S(2)}) copy-start(f32[2,16,2048]{2,1,0:T(8,128)S(1)} %get-tuple-element.25) | copy-start | bytes 786436
